TPU v7x, 32 devices: a whole 2x2x4 slice. The times are simulated.
32 devices in a mesh: block: 1, tile: 32 (over z, y, x, core).
Axes of the slice: x: 2, y: 2, z: 4, core: 2. Of those that a mesh axis runs over, the one named last changes fastest.
Arguments:
- acts: bfloat16 [2, 32, 64, 384], P('block', 'tile'), may hold values from -6 to 6
- gamma: float32 [384], replicated, may hold values from 0.25 to 1.75
- beta: float32 [384], replicated, may hold values from -3 to 3
- weights: bfloat16 [384, 27, 192], P('tile'), may hold values from -0.0625 to 0.0625
- cotangent: bfloat16 [2, 64, 128, 192], P('block', 'tile'), may hold values from -6 to 6
Outputs:
- d_acts: bfloat16 [2, 32, 64, 384], P('block', 'tile')
- d_weights: float32 [384, 27, 192], P('tile')
All inputs are finite; a program needn't handle non-finite values.
Results may differ from a plain program's by a relative error of at most 0.0029.
Values may be sent and summed in bfloat16 or wider, within the bound.
No kernel may reach another device: no remote copies, remote signals or barrier semaphores. Data moves between devices by JAX's collectives and lax.ppermute only.
A program may use at most 128 MiB of HBM per device.

v0:
```python
import jax
import jax.numpy as jnp
from jax import lax
from jax.sharding import PartitionSpec as P

GROUPS = 32


norm_eps = 1e-06


def from_behind(value, axis, steps):
    count = lax.axis_size(axis)
    first, last = (max(0, -steps), min(count, count - steps))
    return lax.ppermute(value, axis, [(source, source + steps) for source in range(first, last)])


def padded_2(value, sides, width):
    for axis, dim in sides:
        size, length = (lax.axis_size(axis), value.shape[dim])
        up = [(i, (i + 1) % size) for i in range(size - 1)]
        down = [(j, i) for i, j in up]
        last = lax.slice_in_dim(value, length - width, length, axis=dim)
        first = lax.slice_in_dim(value, 0, width, axis=dim)
        before = lax.ppermute(last, axis, up)
        after = lax.ppermute(first, axis, down)
        value = jnp.concatenate([before, value, after], axis=dim)
    return value


def group_totals(values, frames, per_group):
    return jnp.sum(values, axis=(1, 2)).reshape(frames, GROUPS, per_group).sum(-1)


def shards(acts, gamma, beta, weights, cotangent):
    frames, low_rows, low_cols, channels = acts.shape
    tiles = lax.axis_size("tile")
    per_group = channels // GROUPS
    group_size = low_rows * tiles * low_cols * per_group
    acts_wide = acts.astype(jnp.float32)
    stat_sum = group_totals(acts_wide, frames, per_group)
    stat_sq = group_totals(acts_wide * acts_wide, frames, per_group)
    stat_sum, stat_sq = lax.psum((stat_sum, stat_sq), "tile")
    group_mean = stat_sum / group_size
    inv_std = lax.rsqrt(stat_sq / group_size - group_mean * group_mean + norm_eps)
    mean_chan = jnp.repeat(group_mean, per_group, axis=1)[:, None, None, :]
    inv_chan = jnp.repeat(inv_std, per_group, axis=1)[:, None, None, :]
    normed = (acts_wide - mean_chan) * inv_chan
    shifted = normed * gamma + beta
    gate_value = jax.nn.sigmoid(shifted)
    hidden = (shifted * gate_value).astype(jnp.bfloat16)
    previous = from_behind(hidden, "block", 1)
    joined = jnp.concatenate([previous, hidden], 0)
    padded = padded_2(joined, (("tile", 1),), 1)
    upsampled = jnp.repeat(jnp.repeat(padded, 2, axis=1), 2, axis=2)[:, 1 : 2 * low_rows + 3]
    upsampled = jnp.pad(upsampled, ((0, 0), (0, 0), (1, 1), (0, 0)))
    following = from_behind(cotangent, "block", -1)
    grad_field = jnp.concatenate([cotangent, following], 0)
    grad_field = padded_2(grad_field, (("tile", 1),), 1)
    grad_field = jnp.pad(grad_field, ((0, 0), (0, 0), (1, 1), (0, 0)))
    up_rows = 2 * low_rows
    up_cols = 2 * low_cols
    num_cells = frames * up_rows * up_cols
    tap_list = [(tap // 9, tap // 3 % 3, tap % 3) for tap in range(27)]
    windows = [
        grad_field[
            2 - tap_t : 2 - tap_t + frames,
            2 - tap_h : 2 - tap_h + up_rows,
            2 - tap_w : 2 - tap_w + up_cols,
        ].reshape(num_cells, -1)
        for tap_t, tap_h, tap_w in tap_list
    ]
    columns = jnp.concatenate(windows, 1)
    piece_rows = lax.all_gather(weights, "tile", axis=0, tiled=True)
    flat_rows = piece_rows.reshape(piece_rows.shape[0], -1)
    back_grad = lax.dot_general(
        columns, flat_rows, (((1,), (1,)), ((), ())), preferred_element_type=jnp.float32
    )
    back_grad = back_grad.reshape(frames, low_rows, 2, low_cols, 2, piece_rows.shape[0])
    act_grad = back_grad.sum(axis=(2, 4))
    silu_slope = gate_value * (1.0 + shifted * (1.0 - gate_value))
    norm_grad = act_grad * silu_slope * gamma
    first_sum = group_totals(norm_grad, frames, per_group)
    second_sum = group_totals(norm_grad * normed, frames, per_group)
    first_sum, second_sum = lax.psum((first_sum, second_sum), "tile")
    first_chan = jnp.repeat(first_sum / group_size, per_group, axis=1)[:, None, None, :]
    second_chan = jnp.repeat(second_sum / group_size, per_group, axis=1)[:, None, None, :]
    d_acts = (inv_chan * (norm_grad - first_chan - normed * second_chan)).astype(jnp.bfloat16)
    flat_grads = cotangent.reshape(num_cells, -1)
    term_list = []
    for tap_t, tap_h, tap_w in tap_list:
        window_h = upsampled[
            tap_t : tap_t + frames, tap_h : tap_h + up_rows, tap_w : tap_w + up_cols
        ].reshape(num_cells, channels)
        term_list.append(
            lax.dot_general(
                window_h, flat_grads, (((0,), (0,)), ((), ())), preferred_element_type=jnp.float32
            )
        )
    whole_terms = jnp.stack(term_list, 1)
    whole_terms = lax.psum(whole_terms, "block")
    d_weights = lax.psum_scatter(whole_terms, "tile", scatter_dimension=0, tiled=True)
    return (d_acts, d_weights)


def solution(mesh):
    placed = (
        P("block", "tile", None, None),
        P(),
        P(),
        P("tile", None, None),
        P("block", "tile", None, None),
    )
    return jax.shard_map(
        shards,
        mesh=mesh,
        in_specs=placed,
        out_specs=(P("block", "tile", None, None), P("tile", None, None)),
        check_vma=False,
    )
```

profile of v0, /device:TPU:0, one launch (start us, length us, event | category | flops | bytes accessed | tf_op | source)
XLA Modules:
  0.0 377.6 jit_solution(13603218473403057538)
XLA Ops:
  11.1 42.5 %all-reduce.3 = (f32[2,32]{1,0:T(2,128)S(1)}, f32[2,32]{1,0:T(2,128)S(1)}) all-reduce(f32[2,32]{1,0:T(2,128)S(1)} %reduce_sum.86, f32[2,32]{1,0:T(2,128)S(1)} %reduce_sum.84), channel_id=1, replica_groups=mesh['block'=1,'tile'=32] {'tile'}, use_global_device_ids=true, to_apply=%region_5.0 | all-reduce | flops 128 | bytes 1024 | tf_op jit(solution)/shard_map/psum | solution.py:43
  58.3 3.5 collective-permute-done.2
  65.9 2.5 fusion.110
  70.1 1.8 copy.86
  72.9 1.8 copy.85
  76.4 1.8 copy.83
  79.8 1.8 copy.82
  83.3 1.8 copy.80
  86.8 1.8 copy.79
  88.6 1.7 copy.106
  90.3 1.8 copy.77
  92.1 1.7 copy.104
  93.8 1.8 copy.76
  95.6 1.7 copy.103
  97.3 1.8 copy.74
  99.1 1.7 copy.101
  100.7 1.8 copy.73
  104.2 1.8 copy.71
  107.7 1.8 copy.70
  111.2 1.8 copy.68
  114.6 1.8 copy.67
  116.4 1.7 copy.94
  118.1 1.8 copy.65
  121.6 9.7 %concatenate.111 = bf16[2,1,2,64,2,5184]{5,3,4,2,0,1:T(8,128)(2,1)} concatenate(bf16[2,1,2,64,2,192]{5,3,4,2,0,1:T(8,128)(2,1)} %copy.92, bf16[2,1,2,64,2,192]{5,3,4,2,0,1:T(8,128)(2,1)S(1)} %copy.93, bf16[2,1,2,64,2,192]{5,3,4,2,0,1:T(8,128)(2,1)} %copy.94, bf16[2,1,2,64,2,192]{5,3,4,2,0,1:T(8,128)(2,1)} %copy.95, bf16[2,1,2,64,2,192]{5,3,4,2,0,1:T(8,128)(2,1)S(1)} %copy.96, ...), dimensions={5} | concatenate | bytes 10616832 | tf_op jit(solution)/shard_map/concatenate | solution.py:73
  131.3 8.6 %copy.119 = bf16[384,27,192]{0,2,1:T(8,128)(2,1)} copy(bf16[384,27,192]{2,1,0:T(8,128)(2,1)} %all-gather.2.cloned.1.call-done) | data formatting | bytes 7962624 | tf_op jit(solution)/shard_map/all_gather | solution.py:74
  139.8 6.7 %fusion.8 = f32[2,64,384]{2,1,0:T(8,128)S(1)} fusion(bf16[384,5184,1,1,1]{0,1,4,3,2:T(8,128)(2,1)} %bitcast.286, bf16[2,1,2,64,2,5184]{5,3,4,2,0,1:T(8,128)(2,1)} %concatenate.111), kind=kOutput, calls=%fused_computation.10 | convolution fusion | flops 2038579200 | bytes 9486336 | tf_op jit(solution)/shard_map/dot_general | solution.py:76
  148.8 12.6 %collective-permute-start.4 = (bf16[4,1,64,384]{3,2,1,0:T(8,128)(2,1)S(1)}, bf16[4,1,64,384]{3,2,1,0:T(8,128)(2,1)S(1)}, u32[]{:S(2)}, u32[]{:S(2)}) collective-permute-start(bf16[4,1,64,384]{3,2,1,0:T(8,128)(2,1)S(1)} %pad_maximum_fusion.3), channel_id=1, source_target_pairs={{0,1},{1,2},{2,3},{3,4},{4,5},{5,6},{6,7},{7,8},{8,9},{9,10},{10,1... | collective-permute-start | bytes 589832 | tf_op jit(solution)/shard_map/ppermute | solution.py:25
  162.5 3.2 broadcast_in_dim.26
  165.7 5.1 %reshape.166 = bf16[4,6,128,384]{3,2,1,0:T(8,128)(2,1)S(1)} reshape(bf16[4,6,64,2,384]{4,3,2,1,0:T(2,128)(2,1)} %broadcast_in_dim.26) | data formatting | bytes 4718592 | tf_op jit(solution)/shard_map/reshape | solution.py:55
  197.7 12.0 %copy.120 = f32[384,27,192]{2,1,0:T(8,128)} copy(f32[384,27,192]{0,2,1:T(8,128)} %fusion.11) | data formatting | bytes 15925248 | tf_op jit(solution)/shard_map/stack | solution.py:100
  210.1 46.7 %all-reduce.2 = (f32[2,32]{1,0:T(2,128)S(1)}, f32[2,32]{1,0:T(2,128)S(1)}) all-reduce(f32[2,32]{1,0:T(2,128)S(1)} %reduce_sum.92, f32[2,32]{1,0:T(2,128)S(1)} %reduce_sum.90), channel_id=1, replica_groups=mesh['block'=1,'tile'=32] {'tile'}, use_global_device_ids=true, to_apply=%region_12.13 | all-reduce | flops 128 | bytes 1024 | tf_op jit(solution)/shard_map/psum | solution.py:85
  257.9 112.9 %reduce-scatter.2.cloned.1.call-done = f32[12,27,192]{2,1,0:T(8,128)} async-done(((f32[384,27,192]{2,1,0:T(8,128)}), f32[12,27,192]{2,1,0:T(8,128)}) %reduce-scatter.2.cloned.1.call-update) | async-done | bytes 248848 | tf_op jit(solution)/shard_map/reduce_scatter | solution.py:102
  (114 shorter events, 61.7 us)
Async XLA Ops:
  7.2 124.1 %all-gather.2.cloned.1.call-start = ((), (), s32[]{:S(2)}) async-start(), calls=%async_computation.1 | async-start | bytes 6488064 | tf_op jit(solution)/shard_map/all_gather | solution.py:74
  7.9 362.9 %reduce-scatter.2.cloned.1.call-start = ((), (), s32[]{:S(2)}) async-start(), calls=%async_computation.2 | async-start | bytes 12976128 | tf_op jit(solution)/shard_map/reduce_scatter | solution.py:102
  7.9 46.6 %collective-permute-start = (bf16[2,2,128,192]{2,3,1,0:T(8,128)(2,1)}, bf16[2,2,128,192]{2,3,1,0:T(8,128)(2,1)S(1)}, u32[]{:S(2)}, u32[]{:S(2)}) collective-permute-start(bf16[2,2,128,192]{2,3,1,0:T(8,128)(2,1)} %param.9), channel_id=1, source_target_pairs={} | collective-permute-start | bytes 589832 | tf_op jit(solution)/shard_map/ppermute | solution.py:15
  54.6 3.6 collective-permute-start.1
  56.3 5.5 %collective-permute-start.2 = (bf16[4,1,128,192]{2,3,1,0:T(8,128)(2,1)S(1)}, bf16[4,1,128,192]{2,3,1,0:T(8,128)(2,1)S(1)}, u32[]{:S(2)}, u32[]{:S(2)}) collective-permute-start(bf16[4,1,128,192]{2,3,1,0:T(8,128)(2,1)S(1)} %get-tuple-element.44), channel_id=1, source_target_pairs={{1,0},{2,1},{3,2},{4,3},{5,4},{6,5},{7,6},{8,7},{9,8},{10,9},{11,1... | collective-permute-start | bytes 589832 | tf_op jit(solution)/shard_map/ppermute | solution.py:26
  139.8 6.7 %copy-start.1 = (bf16[2,1,64,384]{3,2,1,0:T(8,128)(2,1)S(1)}, bf16[2,1,64,384]{3,2,1,0:T(8,128)(2,1)}, u32[]{:S(2)}) copy-start(bf16[2,1,64,384]{3,2,1,0:T(8,128)(2,1)} %param.5) | copy-start | bytes 294916
  139.8 6.7 %copy-start.2 = (f32[384]{0:T(512)S(1)}, f32[384]{0:T(512)}, u32[]{:S(2)}) copy-start(f32[384]{0:T(512)} %param.7) | copy-start | bytes 4612
  139.8 6.7 %copy-start.3 = (f32[384]{0:T(512)S(1)}, f32[384]{0:T(512)}, u32[]{:S(2)}) copy-start(f32[384]{0:T(512)} %param.6) | copy-start | bytes 4612
  146.8 0.7 collective-permute-start.3
  147.5 14.0 %collective-permute-start.5 = (bf16[4,1,64,384]{3,2,1,0:T(8,128)(2,1)S(1)}, bf16[4,1,64,384]{3,2,1,0:T(8,128)(2,1)S(1)}, u32[]{:S(2)}, u32[]{:S(2)}) collective-permute-start(bf16[4,1,64,384]{3,2,1,0:T(8,128)(2,1)S(1)} %pad_maximum_fusion.3), channel_id=1, source_target_pairs={{1,0},{2,1},{3,2},{4,3},{5,4},{6,5},{7,6},{8,7},{9,8},{10,9},{11,1... | collective-permute-start | bytes 589832 | tf_op jit(solution)/shard_map/ppermute | solution.py:26
  148.8 13.5 %collective-permute-start.4 = (bf16[4,1,64,384]{3,2,1,0:T(8,128)(2,1)S(1)}, bf16[4,1,64,384]{3,2,1,0:T(8,128)(2,1)S(1)}, u32[]{:S(2)}, u32[]{:S(2)}) collective-permute-start(bf16[4,1,64,384]{3,2,1,0:T(8,128)(2,1)S(1)} %pad_maximum_fusion.3), channel_id=1, source_target_pairs={{0,1},{1,2},{2,3},{3,4},{4,5},{5,6},{6,7},{7,8},{8,9},{9,10},{10,1... | collective-permute-start | bytes 589832 | tf_op jit(solution)/shard_map/ppermute | solution.py:25
  165.7 5.3 %copy-start = (bf16[2,2,128,192]{2,3,1,0:T(8,128)(2,1)S(1)}, bf16[2,2,128,192]{2,3,1,0:T(8,128)(2,1)}, u32[]{:S(2)}) copy-start(bf16[2,2,128,192]{2,3,1,0:T(8,128)(2,1)} %param.9) | copy-start | bytes 589828
Sparse Core Ops, SparseCore 0:
  10.9 76.7 all-gather.1
  209.8 160.9 reduce-scatter.1
where the time goes:
time: 380 us; the launch traced here: 378 us
  waiting for transfers between devices  118 us (31%)
  local copies, waits for them, and re-layouts  100 us (26%)
  blocking collectives  89.3 us (24%)
  matrix products  33.4 us (9%)
  starting transfers between devices  18.3 us (5%)
  between operations  14.5 us (4%)
  other arithmetic  3.85 us (1%)
    reduce_scatter x1, waiting for transfers between devices, shards(): lax.psum_scatter(whole_terms, 'tile', scatter_dimension=0, tiled=True)  113 us
    psum x1, blocking collectives, shards(): first_sum, second_sum = lax.psum((first_sum, second_sum), 'tile')  46.7 us
    psum x1, blocking collectives, shards(): stat_sum, stat_sq = lax.psum((stat_sum, stat_sq), 'tile')  42.5 us
    concatenate x28, local copies, waits for them, and re-layouts, shards(): columns = jnp.concatenate(windows, 1)  34.5 us
    slice x26, local copies, waits for them, and re-layouts, shards(): grad_field[2 - tap_t:2 - tap_t + frames, 2 - tap_h:2 - tap_h + up_rows, 2...  33.3 us
    dot_general x27, matrix products, shards(): lax.dot_general(window_h, flat_grads, (((0,), (0,)), ((), ())), preferred...  26.7 us
    ppermute x2, starting transfers between devices, padded_2(): before = lax.ppermute(last, axis, up)  14.3 us
    another operation x1, local copies, waits for them, and re-layouts, shards(): whole_terms = jnp.stack(term_list, 1)  12 us
  transfers between devices with their start and end apart: 8, of which 3 were waited for; matrix products, arithmetic and copies ran while one was open for 20% of the time, Pallas kernels for 0%

commit v1 on v0

v1 whole, which is shorter than its diff:
```python
import functools

import jax
import jax.numpy as jnp
from jax import lax
from jax.experimental import pallas as pl
from jax.experimental.pallas import tpu as pltpu
from jax.sharding import PartitionSpec as P

GROUPS = 32
norm_eps = 1e-06


F32 = jnp.float32
BF16 = jnp.bfloat16
SPLIT = 16


class Sizes:
    def __init__(self, acts, weights, cotangent, tiles, blocks):
        self.frames, low_rows, self.cols, self.chans = acts.shape
        self.taps, self.outs = weights.shape[1:]
        self.tiles, self.blocks = tiles, blocks
        self.inner = 1 << (tiles.bit_length() // 2)
        self.outer = tiles // self.inner
        self.pairs = self.inner // 2
        self.per = self.chans // GROUPS
        self.gp = 16
        self.rb = self.outer * self.gp
        self.cells = self.frames * self.cols
        self.wide = 2 * self.cols
        self.grad_frames = self.frames * (2 if blocks > 1 else 1)
        self.first = max(0, 3 - self.frames * blocks)
        self.used = 9 * (3 - self.first)
        self.half = (self.used + 1) // 2 * self.gp
        self.wrows = self.used * self.gp + self.half
        self.lo = 128
        self.hi = self.outs - self.lo
        self.count = float(low_rows * tiles * self.cols * self.per)
        self.edge_steps = [k for k in range(1, self.outer) if k & (k + 1) == 0]
        if low_rows != 1 or tiles != GROUPS or self.hi != 64 or self.outer > 8:
            raise ValueError("unsupported sizes")


def swap(value, mask):
    count = lax.axis_size("tile")
    return lax.ppermute(value, "tile", [(i, i ^ mask) for i in range(count)])


def place(g):
    me = lax.axis_index("tile")
    return lax.div(me, g.inner), lax.rem(me, g.inner)


def iota(shape, dim):
    return lax.broadcasted_iota(jnp.int32, shape, dim)


def dot(a, b, dims=((1,), (0,))):
    return lax.dot_general(a, b, (dims, ((), ())), preferred_element_type=F32)


def channel_select(g, w, count):
    shape = (count * g.rb, g.chans)
    row = iota(shape, 0)
    block = row >> (g.rb.bit_length() - 1)
    group = (row & (g.rb - 1)) >> 4
    lane = row & (g.gp - 1)
    chan = g.per * (g.inner * group + (w ^ block)) + lane
    return (chan == iota(shape, 1)) & (lane < g.per)


def column_select(g):
    shape = (g.cells, g.frames * 3 * g.wide)
    row, col = iota(shape, 0), iota(shape, 1)
    bits = g.wide.bit_length() - 1
    part = col >> bits
    frame, shift = part, part
    frame = (part >= 3).astype(jnp.int32)
    for f in range(2, g.frames):
        frame = frame + (part >= 3 * f).astype(jnp.int32)
    shift = part - 3 * frame
    low = ((col & (g.wide - 1)) + shift - 1) >> 1
    inside = (low >= 0) & (low < g.cols)
    return (inside & (low + frame * g.cols == row)).astype(BF16)


def split(value, parts):
    out = []
    for _ in range(parts):
        piece = value.astype(BF16)
        out.append(piece)
        value = value - piece.astype(F32)
    return out


def pack_acts_kernel(g, acts_ref, *out_refs):
    _, w = place(g)
    x = acts_ref[...].reshape(g.cells, g.chans)
    pick = channel_select(g, w, g.inner).astype(BF16)
    blocks = dot(pick, x, ((1,), (1,))).astype(BF16)
    for k, ref in enumerate(out_refs):
        ref[...] = blocks[2 * k * g.rb : 2 * (k + 1) * g.rb].reshape(2, g.rb, g.cells)


def pack_grads_kernel(g, grads_ref, out_ref):
    for t in range(g.grad_frames):
        for i in range(2):
            out_ref[3 * t + i] = grads_ref[t, i, :, : g.lo]
        out_ref[3 * t + 2] = jnp.concatenate(
            [grads_ref[t, i, :, g.lo :].astype(F32) for i in range(2)], axis=1
        ).astype(BF16)


def pack_rows(g, lo, hi):
    rest = hi[g.half :]
    if rest.shape[0] < g.half:
        rest = jnp.concatenate([rest, jnp.zeros((g.half - rest.shape[0], 128), F32)], axis=0)
    lane = iota((g.half, 128), 1)
    both = jnp.where(lane < 64, hi[: g.half], pltpu.roll(rest, 64, 1))
    return jnp.concatenate([lo, both], axis=0)


def unpack_hi(g, packed):
    lane = iota(packed.shape, 1)
    first = jnp.where(lane < 64, packed, 0.0)
    second = jnp.where(lane < 64, pltpu.roll(packed, 64, 1), 0.0)
    return jnp.concatenate([first, second], axis=0)[: g.used * g.gp]


def pack_weights_kernel(g, weights_ref, out_ref):
    rows = g.used * g.gp
    total = jnp.zeros((rows, g.outs), F32)
    row, tap = iota((rows, g.taps), 0), iota((rows, g.taps), 1)
    base = jnp.where(tap >= 9 * g.first, (tap - 9 * g.first) * g.gp, -g.gp)
    for i in range(g.per):
        total = total + dot((row == base + i).astype(BF16), weights_ref[i])
    hi = jnp.concatenate([total[:, g.lo :], jnp.zeros((rows, 64), F32)], axis=1)
    out_ref[...] = pack_rows(g, total[:, : g.lo], hi).astype(BF16)


def totals(g, first, second):
    pad = jnp.zeros((8 - g.outer, g.cells), F32)
    out = []
    for value in (first, second):
        out += [jnp.sum(value.reshape(g.outer, g.gp, g.cells), axis=1)]
        if g.outer < 8:
            out += [pad]
    return jnp.concatenate(out, axis=0)


def stats_kernel(g, *refs):
    direct, refs = refs[: g.pairs], refs[g.pairs :]
    crossed, refs = refs[: g.pairs], refs[g.pairs :]
    packed_ref, rows_ref, stats_ref, *sends = refs
    z, w = place(g)
    first = jnp.zeros((g.rb, g.cells), F32)
    second = jnp.zeros((g.rb, g.cells), F32)
    for k in range(g.pairs):
        for j, ref in enumerate((direct[k], crossed[k])):
            block = ref[j]
            rows_ref[w ^ (2 * k + j)] = block
            wide = block.astype(F32)
            first = first + wide
            second = second + wide * wide
    stats = totals(g, first, second)
    stats_ref[...] = stats
    pieces = split(stats, 3)
    for k, ref in enumerate(sends, 1):
        ref[: g.wrows] = packed_ref[...]
        for i, piece in enumerate(pieces):
            ref[g.wrows + i * SPLIT : g.wrows + (i + 1) * SPLIT] = piece
        if k in g.edge_steps:
            edge = jnp.where((z ^ k) == z + 1, g.inner - 1, 0)
            ref[g.wrows + 3 * SPLIT :] = rows_ref[edge]


def add_stats(g, own, received, start):
    for ref in received:
        for i in range(3):
            own = own + ref[start + i * SPLIT : start + (i + 1) * SPLIT].astype(F32)
    return own


def spread(g, stats):
    lane = iota((SPLIT, g.cells), 1)
    whole = jnp.zeros((SPLIT, g.cells), F32)
    for t in range(g.frames):
        mine = (lane >= t * g.cols) & (lane < (t + 1) * g.cols)
        part = jnp.sum(jnp.where(mine, stats, 0.0), axis=1, keepdims=True)
        whole = jnp.where(mine, part, whole)
    return tuple(
        jnp.concatenate(
            [
                jnp.broadcast_to(whole[s + q : s + q + 1], (g.gp, g.cells))
                for q in range(g.outer)
            ],
            axis=0,
        )
        for s in (0, 8)
    )


def main_kernel(g, *refs):
    refs = list(refs)
    take = lambda n: [refs.pop(0) for _ in range(n)]
    direct, crossed = take(g.pairs), take(g.pairs)
    rows_ref, stats_ref, packed_ref = take(3)
    received = take(g.outer - 1)
    gamma_ref, beta_ref = take(2)
    sends = take(g.outer - 1)
    own_ref, sums_ref, grad_ref, normed_ref, inv_ref = take(5)
    xs, wl, acc, hidden, slope, ups, field = refs
    z, w = place(g)
    rb, wide, frames = g.rb, g.wide, g.frames

    for k in range(g.pairs):
        for j, ref in enumerate((direct[k], crossed[k])):
            row = w ^ (2 * k + j)
            for t in range(g.grad_frames):
                both = ref[3 * t + 2]
                other = pltpu.roll(both.astype(F32), 64, 1).astype(BF16)
                for i, hi in enumerate((both, other)):
                    xs[t, row, i * wide : (i + 1) * wide, : g.lo] = ref[3 * t + i]
                    xs[t, row, i * wide : (i + 1) * wide, g.lo :] = hi

    for k in range(g.outer):
        ref = packed_ref if k == 0 else received[k - 1]
        rows = g.used * g.gp
        wl[:, z ^ k, :, : g.lo] = ref[:rows].reshape(g.used, g.gp, g.lo)
        hi = unpack_hi(g, ref[rows : g.wrows].astype(F32)).astype(BF16)
        wl[:, z ^ k, :, g.lo :] = hi.reshape(g.used, g.gp, 128)

    stats = add_stats(g, stats_ref[...], received, g.wrows)
    total, total_sq = spread(g, stats)
    mean = total / g.count
    inv = lax.rsqrt(total_sq / g.count - mean * mean + norm_eps)
    inv_ref[...] = inv
    pick = channel_select(g, w, 1)
    gamma = jnp.sum(jnp.where(pick, gamma_ref[...], 0.0), axis=1, keepdims=True)
    beta = jnp.sum(jnp.where(pick, beta_ref[...], 0.0), axis=1, keepdims=True)

    def activate(place_at, block, present):
        normed = (block.astype(F32) - mean) * inv
        shifted = normed * gamma + beta
        gate = jax.nn.sigmoid(shifted)
        normed_ref[place_at] = normed
        hidden[place_at] = (shifted * gate * present).astype(BF16)
        slope[place_at] = gate * (1.0 + shifted * (1.0 - gate)) * gamma * present

    for place_at, step in ((0, -1), (g.inner + 1, 1)):
        block = jnp.zeros((rb, g.cells), BF16)
        for k in g.edge_steps:
            at = g.wrows + 3 * SPLIT
            block = jnp.where((z ^ k) == z + step, received[k - 1][at : at + rb], block)
        inside = (z + step >= 0) & (z + step < g.outer)
        activate(place_at, block, jnp.where(inside, 1.0, 0.0))

    @pl.loop(0, g.inner)
    def _(i):
        activate(i + 1, rows_ref[i], 1.0)

    select = column_select(g)
    count = g.inner + 2
    ups[...] = (
        dot(hidden[...].reshape(count * rb, g.cells), select)
        .astype(BF16)
        .reshape(count, rb, frames * 3 * wide)
    )

    acc[...] = jnp.zeros_like(acc)
    field[...] = jnp.zeros_like(field)

    @pl.loop(0, g.inner)
    def _(i):
        for later in range(g.grad_frames):
            x = xs[later, i]
            for a in range(g.first, 3):
                t = later + a - 2
                if t < 0 or t >= frames:
                    continue
                taps = slice(9 * (a - g.first), 9 * (a - g.first + 1))
                lanes = [slice((3 * t + e) * wide, (3 * t + e + 1) * wide) for e in range(3)]
                pieces = []
                for upper, lower in ((0, 1), (1, 1), (1, 2)):
                    for e in range(3):
                        pieces.append(
                            jnp.concatenate(
                                [ups[i + upper, :, lanes[e]], ups[i + lower, :, lanes[e]]], axis=1
                            )
                        )
                terms = dot(jnp.concatenate(pieces, axis=0), x)
                acc[taps] += terms.reshape(9, g.outer, g.gp, 256)
                back = dot(wl[taps].reshape(9 * rb, 256), x, ((1,), (1,)))
                part = lambda b, e, fine: back[
                    (3 * b + e) * rb : (3 * b + e + 1) * rb, fine * wide : (fine + 1) * wide
                ]
                for e in range(3):
                    field[i, :, lanes[e]] += part(0, e, 0)
                    field[i + 1, :, lanes[e]] += (part(1, e, 0) + part(2, e, 0)) + (
                        part(0, e, 1) + part(1, e, 1)
                    )
                    field[i + 2, :, lanes[e]] += part(2, e, 1)

    flat = field[...].reshape(count * rb, frames * 3 * wide)
    pieces = split(flat, 2)
    act_grad = dot(pieces[0], select, ((1,), (1,))) + dot(pieces[1], select, ((1,), (1,)))
    grad = act_grad.reshape(count, rb, g.cells) * slope[...]
    grad_ref[...] = grad
    sums = totals(g, jnp.sum(grad, axis=0), jnp.sum(grad * normed_ref[...], axis=0))
    sums_ref[...] = sums

    own_ref[...] = acc[:, z].reshape(g.used * g.gp, 256)
    parts = split(sums, 3)
    for k, ref in enumerate(sends, 1):
        terms = acc[:, z ^ k].reshape(g.used * g.gp, 256)
        ref[: g.wrows] = pack_rows(g, terms[:, : g.lo], terms[:, g.lo :]).astype(BF16)
        for i, piece in enumerate(parts):
            ref[g.wrows + i * SPLIT : g.wrows + (i + 1) * SPLIT] = piece
        if k in g.edge_steps:
            edge = grad_ref[jnp.where((z ^ k) == z + 1, g.inner + 1, 0)]
            for i, piece in enumerate(split(edge, 2)):
                at = g.wrows + 3 * SPLIT + i * rb
                ref[at : at + rb] = piece


def finish_kernel(g, *refs):
    refs = list(refs)
    take = lambda n: [refs.pop(0) for _ in range(n)]
    sums_ref, grad_ref, normed_ref, inv_ref = take(4)
    received = take(g.outer - 1)
    sends = refs
    z, w = place(g)
    sums = add_stats(g, sums_ref[...], received, g.wrows)
    first, second = spread(g, sums)
    first, second = first / g.count, second / g.count
    inv = inv_ref[...]
    edges = []
    for step in (-1, 1):
        edge = jnp.zeros((g.rb, g.cells), F32)
        for k in g.edge_steps:
            at = g.wrows + 3 * SPLIT
            value = received[k - 1][at : at + g.rb].astype(F32)
            value = value + received[k - 1][at + g.rb : at + 2 * g.rb].astype(F32)
            edge = jnp.where((z ^ k) == z + step, value, edge)
        edges.append(edge)
    for k, ref in enumerate(sends):
        for j in range(2):
            row = w ^ (2 * k + j)
            grad = grad_ref[row + 1]
            grad = grad + jnp.where(row == 0, edges[0], 0.0)
            grad = grad + jnp.where(row == g.inner - 1, edges[1], 0.0)
            ref[j] = (inv * (grad - first - normed_ref[row + 1] * second)).astype(BF16)


def unpack_acts_kernel(g, *refs):
    direct, crossed, out_ref = refs[: g.pairs], refs[g.pairs : 2 * g.pairs], refs[-1]
    _, w = place(g)
    pick = channel_select(g, w, g.inner).astype(BF16)
    blocks = []
    for k in range(g.pairs):
        blocks += [direct[k][0], crossed[k][1]]
    out = dot(jnp.concatenate(blocks, axis=0), pick, ((0,), (0,)))
    out_ref[...] = out.astype(BF16).reshape(out_ref.shape)


def unpack_weights_kernel(g, own_ref, *refs):
    *received, out_ref, low, high = refs
    rows = g.used * g.gp
    lo = own_ref[:, : g.lo]
    hi = jnp.zeros((g.half, 128), F32)
    for ref in received:
        lo = lo + ref[:rows].astype(F32)
        hi = hi + ref[rows : g.wrows].astype(F32)
    low[...] = lo
    high[...] = own_ref[:, g.lo :] + unpack_hi(g, hi)
    for i in range(g.per):
        at = pl.ds(i, g.used, stride=g.gp)
        if g.first:
            out_ref[i, : 9 * g.first, :] = jnp.zeros((9 * g.first, g.outs), F32)
        out_ref[i, 9 * g.first :, : g.lo] = low[at, :]
        out_ref[i, 9 * g.first :, g.lo :] = high[at, :][:, : g.hi]


def call(g, kernel, name, outs, args, scratch=(), flops=0):
    shapes = [jax.ShapeDtypeStruct(shape, kind) for shape, kind in outs]
    whole = pl.BlockSpec(memory_space=pltpu.VMEM)
    moved = sum(a.size * a.dtype.itemsize for a in list(args) + shapes)
    return pl.pallas_call(
        functools.partial(kernel, g),
        out_shape=shapes,
        in_specs=[whole] * len(args),
        out_specs=[whole] * len(shapes),
        scratch_shapes=list(scratch),
        compiler_params=pltpu.CompilerParams(vmem_limit_bytes=48 * 1024 * 1024),
        cost_estimate=pl.CostEstimate(flops=flops, bytes_accessed=moved, transcendentals=0),
        name=name,
    )(*args)


def shards(acts, gamma, beta, weights, cotangent):
    g = Sizes(acts, weights, cotangent, lax.axis_size("tile"), lax.axis_size("block"))
    if g.blocks > 1:
        pairs = [(i + 1, i) for i in range(g.blocks - 1)]
        following = lax.ppermute(cotangent, "block", pairs)
        cotangent = jnp.concatenate([cotangent, following], 0)
    block = ((2, g.rb, g.cells), BF16)
    sends = call(g, pack_acts_kernel, "pack_acts", [block] * g.pairs, [acts])
    acts_direct = [sends[0]] + [swap(sends[k], 2 * k) for k in range(1, g.pairs)]

    grads_shape = ((3 * g.grad_frames, g.wide, 128), BF16)
    (packed_grads,) = call(g, pack_grads_kernel, "pack_grads", [grads_shape], [cotangent])
    grads_direct = [packed_grads] + [swap(packed_grads, 2 * k) for k in range(1, g.pairs)]

    acts_crossed = [swap(v, 1) for v in acts_direct]
    (packed,) = call(
        g, pack_weights_kernel, "pack_weights", [((g.wrows, 128), BF16)], [weights]
    )

    stats_shape = ((SPLIT, g.cells), F32)
    steps = range(1, g.outer)
    extra = [g.rb if k in g.edge_steps else 0 for k in steps]
    rows, stats, *sends = call(
        g,
        stats_kernel,
        "stats",
        [((g.inner, g.rb, g.cells), BF16), stats_shape]
        + [((g.wrows + 3 * SPLIT + n, 128), BF16) for n in extra],
        acts_direct + acts_crossed + [packed],
    )
    received = [swap(v, g.inner * k) for k, v in zip(steps, sends)]
    grads_crossed = [swap(v, 1) for v in grads_direct]

    count = g.inner + 2
    outs = [((g.wrows + 3 * SPLIT + 2 * n, 128), BF16) for n in extra]
    outs += [((g.used * g.gp, 256), F32), stats_shape]
    outs += [((count, g.rb, g.cells), F32)] * 2 + [((g.rb, g.cells), F32)]
    scratch = [
        pltpu.VMEM((g.grad_frames, g.inner, 2 * g.wide, 256), BF16),
        pltpu.VMEM((g.used, g.outer, g.gp, 256), BF16),
        pltpu.VMEM((g.used, g.outer, g.gp, 256), F32),
        pltpu.VMEM((count, g.rb, g.cells), BF16),
        pltpu.VMEM((count, g.rb, g.cells), F32),
        pltpu.VMEM((count, g.rb, g.frames * 3 * g.wide), BF16),
        pltpu.VMEM((count, g.rb, g.frames * 3 * g.wide), F32),
    ]
    *sends, own, sums, grad, normed, inv = call(
        g,
        main_kernel,
        "main",
        outs,
        grads_direct
        + grads_crossed
        + [rows, stats, packed]
        + received
        + [gamma.reshape(1, -1), beta.reshape(1, -1)],
        scratch,
        flops=2 * 4 * g.inner * 9 * g.rb * 256 * 256 * g.grad_frames,
    )
    received = [swap(v, g.inner * k) for k, v in zip(steps, sends)]
    sends = call(
        g, finish_kernel, "finish", [block] * g.pairs, [sums, grad, normed, inv] + received
    )
    direct = [sends[0]] + [swap(sends[k], 2 * k) for k in range(1, g.pairs)]
    crossed = [swap(v, 1) for v in direct]
    (d_acts,) = call(
        g, unpack_acts_kernel, "unpack_acts", [(acts.shape, BF16)], direct + crossed
    )
    (d_weights,) = call(
        g,
        unpack_weights_kernel,
        "unpack_weights",
        [(weights.shape, F32)],
        [own] + received,
        [pltpu.VMEM((g.used * g.gp, 128), F32)] * 2,
    )
    if g.blocks > 1:
        d_weights = lax.psum(d_weights, "block")
    return (d_acts, d_weights)


def solution(mesh):
    placed = (
        P("block", "tile", None, None),
        P(),
        P(),
        P("tile", None, None),
        P("block", "tile", None, None),
    )
    return jax.shard_map(
        shards,
        mesh=mesh,
        in_specs=placed,
        out_specs=(P("block", "tile", None, None), P("tile", None, None)),
        check_vma=False,
    )
```

time: 380 us -> 68 us (0.18)
  local copies, waits for them, and re-layouts: 100 us -> 1.97 us
  blocking collectives: 89.3 us -> 0 us
  waiting for transfers between devices: 118 us -> 31.4 us
  matrix products: 33.4 us -> 0 us
  between operations: 14.5 us -> 0.73 us
  Pallas kernels: 0 us -> 10.4 us
  starting transfers between devices: 18.3 us -> 23.3 us
  other arithmetic: 3.85 us -> 0 us
    reduce_scatter x1 -> x0, waiting for transfers between devices: 113 us -> none  [shards(): lax.psum_scatter(whole_terms, 'tile', scatter_dimension=0, tiled=True)]
    psum x2 -> x0, blocking collectives: 89.3 us -> none  [the longest x1 46.7 us: shards(): first_sum, second_sum = lax.psum((first_sum, second_sum), 'tile')]
    concatenate x29 -> x0, local copies, waits for them, and re-layouts: 34.5 us -> none  [the longest x28 34.5 us: shards(): columns = jnp.concatenate(windows, 1)]
    slice x28 -> x0, local copies, waits for them, and re-layouts: 33.5 us -> none  [the longest x26 33.3 us: shards(): grad_field[2 - tap_t:2 - tap_t + frames, 2 - tap_h:2 - tap_h + up_rows, 2...]
    dot_general x28 -> x0, matrix products: 33.4 us -> none  [the longest x27 26.7 us: shards(): lax.dot_general(window_h, flat_grads, (((0,), (0,)), ((), ())), preferred...]
    ppermute x6 -> x27, waiting for transfers between devices: 4.37 us -> 31.4 us  [swap(): return lax.ppermute(value, 'tile', [(i, i ^ mask) for i in range(count)])]
    another operation x1 -> x0, local copies, waits for them, and re-layouts: 12 us -> none  [shards(): whole_terms = jnp.stack(term_list, 1)]
    pallas_call x0 -> x8, Pallas kernels: none -> 10.4 us  [call(): pl.pallas_call(functools.partial(kernel, g), out_shape=shapes, in_specs=[...]
  transfers between devices with their start and end apart: 8 -> 27, of which waited for: 3 -> 14; matrix products, arithmetic and copies ran while one was open for 20% -> 2% of each run, Pallas kernels for 0% -> 3%
where the time goes in v1:
time: 68 us; the launch traced here: 67.8 us
  waiting for transfers between devices  31.4 us (46%)
  starting transfers between devices  23.3 us (34%)
  Pallas kernels  10.4 us (15%)
  local copies, waits for them, and re-layouts  1.97 us (3%)
  between operations  0.73 us (1%)
    ppermute x27, waiting for transfers between devices, swap(): return lax.ppermute(value, 'tile', [(i, i ^ mask) for i in range(count)])  31.4 us
    ppermute x27, starting transfers between devices, swap(): return lax.ppermute(value, 'tile', [(i, i ^ mask) for i in range(count)])  23.3 us
    pallas_call x8, Pallas kernels, call(): pl.pallas_call(functools.partial(kernel, g), out_shape=shapes, in_specs=[...  10.4 us
    unnamed x9, local copies, waits for them, and re-layouts  1.96 us
  transfers between devices with their start and end apart: 27, of which 14 were waited for; matrix products, arithmetic and copies ran while one was open for 2% of the time, Pallas kernels for 3%

profile of v1, /device:TPU:0, one launch (start us, length us, event | category | flops | bytes accessed | tf_op | source)
XLA Modules:
  0.0 67.8 jit_solution(15055376134166063955)
XLA Ops:
  0.6 0.9 %copy-done.1 = bf16[2,1,64,384]{3,2,1,0:T(8,128)(2,1)S(1)} copy-done((bf16[2,1,64,384]{3,2,1,0:T(8,128)(2,1)S(1)}, bf16[2,1,64,384]{3,2,1,0:T(8,128)(2,1)}, u32[]{:S(2)}) %copy-start.1) | copy-done | bytes 98328
  1.5 0.3 pack_acts.1
  1.8 3.0 %collective-permute-start.7 = (bf16[2,64,128]{2,1,0:T(8,128)(2,1)S(1)}, bf16[2,64,128]{2,1,0:T(8,128)(2,1)S(1)}, u32[]{:S(2)}, u32[]{:S(2)}) collective-permute-start(bf16[2,64,128]{2,1,0:T(8,128)(2,1)S(1)} %get-tuple-element.24), channel_id=1, source_target_pairs={{0,2},{1,3},{2,0},{3,1},{4,6},{5,7},{6,4},{7,5},{8,10},{9,11},{10,... | collective-permute-start | bytes 98312 | tf_op jit(solution)/shard_map/ppermute | solution.py:47
  4.8 1.5 %collective-permute-start.8 = (bf16[2,64,128]{2,1,0:T(8,128)(2,1)S(1)}, bf16[2,64,128]{2,1,0:T(8,128)(2,1)S(1)}, u32[]{:S(2)}, u32[]{:S(2)}) collective-permute-start(bf16[2,64,128]{2,1,0:T(8,128)(2,1)S(1)} %get-tuple-element.25), channel_id=1, source_target_pairs={{0,4},{1,5},{2,6},{3,7},{4,0},{5,1},{6,2},{7,3},{8,12},{9,13},{10,... | collective-permute-start | bytes 98312 | tf_op jit(solution)/shard_map/ppermute | solution.py:47
  6.4 1.1 %copy.7.grads_ref = bf16[2,2,128,192]{3,2,1,0:T(8,128)(2,1)S(1)} copy(bf16[2,2,128,192]{2,3,1,0:T(8,128)(2,1)} %param.9) | data formatting | bytes 393216 | tf_op args[4]
  7.5 3.0 %collective-permute-start.2 = (bf16[6,128,128]{2,1,0:T(8,128)(2,1)S(1)}, bf16[6,128,128]{2,1,0:T(8,128)(2,1)S(1)}, u32[]{:S(2)}, u32[]{:S(2)}) collective-permute-start(bf16[6,128,128]{2,1,0:T(8,128)(2,1)S(1)} %pack_grads.1.refs_0_), channel_id=1, source_target_pairs={{0,6},{1,7},{2,4},{3,5},{4,2},{5,3},{6,0},{7,1},{8,14},{9,15},{10,... | collective-permute-start | bytes 589832 | tf_op jit(solution)/shard_map/ppermute | solution.py:47
  10.5 0.5 collective-permute-start.1
  11.7 0.7 %collective-permute-done.10.refs_4_ = bf16[2,64,128]{2,1,0:T(8,128)(2,1)S(1)} collective-permute-done((bf16[2,64,128]{2,1,0:T(8,128)(2,1)S(1)}, bf16[2,64,128]{2,1,0:T(8,128)(2,1)S(1)}, u32[]{:S(2)}, u32[]{:S(2)}) %collective-permute-start.10) | collective-permute-done | bytes 32800 | tf_op jit(solution)/shard_map/ppermute | solution.py:47
  12.9 1.0 %collective-permute-done.12.refs_6_ = bf16[2,64,128]{2,1,0:T(8,128)(2,1)S(1)} collective-permute-done((bf16[2,64,128]{2,1,0:T(8,128)(2,1)S(1)}, bf16[2,64,128]{2,1,0:T(8,128)(2,1)S(1)}, u32[]{:S(2)}, u32[]{:S(2)}) %collective-permute-start.12) | collective-permute-done | bytes 32800 | tf_op jit(solution)/shard_map/ppermute | solution.py:47
  14.1 0.7 pack_weights.1.refs_8_.refs_10_
  14.8 0.3 collective-permute-done.13.refs_7_
  15.2 3.1 %collective-permute-start.15 = (bf16[480,128]{1,0:T(8,128)(2,1)S(1)}, bf16[480,128]{1,0:T(8,128)(2,1)S(1)}, u32[]{:S(2)}, u32[]{:S(2)}) collective-permute-start(bf16[480,128]{1,0:T(8,128)(2,1)S(1)} %get-tuple-element.30), channel_id=1, source_target_pairs={{0,16},{1,17},{2,18},{3,19},{4,20},{5,21},{6,22},{7,23},{8,24},{9,... | collective-permute-start | bytes 368648 | tf_op jit(solution)/shard_map/ppermute | solution.py:47
  18.2 0.9 %collective-permute-done.1.refs_2_ = bf16[6,128,128]{2,1,0:T(8,128)(2,1)S(1)} collective-permute-done((bf16[6,128,128]{2,1,0:T(8,128)(2,1)S(1)}, bf16[6,128,128]{2,1,0:T(8,128)(2,1)S(1)}, u32[]{:S(2)}, u32[]{:S(2)}) %collective-permute-start.1) | collective-permute-done | bytes 196640 | tf_op jit(solution)/shard_map/ppermute | solution.py:47
  19.2 0.5 collective-permute-start.4
  19.7 4.9 %collective-permute-done.15.refs_12_ = bf16[480,128]{1,0:T(8,128)(2,1)S(1)} collective-permute-done((bf16[480,128]{1,0:T(8,128)(2,1)S(1)}, bf16[480,128]{1,0:T(8,128)(2,1)S(1)}, u32[]{:S(2)}, u32[]{:S(2)}) %collective-permute-start.15) | collective-permute-done | bytes 122912 | tf_op jit(solution)/shard_map/ppermute | solution.py:47
  24.6 0.7 %collective-permute-start.14 = (bf16[544,128]{1,0:T(8,128)(2,1)S(1)}, bf16[544,128]{1,0:T(8,128)(2,1)S(1)}, u32[]{:S(2)}, u32[]{:S(2)}) collective-permute-start(bf16[544,128]{1,0:T(8,128)(2,1)S(1)} %get-tuple-element.29), channel_id=1, source_target_pairs={{0,8},{1,9},{2,10},{3,11},{4,12},{5,13},{6,14},{7,15},{8,0},{9,1},... | collective-permute-start | bytes 417800 | tf_op jit(solution)/shard_map/ppermute | solution.py:47
  25.3 2.9 %collective-permute-start.16 = (bf16[544,128]{1,0:T(8,128)(2,1)S(1)}, bf16[544,128]{1,0:T(8,128)(2,1)S(1)}, u32[]{:S(2)}, u32[]{:S(2)}) collective-permute-start(bf16[544,128]{1,0:T(8,128)(2,1)S(1)} %get-tuple-element.31), channel_id=1, source_target_pairs={{0,24},{1,25},{2,26},{3,27},{4,28},{5,29},{6,30},{7,31},{8,16},{9,... | collective-permute-start | bytes 417800 | tf_op jit(solution)/shard_map/ppermute | solution.py:47
  28.2 1.7 %collective-permute-done.14.refs_11_ = bf16[544,128]{1,0:T(8,128)(2,1)S(1)} collective-permute-done((bf16[544,128]{1,0:T(8,128)(2,1)S(1)}, bf16[544,128]{1,0:T(8,128)(2,1)S(1)}, u32[]{:S(2)}, u32[]{:S(2)}) %collective-permute-start.14) | collective-permute-done | bytes 139296 | tf_op jit(solution)/shard_map/ppermute | solution.py:47
  29.9 5.2 %collective-permute-done.16.refs_13_ = bf16[544,128]{1,0:T(8,128)(2,1)S(1)} collective-permute-done((bf16[544,128]{1,0:T(8,128)(2,1)S(1)}, bf16[544,128]{1,0:T(8,128)(2,1)S(1)}, u32[]{:S(2)}, u32[]{:S(2)}) %collective-permute-start.16) | collective-permute-done | bytes 139296 | tf_op jit(solution)/shard_map/ppermute | solution.py:47
  35.1 7.3 %main.1 = (bf16[608,128]{1,0:T(8,128)(2,1)S(1)}, bf16[480,128]{1,0:T(8,128)(2,1)S(1)}, bf16[608,128]{1,0:T(8,128)(2,1)S(1)}, f32[288,256]{1,0:T(8,128)S(1)}, f32...) custom-call(bf16[6,128,128]{2,1,0:T(8,128)(2,1)S(1)} %pack_grads.1.refs_0_,, ...), custom_call_target="tpu_custom_call" | custom-call | flops 4831838208 | bytes 3652608 | tf_op jit(solution)/shard_map/main/pallas_call | solution.py:389
  42.4 0.8 %collective-permute-start.17 = (bf16[608,128]{1,0:T(8,128)(2,1)S(1)}, bf16[608,128]{1,0:T(8,128)(2,1)S(1)}, u32[]{:S(2)}, u32[]{:S(2)}) collective-permute-start(bf16[608,128]{1,0:T(8,128)(2,1)S(1)} %get-tuple-element.36), channel_id=1, source_target_pairs={{0,8},{1,9},{2,10},{3,11},{4,12},{5,13},{6,14},{7,15},{8,0},{9,1},... | collective-permute-start | bytes 466952 | tf_op jit(solution)/shard_map/ppermute | solution.py:47
  43.2 2.6 %collective-permute-start.19 = (bf16[608,128]{1,0:T(8,128)(2,1)S(1)}, bf16[608,128]{1,0:T(8,128)(2,1)S(1)}, u32[]{:S(2)}, u32[]{:S(2)}) collective-permute-start(bf16[608,128]{1,0:T(8,128)(2,1)S(1)} %get-tuple-element.38), channel_id=1, source_target_pairs={{0,24},{1,25},{2,26},{3,27},{4,28},{5,29},{6,30},{7,31},{8,16},{9,... | collective-permute-start | bytes 466952 | tf_op jit(solution)/shard_map/ppermute | solution.py:47
  45.9 11.7 %collective-permute-done.18.refs_5_.refs_1_ = bf16[480,128]{1,0:T(8,128)(2,1)S(1)} collective-permute-done((bf16[480,128]{1,0:T(8,128)(2,1)S(1)}, bf16[480,128]{1,0:T(8,128)(2,1)S(1)}, u32[]{:S(2)}, u32[]{:S(2)}) %collective-permute-start.18) | collective-permute-done | bytes 122912 | tf_op jit(solution)/shard_map/ppermute | solution.py:47
  57.7 1.6 %collective-permute-start.20 = (bf16[2,64,128]{2,1,0:T(8,128)(2,1)S(1)}, bf16[2,64,128]{2,1,0:T(8,128)(2,1)S(1)}, u32[]{:S(2)}, u32[]{:S(2)}) collective-permute-start(bf16[2,64,128]{2,1,0:T(8,128)(2,1)S(1)} %get-tuple-element.40), channel_id=1, source_target_pairs={{0,2},{1,3},{2,0},{3,1},{4,6},{5,7},{6,4},{7,5},{8,10},{9,11},{10,... | collective-permute-start | bytes 98312 | tf_op jit(solution)/shard_map/ppermute | solution.py:47
  59.3 1.5 %collective-permute-start.21 = (bf16[2,64,128]{2,1,0:T(8,128)(2,1)S(1)}, bf16[2,64,128]{2,1,0:T(8,128)(2,1)S(1)}, u32[]{:S(2)}, u32[]{:S(2)}) collective-permute-start(bf16[2,64,128]{2,1,0:T(8,128)(2,1)S(1)} %get-tuple-element.41), channel_id=1, source_target_pairs={{0,4},{1,5},{2,6},{3,7},{4,0},{5,1},{6,2},{7,3},{8,12},{9,13},{10,... | collective-permute-start | bytes 98312 | tf_op jit(solution)/shard_map/ppermute | solution.py:47
  60.8 0.5 collective-permute-start.22
  61.3 0.6 collective-permute-done.20.refs_1_
  61.9 1.4 %collective-permute-done.21.refs_2_ = bf16[2,64,128]{2,1,0:T(8,128)(2,1)S(1)} collective-permute-done((bf16[2,64,128]{2,1,0:T(8,128)(2,1)S(1)}, bf16[2,64,128]{2,1,0:T(8,128)(2,1)S(1)}, u32[]{:S(2)}, u32[]{:S(2)}) %collective-permute-start.21) | collective-permute-done | bytes 32800 | tf_op jit(solution)/shard_map/ppermute | solution.py:47
  63.2 2.4 %collective-permute-done.22.refs_3_ = bf16[2,64,128]{2,1,0:T(8,128)(2,1)S(1)} collective-permute-done((bf16[2,64,128]{2,1,0:T(8,128)(2,1)S(1)}, bf16[2,64,128]{2,1,0:T(8,128)(2,1)S(1)}, u32[]{:S(2)}, u32[]{:S(2)}) %collective-permute-start.22) | collective-permute-done | bytes 32800 | tf_op jit(solution)/shard_map/ppermute | solution.py:47
  65.6 0.9 %unpack_weights.1 = f32[12,27,192]{2,1,0:T(8,128)} custom-call(f32[288,256]{1,0:T(8,128)S(1)} %get-tuple-element.43.own_ref, bf16[608,128]{1,0:T(8,128)(2,1)S(1)} %collective-permute-done.17.refs_4_.refs_0_, bf16[480,128]{1,0:T(8,128)(2,1)S(1)} %collective-permute-done.18.refs_5_.refs_1_, bf16[608,128]{1,0:T(8,128)(2,1)S(1)} %collective-permute-done.19.refs_6_.refs_2_), custom_call_target="tpu_custom_call" | custom-call | bytes 977920 | tf_op jit(solution)/shard_map/unpack_weights/pallas_call | solution.py:389
  66.6 0.3 collective-permute-done.26.refs_7_
  66.8 1.0 %unpack_acts.1 = bf16[2,1,64,384]{3,2,1,0:T(8,128)(2,1)} custom-call(bf16[2,64,128]{2,1,0:T(8,128)(2,1)S(1)} %get-tuple-element.39.refs_0_, bf16[2,64,128]{2,1,0:T(8,128)(2,1)S(1)} %collective-permute-done.20.refs_1_, bf16[2,64,128]{2,1,0:T(8,128)(2,1)S(1)} %collective-permute-done.21.refs_2_, bf16[2,64,128]{2,1,0:T(8,128)(2,1)S(1)} %collective-permute-done.22.refs_3_, ...), custom_call_target="tpu_custom_call" | custom-call | bytes 360448 | tf_op jit(solution)/shard_map/unpack_acts/pallas_call | solution.py:389
  (41 shorter events, 1.9 us)
Async XLA Ops:
  0.6 0.9 %copy-start.1 = (bf16[2,1,64,384]{3,2,1,0:T(8,128)(2,1)S(1)}, bf16[2,1,64,384]{3,2,1,0:T(8,128)(2,1)}, u32[]{:S(2)}) copy-start(bf16[2,1,64,384]{3,2,1,0:T(8,128)(2,1)} %acts_ref.1) | copy-start | bytes 294916
  1.8 9.2 %collective-permute-start.7 = (bf16[2,64,128]{2,1,0:T(8,128)(2,1)S(1)}, bf16[2,64,128]{2,1,0:T(8,128)(2,1)S(1)}, u32[]{:S(2)}, u32[]{:S(2)}) collective-permute-start(bf16[2,64,128]{2,1,0:T(8,128)(2,1)S(1)} %get-tuple-element.24), channel_id=1, source_target_pairs={{0,2},{1,3},{2,0},{3,1},{4,6},{5,7},{6,4},{7,5},{8,10},{9,11},{10,... | collective-permute-start | bytes 98312 | tf_op jit(solution)/shard_map/ppermute | solution.py:47
  4.8 6.3 %collective-permute-start.8 = (bf16[2,64,128]{2,1,0:T(8,128)(2,1)S(1)}, bf16[2,64,128]{2,1,0:T(8,128)(2,1)S(1)}, u32[]{:S(2)}, u32[]{:S(2)}) collective-permute-start(bf16[2,64,128]{2,1,0:T(8,128)(2,1)S(1)} %get-tuple-element.25), channel_id=1, source_target_pairs={{0,4},{1,5},{2,6},{3,7},{4,0},{5,1},{6,2},{7,3},{8,12},{9,13},{10,... | collective-permute-start | bytes 98312 | tf_op jit(solution)/shard_map/ppermute | solution.py:47
  6.3 5.1 %collective-permute-start.9 = (bf16[2,64,128]{2,1,0:T(8,128)(2,1)S(1)}, bf16[2,64,128]{2,1,0:T(8,128)(2,1)S(1)}, u32[]{:S(2)}, u32[]{:S(2)}) collective-permute-start(bf16[2,64,128]{2,1,0:T(8,128)(2,1)S(1)} %get-tuple-element.26), channel_id=1, source_target_pairs={{0,6},{1,7},{2,4},{3,5},{4,2},{5,3},{6,0},{7,1},{8,14},{9,15},{10,... | collective-permute-start | bytes 98312 | tf_op jit(solution)/shard_map/ppermute | solution.py:47
  7.4 6.7 %copy-start = (bf16[12,27,192]{2,1,0:T(8,128)(2,1)S(1)}, bf16[12,27,192]{2,1,0:T(8,128)(2,1)}, u32[]{:S(2)}) copy-start(bf16[12,27,192]{2,1,0:T(8,128)(2,1)} %weights_ref.1) | copy-start | bytes 373252
  7.5 10.7 %collective-permute-start.2 = (bf16[6,128,128]{2,1,0:T(8,128)(2,1)S(1)}, bf16[6,128,128]{2,1,0:T(8,128)(2,1)S(1)}, u32[]{:S(2)}, u32[]{:S(2)}) collective-permute-start(bf16[6,128,128]{2,1,0:T(8,128)(2,1)S(1)} %pack_grads.1.refs_0_), channel_id=1, source_target_pairs={{0,6},{1,7},{2,4},{3,5},{4,2},{5,3},{6,0},{7,1},{8,14},{9,15},{10,... | collective-permute-start | bytes 589832 | tf_op jit(solution)/shard_map/ppermute | solution.py:47
  10.5 8.6 %collective-permute-start.1 = (bf16[6,128,128]{2,1,0:T(8,128)(2,1)S(1)}, bf16[6,128,128]{2,1,0:T(8,128)(2,1)S(1)}, u32[]{:S(2)}, u32[]{:S(2)}) collective-permute-start(bf16[6,128,128]{2,1,0:T(8,128)(2,1)S(1)} %pack_grads.1.refs_0_), channel_id=1, source_target_pairs={{0,4},{1,5},{2,6},{3,7},{4,0},{5,1},{6,2},{7,3},{8,12},{9,13},{10,... | collective-permute-start | bytes 589832 | tf_op jit(solution)/shard_map/ppermute | solution.py:47
  11.0 8.1 %collective-permute-start = (bf16[6,128,128]{2,1,0:T(8,128)(2,1)S(1)}, bf16[6,128,128]{2,1,0:T(8,128)(2,1)S(1)}, u32[]{:S(2)}, u32[]{:S(2)}) collective-permute-start(bf16[6,128,128]{2,1,0:T(8,128)(2,1)S(1)} %pack_grads.1.refs_0_), channel_id=1, source_target_pairs={{0,2},{1,3},{2,0},{3,1},{4,6},{5,7},{6,4},{7,5},{8,10},{9,11},{10,... | collective-permute-start | bytes 589832 | tf_op jit(solution)/shard_map/ppermute | solution.py:47
  11.2 1.2 %collective-permute-start.10 = (bf16[2,64,128]{2,1,0:T(8,128)(2,1)S(1)}, bf16[2,64,128]{2,1,0:T(8,128)(2,1)S(1)}, u32[]{:S(2)}, u32[]{:S(2)}) collective-permute-start(bf16[2,64,128]{2,1,0:T(8,128)(2,1)S(1)} %get-tuple-element.23.refs_0_), channel_id=1, source_target_pairs={{0,1},{1,0},{2,3},{3,2},{4,5},{5,4},{6,7},{7,6},{8,9},{9,8},{10,11... | collective-permute-start | bytes 98312 | tf_op jit(solution)/shard_map/ppermute | solution.py:47
  11.4 1.2 %collective-permute-start.11 = (bf16[2,64,128]{2,1,0:T(8,128)(2,1)S(1)}, bf16[2,64,128]{2,1,0:T(8,128)(2,1)S(1)}, u32[]{:S(2)}, u32[]{:S(2)}) collective-permute-start(bf16[2,64,128]{2,1,0:T(8,128)(2,1)S(1)} %collective-permute-done.7.refs_1_), channel_id=1, source_target_pairs={{0,1},{1,0},{2,3},{3,2},{4,5},{5,4},{6,7},{7,6},{8,9},{9,8},{10,11... | collective-permute-start | bytes 98312 | tf_op jit(solution)/shard_map/ppermute | solution.py:47
  12.4 12.9 %collective-permute-start.3 = (bf16[6,128,128]{2,1,0:T(8,128)(2,1)S(1)}, bf16[6,128,128]{2,1,0:T(8,128)(2,1)S(1)}, u32[]{:S(2)}, u32[]{:S(2)}) collective-permute-start(bf16[6,128,128]{2,1,0:T(8,128)(2,1)S(1)} %pack_grads.1.refs_0_), channel_id=1, source_target_pairs={{0,1},{1,0},{2,3},{3,2},{4,5},{5,4},{6,7},{7,6},{8,9},{9,8},{10,11... | collective-permute-start | bytes 589832 | tf_op jit(solution)/shard_map/ppermute | solution.py:47
  12.6 1.2 %collective-permute-start.12 = (bf16[2,64,128]{2,1,0:T(8,128)(2,1)S(1)}, bf16[2,64,128]{2,1,0:T(8,128)(2,1)S(1)}, u32[]{:S(2)}, u32[]{:S(2)}) collective-permute-start(bf16[2,64,128]{2,1,0:T(8,128)(2,1)S(1)} %collective-permute-done.8.refs_2_), channel_id=1, source_target_pairs={{0,1},{1,0},{2,3},{3,2},{4,5},{5,4},{6,7},{7,6},{8,9},{9,8},{10,11... | collective-permute-start | bytes 98312 | tf_op jit(solution)/shard_map/ppermute | solution.py:47
  13.9 1.2 %collective-permute-start.13 = (bf16[2,64,128]{2,1,0:T(8,128)(2,1)S(1)}, bf16[2,64,128]{2,1,0:T(8,128)(2,1)S(1)}, u32[]{:S(2)}, u32[]{:S(2)}) collective-permute-start(bf16[2,64,128]{2,1,0:T(8,128)(2,1)S(1)} %collective-permute-done.9.refs_3_), channel_id=1, source_target_pairs={{0,1},{1,0},{2,3},{3,2},{4,5},{5,4},{6,7},{7,6},{8,9},{9,8},{10,11... | collective-permute-start | bytes 98312 | tf_op jit(solution)/shard_map/ppermute | solution.py:47
  15.2 13.0 %copy-start.2 = (f32[384]{0:T(512)S(1)}, f32[384]{0:T(512)}, u32[]{:S(2)}) copy-start(f32[384]{0:T(512)} %param.6) | copy-start | bytes 4612
  15.2 9.4 %collective-permute-start.15 = (bf16[480,128]{1,0:T(8,128)(2,1)S(1)}, bf16[480,128]{1,0:T(8,128)(2,1)S(1)}, u32[]{:S(2)}, u32[]{:S(2)}) collective-permute-start(bf16[480,128]{1,0:T(8,128)(2,1)S(1)} %get-tuple-element.30), channel_id=1, source_target_pairs={{0,16},{1,17},{2,18},{3,19},{4,20},{5,21},{6,22},{7,23},{8,24},{9,... | collective-permute-start | bytes 368648 | tf_op jit(solution)/shard_map/ppermute | solution.py:47
  18.2 16.9 %collective-permute-start.6 = (bf16[6,128,128]{2,1,0:T(8,128)(2,1)S(1)}, bf16[6,128,128]{2,1,0:T(8,128)(2,1)S(1)}, u32[]{:S(2)}, u32[]{:S(2)}) collective-permute-start(bf16[6,128,128]{2,1,0:T(8,128)(2,1)S(1)} %collective-permute-done.2.refs_3_), channel_id=1, source_target_pairs={{0,1},{1,0},{2,3},{3,2},{4,5},{5,4},{6,7},{7,6},{8,9},{9,8},{10,11... | collective-permute-start | bytes 589832 | tf_op jit(solution)/shard_map/ppermute | solution.py:47
  19.1 15.9 %collective-permute-start.5 = (bf16[6,128,128]{2,1,0:T(8,128)(2,1)S(1)}, bf16[6,128,128]{2,1,0:T(8,128)(2,1)S(1)}, u32[]{:S(2)}, u32[]{:S(2)}) collective-permute-start(bf16[6,128,128]{2,1,0:T(8,128)(2,1)S(1)} %collective-permute-done.1.refs_2_), channel_id=1, source_target_pairs={{0,1},{1,0},{2,3},{3,2},{4,5},{5,4},{6,7},{7,6},{8,9},{9,8},{10,11... | collective-permute-start | bytes 589832 | tf_op jit(solution)/shard_map/ppermute | solution.py:47
  19.2 15.9 %collective-permute-start.4 = (bf16[6,128,128]{2,1,0:T(8,128)(2,1)S(1)}, bf16[6,128,128]{2,1,0:T(8,128)(2,1)S(1)}, u32[]{:S(2)}, u32[]{:S(2)}) collective-permute-start(bf16[6,128,128]{2,1,0:T(8,128)(2,1)S(1)} %collective-permute-done.refs_1_), channel_id=1, source_target_pairs={{0,1},{1,0},{2,3},{3,2},{4,5},{5,4},{6,7},{7,6},{8,9},{9,8},{10,11... | collective-permute-start | bytes 589832 | tf_op jit(solution)/shard_map/ppermute | solution.py:47
  24.6 5.3 %collective-permute-start.14 = (bf16[544,128]{1,0:T(8,128)(2,1)S(1)}, bf16[544,128]{1,0:T(8,128)(2,1)S(1)}, u32[]{:S(2)}, u32[]{:S(2)}) collective-permute-start(bf16[544,128]{1,0:T(8,128)(2,1)S(1)} %get-tuple-element.29), channel_id=1, source_target_pairs={{0,8},{1,9},{2,10},{3,11},{4,12},{5,13},{6,14},{7,15},{8,0},{9,1},... | collective-permute-start | bytes 417800 | tf_op jit(solution)/shard_map/ppermute | solution.py:47
  25.3 2.9 %copy-start.3 = (f32[384]{0:T(512)S(1)}, f32[384]{0:T(512)}, u32[]{:S(2)}) copy-start(f32[384]{0:T(512)} %param.7) | copy-start | bytes 4612
  25.3 9.8 %collective-permute-start.16 = (bf16[544,128]{1,0:T(8,128)(2,1)S(1)}, bf16[544,128]{1,0:T(8,128)(2,1)S(1)}, u32[]{:S(2)}, u32[]{:S(2)}) collective-permute-start(bf16[544,128]{1,0:T(8,128)(2,1)S(1)} %get-tuple-element.31), channel_id=1, source_target_pairs={{0,24},{1,25},{2,26},{3,27},{4,28},{5,29},{6,30},{7,31},{8,16},{9,... | collective-permute-start | bytes 417800 | tf_op jit(solution)/shard_map/ppermute | solution.py:47
  42.4 15.2 %collective-permute-start.17 = (bf16[608,128]{1,0:T(8,128)(2,1)S(1)}, bf16[608,128]{1,0:T(8,128)(2,1)S(1)}, u32[]{:S(2)}, u32[]{:S(2)}) collective-permute-start(bf16[608,128]{1,0:T(8,128)(2,1)S(1)} %get-tuple-element.36), channel_id=1, source_target_pairs={{0,8},{1,9},{2,10},{3,11},{4,12},{5,13},{6,14},{7,15},{8,0},{9,1},... | collective-permute-start | bytes 466952 | tf_op jit(solution)/shard_map/ppermute | solution.py:47
  43.2 14.4 %collective-permute-start.19 = (bf16[608,128]{1,0:T(8,128)(2,1)S(1)}, bf16[608,128]{1,0:T(8,128)(2,1)S(1)}, u32[]{:S(2)}, u32[]{:S(2)}) collective-permute-start(bf16[608,128]{1,0:T(8,128)(2,1)S(1)} %get-tuple-element.38), channel_id=1, source_target_pairs={{0,24},{1,25},{2,26},{3,27},{4,28},{5,29},{6,30},{7,31},{8,16},{9,... | collective-permute-start | bytes 466952 | tf_op jit(solution)/shard_map/ppermute | solution.py:47
  45.8 11.8 %collective-permute-start.18 = (bf16[480,128]{1,0:T(8,128)(2,1)S(1)}, bf16[480,128]{1,0:T(8,128)(2,1)S(1)}, u32[]{:S(2)}, u32[]{:S(2)}) collective-permute-start(bf16[480,128]{1,0:T(8,128)(2,1)S(1)} %get-tuple-element.37), channel_id=1, source_target_pairs={{0,16},{1,17},{2,18},{3,19},{4,20},{5,21},{6,22},{7,23},{8,24},{9,... | collective-permute-start | bytes 368648 | tf_op jit(solution)/shard_map/ppermute | solution.py:47
  57.7 4.1 %collective-permute-start.20 = (bf16[2,64,128]{2,1,0:T(8,128)(2,1)S(1)}, bf16[2,64,128]{2,1,0:T(8,128)(2,1)S(1)}, u32[]{:S(2)}, u32[]{:S(2)}) collective-permute-start(bf16[2,64,128]{2,1,0:T(8,128)(2,1)S(1)} %get-tuple-element.40), channel_id=1, source_target_pairs={{0,2},{1,3},{2,0},{3,1},{4,6},{5,7},{6,4},{7,5},{8,10},{9,11},{10,... | collective-permute-start | bytes 98312 | tf_op jit(solution)/shard_map/ppermute | solution.py:47
  59.3 3.9 %collective-permute-start.21 = (bf16[2,64,128]{2,1,0:T(8,128)(2,1)S(1)}, bf16[2,64,128]{2,1,0:T(8,128)(2,1)S(1)}, u32[]{:S(2)}, u32[]{:S(2)}) collective-permute-start(bf16[2,64,128]{2,1,0:T(8,128)(2,1)S(1)} %get-tuple-element.41), channel_id=1, source_target_pairs={{0,4},{1,5},{2,6},{3,7},{4,0},{5,1},{6,2},{7,3},{8,12},{9,13},{10,... | collective-permute-start | bytes 98312 | tf_op jit(solution)/shard_map/ppermute | solution.py:47
  60.8 4.8 %collective-permute-start.22 = (bf16[2,64,128]{2,1,0:T(8,128)(2,1)S(1)}, bf16[2,64,128]{2,1,0:T(8,128)(2,1)S(1)}, u32[]{:S(2)}, u32[]{:S(2)}) collective-permute-start(bf16[2,64,128]{2,1,0:T(8,128)(2,1)S(1)} %get-tuple-element.42), channel_id=1, source_target_pairs={{0,6},{1,7},{2,4},{3,5},{4,2},{5,3},{6,0},{7,1},{8,14},{9,15},{10,... | collective-permute-start | bytes 98312 | tf_op jit(solution)/shard_map/ppermute | solution.py:47
  61.3 5.3 %collective-permute-start.23 = (bf16[2,64,128]{2,1,0:T(8,128)(2,1)S(1)}, bf16[2,64,128]{2,1,0:T(8,128)(2,1)S(1)}, u32[]{:S(2)}, u32[]{:S(2)}) collective-permute-start(bf16[2,64,128]{2,1,0:T(8,128)(2,1)S(1)} %get-tuple-element.39.refs_0_), channel_id=1, source_target_pairs={{0,1},{1,0},{2,3},{3,2},{4,5},{5,4},{6,7},{7,6},{8,9},{9,8},{10,11... | collective-permute-start | bytes 98312 | tf_op jit(solution)/shard_map/ppermute | solution.py:47
  61.8 4.7 %collective-permute-start.24 = (bf16[2,64,128]{2,1,0:T(8,128)(2,1)S(1)}, bf16[2,64,128]{2,1,0:T(8,128)(2,1)S(1)}, u32[]{:S(2)}, u32[]{:S(2)}) collective-permute-start(bf16[2,64,128]{2,1,0:T(8,128)(2,1)S(1)} %collective-permute-done.20.refs_1_), channel_id=1, source_target_pairs={{0,1},{1,0},{2,3},{3,2},{4,5},{5,4},{6,7},{7,6},{8,9},{9,8},{10,11... | collective-permute-start | bytes 98312 | tf_op jit(solution)/shard_map/ppermute | solution.py:47
  63.2 3.3 %collective-permute-start.25 = (bf16[2,64,128]{2,1,0:T(8,128)(2,1)S(1)}, bf16[2,64,128]{2,1,0:T(8,128)(2,1)S(1)}, u32[]{:S(2)}, u32[]{:S(2)}) collective-permute-start(bf16[2,64,128]{2,1,0:T(8,128)(2,1)S(1)} %collective-permute-done.21.refs_2_), channel_id=1, source_target_pairs={{0,1},{1,0},{2,3},{3,2},{4,5},{5,4},{6,7},{7,6},{8,9},{9,8},{10,11... | collective-permute-start | bytes 98312 | tf_op jit(solution)/shard_map/ppermute | solution.py:47
  65.6 1.2 %collective-permute-start.26 = (bf16[2,64,128]{2,1,0:T(8,128)(2,1)S(1)}, bf16[2,64,128]{2,1,0:T(8,128)(2,1)S(1)}, u32[]{:S(2)}, u32[]{:S(2)}) collective-permute-start(bf16[2,64,128]{2,1,0:T(8,128)(2,1)S(1)} %collective-permute-done.22.refs_3_), channel_id=1, source_target_pairs={{0,1},{1,0},{2,3},{3,2},{4,5},{5,4},{6,7},{7,6},{8,9},{9,8},{10,11... | collective-permute-start | bytes 98312 | tf_op jit(solution)/shard_map/ppermute | solution.py:47

commit v2 on v1

v2 whole, which is shorter than its diff:
```python
import jax
import jax.numpy as jnp
from jax import lax
from jax.experimental import pallas as pl
from jax.experimental.pallas import tpu as pltpu
from jax.sharding import PartitionSpec as P

GROUPS = 32
norm_eps = 1e-06


F32 = jnp.float32
BF16 = jnp.bfloat16
SPLIT = 16


class Sizes:
    def __init__(self, acts, weights, cotangent, tiles, blocks):
        self.frames, low_rows, self.cols, self.chans = acts.shape
        self.taps, self.outs = weights.shape[1:]
        self.tiles, self.blocks = tiles, blocks
        self.inner = 1 << (tiles.bit_length() // 2)
        self.outer = tiles // self.inner
        self.pairs = self.inner // 2
        self.per = self.chans // GROUPS
        self.gp = 16
        self.rb = self.outer * self.gp
        self.cells = self.frames * self.cols
        self.wide = 2 * self.cols
        self.grad_frames = self.frames * (2 if blocks > 1 else 1)
        self.first = max(0, 3 - self.frames * blocks)
        self.used = 9 * (3 - self.first)
        self.half = -(-self.used * self.per // 32) * 16
        self.sent = 2 * self.half
        self.wrows = self.sent + self.half
        self.lo = 128
        self.hi = self.outs - self.lo
        self.order = [*range(1, self.outer, 2), *range(0, self.outer, 2)]
        self.grows = 2 * self.grad_frames * self.outs
        self.count = float(low_rows * tiles * self.cols * self.per)
        self.steps = [k for k in range(1, self.outer) if k & (k + 1) == 0]
        if low_rows != 1 or tiles != GROUPS or self.hi != 64 or self.outer > 8:
            raise ValueError("unsupported sizes")


def swap(value, mask):
    count = lax.axis_size("tile")
    return lax.ppermute(value, "tile", [(i, i ^ mask) for i in range(count)])


def place(g):
    me = lax.axis_index("tile")
    return lax.div(me, g.inner), lax.rem(me, g.inner)


def iota(shape, dim):
    return lax.broadcasted_iota(jnp.int32, shape, dim)


def dot(a, b, dims=((1,), (0,))):
    return lax.dot_general(a, b, (dims, ((), ())), preferred_element_type=F32)


def channel_select(g, w, count):
    shape = (count * g.rb, g.chans)
    row = iota(shape, 0)
    block = row >> (g.rb.bit_length() - 1)
    group = (row & (g.rb - 1)) >> 4
    lane = row & (g.gp - 1)
    chan = g.per * (g.inner * group + (w ^ block)) + lane
    return (chan == iota(shape, 1)) & (lane < g.per)


def column_select(g):
    shape = (g.cells, g.frames * 3 * g.wide)
    row, col = iota(shape, 0), iota(shape, 1)
    bits = g.wide.bit_length() - 1
    part = col >> bits
    frame, shift = part, part
    frame = (part >= 3).astype(jnp.int32)
    for f in range(2, g.frames):
        frame = frame + (part >= 3 * f).astype(jnp.int32)
    shift = part - 3 * frame
    low = ((col & (g.wide - 1)) + shift - 1) >> 1
    inside = (low >= 0) & (low < g.cols)
    return (inside & (low + frame * g.cols == row)).astype(BF16)


def split(value, parts):
    out = []
    for _ in range(parts):
        piece = value.astype(BF16)
        out.append(piece)
        value = value - piece.astype(F32)
    return out


def sort_acts_kernel(g, acts_ref, out_ref):
    _, w = place(g)
    pick = channel_select(g, w, g.inner).astype(BF16)
    out_ref[...] = dot(pick, acts_ref[...], ((1,), (1,))).astype(BF16)


def pack_kernel(g, blocks_ref, grads_ref, *out_refs):
    for k, ref in enumerate(out_refs):
        ref[: g.grows] = grads_ref[...]
        ref[g.grows :] = blocks_ref[2 * k * g.rb : 2 * (k + 1) * g.rb]


def pack_rows(g, value):
    hi = jnp.concatenate([value[:, g.lo :], jnp.zeros((g.sent, 64), F32)], axis=1)
    lane = iota((g.half, 128), 1)
    both = jnp.where(lane < 64, hi[: g.half], pltpu.roll(hi[g.half :], 64, 1))
    return jnp.concatenate([value[:, : g.lo], both], axis=0).astype(BF16)


def unpack_rows(g, packed):
    both = packed[g.sent :].astype(F32)
    lane = iota(both.shape, 1)
    first = jnp.where(lane < 64, both, 0.0)
    second = jnp.where(lane < 64, pltpu.roll(both, 64, 1), 0.0)
    hi = jnp.concatenate([first, second], axis=0).astype(BF16)
    return jnp.concatenate([packed[: g.sent], hi], axis=1)


def pack_weights_kernel(g, weights_ref, out_ref):
    total = jnp.zeros((g.sent, g.outs), F32)
    row, tap = iota((g.sent, g.taps), 0), iota((g.sent, g.taps), 1) - 9 * g.first
    for i in range(g.per):
        pick = (row == tap * g.per + i) & (tap >= 0)
        total = total + dot(pick.astype(BF16), weights_ref[i])
    out_ref[...] = pack_rows(g, total)


def totals(g, first, second):
    pad = jnp.zeros((8 - g.outer, g.cells), F32)
    out = []
    for value in (first, second):
        out += [jnp.sum(value.reshape(g.outer, g.gp, g.cells), axis=1)]
        if g.outer < 8:
            out += [pad]
    return jnp.concatenate(out, axis=0)


def send_stats(g, refs, stats, z, rows_ref, parts):
    pieces = split(stats, 3)
    last = rows_ref.shape[0] - 1
    for k, ref in enumerate(refs, 1):
        for i, piece in enumerate(pieces):
            ref[i * SPLIT : (i + 1) * SPLIT] = piece
        if k in g.steps:
            edge = rows_ref[jnp.where((z ^ k) == z + 1, last, 0)]
            for i, piece in enumerate(split(edge, parts) if parts > 1 else [edge]):
                ref[3 * SPLIT + i * g.rb : 3 * SPLIT + (i + 1) * g.rb] = piece


def stats_kernel(g, *refs):
    direct, crossed, refs = refs[: g.pairs], refs[g.pairs : 2 * g.pairs], refs[2 * g.pairs :]
    rows_ref, stats_ref, *sends = refs
    z, w = place(g)
    first = jnp.zeros((g.rb, g.cells), F32)
    second = jnp.zeros((g.rb, g.cells), F32)
    for k in range(g.pairs):
        for j, ref in enumerate((direct[k], crossed[k])):
            block = ref[g.grows + j * g.rb : g.grows + (j + 1) * g.rb]
            rows_ref[w ^ (2 * k + j)] = block
            wide = block.astype(F32)
            first = first + wide
            second = second + wide * wide
    stats = totals(g, first, second)
    stats_ref[...] = stats
    send_stats(g, sends, stats, z, rows_ref, 1)


def add_stats(own, received):
    for ref in received:
        for i in range(3):
            own = own + ref[i * SPLIT : (i + 1) * SPLIT].astype(F32)
    return own


def spread(g, stats):
    lane = iota((SPLIT, g.cells), 1)
    whole = jnp.zeros((SPLIT, g.cells), F32)
    for t in range(g.frames):
        mine = (lane >= t * g.cols) & (lane < (t + 1) * g.cols)
        part = jnp.sum(jnp.where(mine, stats, 0.0), axis=1, keepdims=True)
        whole = jnp.where(mine, part, whole)
    return tuple(
        jnp.concatenate(
            [
                jnp.broadcast_to(whole[s + q : s + q + 1], (g.gp, g.cells))
                for q in range(g.outer)
            ],
            axis=0,
        )
        for s in (0, 8)
    )


def prepare_weights_kernel(g, *refs):
    *packed, out_ref = refs
    z, _ = place(g)
    shape = (g.used * g.gp, g.sent)
    row, col = iota(shape, 0), iota(shape, 1)
    tap, lane = row >> 4, row & (g.gp - 1)
    pick = ((col == tap * g.per + lane) & (lane < g.per)).astype(BF16)
    blocks = [(ref, at) for ref in packed for at in range(0, ref.shape[0], g.wrows)]
    for k, (ref, at) in enumerate(blocks):
        value = dot(pick, unpack_rows(g, ref[at : at + g.wrows])).astype(BF16)
        out_ref[:, z ^ k] = value.reshape(g.used, g.gp, 256)


def meetings(g, later):
    pairs = [(a, later + a - 2) for a in range(g.first, 3)]
    return [(a, t) for a, t in pairs if 0 <= t < g.frames]


def fine_rows(g, ref, later):
    at = 2 * later * g.outs
    return jnp.concatenate([ref[at : at + g.outs], ref[at + g.outs : at + 2 * g.outs]], axis=1)


def lanes_of(g, t, e):
    return slice((3 * t + e) * g.wide, (3 * t + e + 1) * g.wide)


def field_kernel(g, *refs):
    direct, crossed, refs = refs[: g.pairs], refs[g.pairs : 2 * g.pairs], refs[2 * g.pairs :]
    weights_ref, field = refs
    _, w = place(g)
    rb, wide = g.rb, g.wide
    field[...] = jnp.zeros_like(field)
    for k in range(g.pairs):
        for j, ref in enumerate((direct[k], crossed[k])):
            row = w ^ (2 * k + j)
            for later in range(g.grad_frames):
                pairs = meetings(g, later)
                if not pairs:
                    continue
                low, high = pairs[0][0] - g.first, pairs[-1][0] - g.first + 1
                taps = weights_ref[9 * low : 9 * high].reshape(9 * (high - low) * rb, 256)
                every = dot(taps[:, : g.outs], fine_rows(g, ref, later))
                for n, (_, t) in enumerate(pairs):
                    back = every[9 * n * rb : 9 * (n + 1) * rb]
                    part = lambda b, e, fine: back[
                        (3 * b + e) * rb : (3 * b + e + 1) * rb, fine * wide : (fine + 1) * wide
                    ]
                    for e in range(3):
                        lanes = lanes_of(g, t, e)
                        field[row, :, lanes] += part(0, e, 0)
                        field[row + 1, :, lanes] += (part(1, e, 0) + part(2, e, 0)) + (
                            part(0, e, 1) + part(1, e, 1)
                        )
                        field[row + 2, :, lanes] += part(2, e, 1)


def norm_grad_kernel(g, *refs):
    rows_ref, stats_ref, gamma_ref, beta_ref, field_ref, *refs = refs
    received, refs = refs[: g.outer - 1], refs[g.outer - 1 :]
    normed_ref, hidden_ref, inv_ref, sums_ref, grad_ref, *sends, slope_ref, hidden_scratch = refs
    z, w = place(g)
    rb = g.rb
    total, total_sq = spread(g, add_stats(stats_ref[...], received))
    mean = total / g.count
    inv = lax.rsqrt(total_sq / g.count - mean * mean + norm_eps)
    inv_ref[...] = inv
    pick = channel_select(g, w, 1)
    gamma = jnp.sum(jnp.where(pick, gamma_ref[...].reshape(1, g.chans), 0.0), axis=1, keepdims=True)
    beta = jnp.sum(jnp.where(pick, beta_ref[...].reshape(1, g.chans), 0.0), axis=1, keepdims=True)

    def activate(place_at, block, present):
        normed = (block.astype(F32) - mean) * inv
        shifted = normed * gamma + beta
        gate = jax.nn.sigmoid(shifted)
        normed_ref[place_at] = normed
        hidden = (shifted * gate * present).astype(BF16).reshape(g.outer, g.gp, g.cells)
        hidden_scratch[...] = hidden
        for at, k in enumerate(g.order):
            hidden_ref[at, place_at] = hidden_scratch[z ^ k]
        slope_ref[place_at] = gate * (1.0 + shifted * (1.0 - gate)) * gamma * present

    for place_at, step in ((0, -1), (g.inner + 1, 1)):
        block = jnp.zeros((rb, g.cells), BF16)
        for k in g.steps:
            edge = received[k - 1][3 * SPLIT : 3 * SPLIT + rb]
            block = jnp.where((z ^ k) == z + step, edge, block)
        inside = (z + step >= 0) & (z + step < g.outer)
        activate(place_at, block, jnp.where(inside, 1.0, 0.0))

    @pl.loop(0, g.inner)
    def _(i):
        activate(i + 1, rows_ref[i], 1.0)

    count = g.inner + 2
    select = column_select(g)
    flat = field_ref[...].reshape(count * rb, g.frames * 3 * g.wide)
    pieces = split(flat, 2)
    act_grad = dot(pieces[0], select, ((1,), (1,))) + dot(pieces[1], select, ((1,), (1,)))
    grad = act_grad.reshape(count, rb, g.cells) * slope_ref[...]
    grad_ref[...] = grad
    sums = totals(g, jnp.sum(grad, axis=0), jnp.sum(grad * normed_ref[...], axis=0))
    sums_ref[...] = sums
    send_stats(g, sends, sums, z, grad_ref, 2)


def kernel_terms(g, first, direct, crossed, hidden_ref, acc, ups):
    _, w = place(g)
    part = acc.shape[0]
    flat = hidden_ref[first : first + part].reshape(-1, g.cells)
    ups[...] = dot(flat, column_select(g)).astype(BF16).reshape(ups.shape)
    started = set()
    for later in range(g.grad_frames):
        for a, t in meetings(g, later):
            left, right = [], []
            for k in range(g.pairs):
                for j, ref in enumerate((direct[k], crossed[k])):
                    row = w ^ (2 * k + j)
                    pieces = []
                    for group in range(part):
                        for upper, lower in ((0, 1), (1, 1), (1, 2)):
                            for e in range(3):
                                lanes = lanes_of(g, t, e)
                                sides = [ups[group, row + at, :, lanes] for at in (upper, lower)]
                                pieces.append(jnp.concatenate(sides, axis=1))
                    left.append(jnp.concatenate(pieces, axis=0))
                    right.append(fine_rows(g, ref, later))
            terms = dot(
                jnp.concatenate(left, axis=1), jnp.concatenate(right, axis=1), ((1,), (1,))
            ).reshape(part, 9, g.gp, g.outs)
            taps = slice(9 * (a - g.first), 9 * (a - g.first + 1))
            if a in started:
                acc[:, taps] += terms
            else:
                acc[:, taps] = terms
                started.add(a)


def sent_order(g):
    shape = (g.sent, g.used * g.gp)
    row, col = iota(shape, 0), iota(shape, 1)
    tap, lane = col >> 4, col & (g.gp - 1)
    return ((row == tap * g.per + lane) & (lane < g.per)).astype(BF16)


def sent_terms_kernel(g, *refs):
    direct, crossed, refs = refs[: g.pairs], refs[g.pairs : 2 * g.pairs], refs[2 * g.pairs :]
    hidden_ref, send_ref, acc, ups = refs
    kernel_terms(g, 0, direct, crossed, hidden_ref, acc, ups)
    pick = sent_order(g)
    for i in range(g.outer // 2):
        terms = acc[i].reshape(g.used * g.gp, g.outs).astype(BF16)
        send_ref[i * g.wrows : (i + 1) * g.wrows] = pack_rows(g, dot(pick, terms))


def kept_terms_kernel(g, *refs):
    direct, crossed, refs = refs[: g.pairs], refs[g.pairs : 2 * g.pairs], refs[2 * g.pairs :]
    hidden_ref, own_ref, *kept, acc, ups = refs
    kernel_terms(g, g.outer // 2, direct, crossed, hidden_ref, acc, ups)
    own_ref[...] = acc[0].reshape(g.used * g.gp, g.outs)
    pick = sent_order(g)
    for i in range(1, g.outer // 2):
        terms = acc[i].reshape(g.used * g.gp, g.outs)
        kept[0][i - 1] = sum(dot(pick, piece) for piece in split(terms, 2))


def halve_kernel(g, bit, keep_ref, received_ref, *refs):
    send_ref, *kept = refs
    for i in range(keep_ref.shape[0]):
        block = received_ref[(i + 1) * g.wrows : (i + 2) * g.wrows]
        total = keep_ref[i] + unpack_rows(g, block).astype(F32)[:, : g.outs]
        if i % 2:
            kept[0][i // 2] = total
        else:
            send_ref[i // 2 * g.wrows : (i // 2 + 1) * g.wrows] = pack_rows(g, total)


def finish_kernel(g, *refs):
    sums_ref, grad_ref, normed_ref, inv_ref, *refs = refs
    received, sends = refs[: g.outer - 1], refs[g.outer - 1 :]
    z, w = place(g)
    first, second = spread(g, add_stats(sums_ref[...], received))
    first, second = first / g.count, second / g.count
    inv = inv_ref[...]
    edges = []
    for step in (-1, 1):
        edge = jnp.zeros((g.rb, g.cells), F32)
        for k in g.steps:
            ref, at = received[k - 1], 3 * SPLIT
            value = ref[at : at + g.rb].astype(F32) + ref[at + g.rb :].astype(F32)
            edge = jnp.where((z ^ k) == z + step, value, edge)
        edges.append(edge)
    for k, ref in enumerate(sends):
        for j in range(2):
            row = w ^ (2 * k + j)
            grad = grad_ref[row + 1]
            grad = grad + jnp.where(row == 0, edges[0], 0.0)
            grad = grad + jnp.where(row == g.inner - 1, edges[1], 0.0)
            ref[j] = (inv * (grad - first - normed_ref[row + 1] * second)).astype(BF16)


def unpack_kernel(g, own_ref, *refs):
    steps = g.outer.bit_length() - 1
    received, refs = refs[:steps], refs[steps:]
    direct, (crossed, acts_ref, out_ref, low, high) = refs[: g.pairs], refs[g.pairs :]
    _, w = place(g)
    pick = channel_select(g, w, g.inner).astype(BF16)
    blocks = []
    for k in range(g.pairs):
        blocks += [direct[k][0], crossed[k]]
    d_acts = dot(jnp.concatenate(blocks, axis=0), pick, ((0,), (0,)))
    acts_ref[...] = d_acts.astype(BF16).reshape(acts_ref.shape)

    step = 32
    shape = (g.per * step, g.sent)
    row, col = iota(shape, 0), iota(shape, 1)
    tap, lane = row & (step - 1), row >> 5
    pick = ((col == tap * g.per + lane) & (tap < g.used)).astype(BF16)
    total = jnp.zeros((g.per * step, 256), F32)
    for ref in received:
        total = total + dot(pick, unpack_rows(g, ref[: g.wrows]))
    low[...] = own_ref[:, : g.lo]
    high[:, : g.hi] = own_ref[:, g.lo :]
    for i in range(g.per):
        at = pl.ds(i, g.used, stride=g.gp)
        there = total[i * step : i * step + g.used]
        if g.first:
            out_ref[i, : 9 * g.first, :] = jnp.zeros((9 * g.first, g.outs), F32)
        out_ref[i, 9 * g.first :, : g.lo] = low[at, :] + there[:, : g.lo]
        out_ref[i, 9 * g.first :, g.lo :] = high[at, :][:, : g.hi] + there[:, g.lo : g.outs]


def call(g, kernel, name, outs, args, scratch=(), flops=0, after=()):
    shapes = [jax.ShapeDtypeStruct(shape, kind) for shape, kind in outs]
    whole = pl.BlockSpec(memory_space=pltpu.VMEM)
    moved = sum(a.size * a.dtype.itemsize for a in list(args) + shapes)
    count = len(args)
    rest = count + len(after)
    return pl.pallas_call(
        lambda *refs: kernel(g, *refs[:count], *refs[rest:]),
        out_shape=shapes,
        in_specs=[whole] * count + [pl.BlockSpec(memory_space=pl.ANY)] * len(after),
        out_specs=[whole] * len(shapes),
        scratch_shapes=list(scratch),
        compiler_params=pltpu.CompilerParams(vmem_limit_bytes=48 * 1024 * 1024),
        cost_estimate=pl.CostEstimate(flops=flops, bytes_accessed=moved, transcendentals=0),
        name=name,
    )(*args, *after)


def copy_kernel(g, in_ref, out_ref):
    out_ref[...] = in_ref[...]


def join_kernel(g, *refs):
    *parts, out_ref = refs
    at = 0
    for ref in parts:
        out_ref[at : at + ref.shape[0]] = ref[...]
        at += ref.shape[0]


def cross_kernel(g, *refs):
    *blocks, out_ref = refs
    for k, ref in enumerate(blocks):
        out_ref[k] = ref[1]


def cross(g, name, direct):
    shape = (g.pairs, g.rb, g.cells)
    (out,) = call(g, cross_kernel, name, [(shape, BF16)], direct)
    return swap(out, 1)


def shards(acts, gamma, beta, weights, cotangent):
    g = Sizes(acts, weights, cotangent, lax.axis_size("tile"), lax.axis_size("block"))
    if g.blocks > 1:
        pairs = [(i + 1, i) for i in range(g.blocks - 1)]
        following = lax.ppermute(cotangent, "block", pairs)
        cotangent = jnp.concatenate([cotangent, following], 0)
    count = g.inner + 2
    block = ((2, g.rb, g.cells), BF16)
    rows_shape = ((count, g.rb, g.cells), F32)
    stats_shape = ((SPLIT, g.cells), F32)
    packed_shape = ((g.wrows, 128), BF16)
    wide_shape = (count, g.rb, g.frames * 3 * g.wide)
    over_z = lambda values: [swap(v, g.inner * k) for k, v in enumerate(values, 1)]
    sums_shapes = lambda parts: [
        ((3 * SPLIT + (parts * g.rb if k in g.steps else 0), 128), BF16)
        for k in range(1, g.outer)
    ]

    packed = list(
        call(g, pack_weights_kernel, "pack_weights", [packed_shape], [weights], flops=6 * 10**9)
    )
    for bit in range(g.outer.bit_length() - 1):
        whole = packed[0]
        if bit:
            shape = ((g.wrows << bit, 128), BF16)
            (whole,) = call(g, join_kernel, "join_kernel_rows", [shape], packed)
        packed.append(swap(whole, g.inner << bit))
    (blocks,) = call(
        g,
        sort_acts_kernel,
        "sort_acts",
        [((g.inner * g.rb, g.cells), BF16)],
        [acts.reshape(g.cells, g.chans)],
        flops=6 * 10**9,
    )
    sends = call(
        g,
        pack_kernel,
        "pack",
        [((g.grows + 2 * g.rb, g.cells), BF16)] * g.pairs,
        [blocks, jnp.swapaxes(cotangent, 2, 3).reshape(g.grows, g.wide)],
    )
    direct = [sends[0]] + [swap(sends[k], 2 * k) for k in range(1, g.pairs)]
    (last,) = call(
        g, copy_kernel, "pass_on", [(sends[0].shape, BF16)], direct[-1:], after=packed[1:]
    )
    arrived = direct + [swap(v, 1) for v in direct[:-1] + [last]]
    rows, stats, *sends = call(
        g,
        stats_kernel,
        "stats",
        [((g.inner, g.rb, g.cells), BF16), stats_shape] + sums_shapes(1),
        arrived,
    )
    received = over_z(sends)
    kernel_shape = ((g.used, g.outer, g.gp, 256), BF16)
    (rows_of_kernel,) = call(g, prepare_weights_kernel, "kernel_rows", [kernel_shape], packed)
    flops = 2 * 2 * g.inner * 9 * g.rb * 256 * 256 * g.grad_frames
    (field,) = call(
        g, field_kernel, "field_grad", [(wide_shape, F32)], arrived + [rows_of_kernel], flops=flops
    )
    hidden_shape = ((g.outer, count, g.gp, g.cells), BF16)
    normed, hidden, inv, sums, grad, *sends = call(
        g,
        norm_grad_kernel,
        "norm_grad",
        [rows_shape, hidden_shape, ((g.rb, g.cells), F32), stats_shape, rows_shape]
        + sums_shapes(2),
        [rows, stats, gamma, beta, field] + received,
        [pltpu.VMEM(*rows_shape), pltpu.VMEM((g.outer, g.gp, g.cells), BF16)],
    )
    received = over_z(sends)
    half = g.outer // 2
    kept_shape = lambda count: [((count, g.sent, g.outs), F32)] if count else []
    scratch = [
        pltpu.VMEM((half, g.used, g.gp, g.outs), F32),
        pltpu.VMEM((half, count, g.gp, wide_shape[-1]), BF16),
    ]
    (send,) = call(
        g,
        sent_terms_kernel,
        "sent_terms",
        [((half * g.wrows, 128), BF16)],
        arrived + [hidden],
        scratch,
        flops // 2,
    )
    (send,) = call(g, copy_kernel, "pass_terms", [(send.shape, BF16)], [send], after=received)
    terms = [swap(send, g.inner)]
    sends = call(
        g,
        finish_kernel,
        "finish",
        [block] * g.pairs,
        [sums, grad, normed, inv] + received,
        after=[send],
    )
    direct = [sends[0]] + [swap(sends[k], 2 * k) for k in range(1, g.pairs)]
    own, *kept = call(
        g,
        kept_terms_kernel,
        "kept_terms",
        [((g.used * g.gp, g.outs), F32)] + kept_shape(half - 1),
        arrived + [hidden],
        scratch,
        flops // 2,
        after=sends[:1],
    )
    bit = 1
    while kept:
        half //= 2
        send, *kept = call(
            g,
            lambda g, *refs, bit=bit: halve_kernel(g, bit, *refs),
            "halve",
            [((half * g.wrows, 128), BF16)] + kept_shape(half - 1),
            [kept[0], terms[-1]],
            after=direct[1:2],
        )
        terms.append(swap(send, g.inner << bit))
        bit += 1
    crossed = cross(g, "cross_grads", direct)
    d_acts, d_weights = call(
        g,
        unpack_kernel,
        "unpack",
        [(acts.shape, BF16), (weights.shape, F32)],
        [own] + terms + direct + [crossed],
        [pltpu.VMEM((g.used * g.gp, 128), F32)] * 2,
    )
    if g.blocks > 1:
        d_weights = lax.psum(d_weights, "block")
    return (d_acts, d_weights)


def solution(mesh):
    placed = (
        P("block", "tile", None, None),
        P(),
        P(),
        P("tile", None, None),
        P("block", "tile", None, None),
    )
    return jax.shard_map(
        shards,
        mesh=mesh,
        in_specs=placed,
        out_specs=(P("block", "tile", None, None), P("tile", None, None)),
        check_vma=False,
    )
```

time: 68 us -> 53.4 us (0.79)
  waiting for transfers between devices: 31.4 us -> 14.5 us
  starting transfers between devices: 23.3 us -> 26.1 us
    ppermute x27 -> x21, waiting for transfers between devices: 31.4 us -> 14.5 us  [swap(): return lax.ppermute(value, 'tile', [(i, i ^ mask) for i in range(count)])]
    ppermute x27 -> x21, starting transfers between devices: 23.3 us -> 26.1 us  [swap(): return lax.ppermute(value, 'tile', [(i, i ^ mask) for i in range(count)])]
    unnamed x9 -> x10, local copies, waits for them, and re-layouts: 1.96 us -> 1.56 us
    pallas_call x8 -> x16, Pallas kernels: 10.4 us -> 10.2 us  [call(): pl.pallas_call(lambda *refs: kernel(g, *refs[:count], *refs[rest:]), out_...]
  transfers between devices with their start and end apart: 27 -> 21, of which waited for: 14 -> 8; matrix products, arithmetic and copies ran while one was open for 2% -> 0% of each run, Pallas kernels for 3% -> 14%
where the time goes in v2:
time: 53.4 us; the launch traced here: 53.2 us
  starting transfers between devices  26.1 us (49%)
  waiting for transfers between devices  14.5 us (27%)
  Pallas kernels  10.2 us (19%)
  local copies, waits for them, and re-layouts  1.56 us (3%)
  between operations  0.82 us (2%)
    ppermute x21, starting transfers between devices, swap(): return lax.ppermute(value, 'tile', [(i, i ^ mask) for i in range(count)])  26.1 us
    ppermute x21, waiting for transfers between devices, swap(): return lax.ppermute(value, 'tile', [(i, i ^ mask) for i in range(count)])  14.5 us
    pallas_call x16, Pallas kernels, call(): pl.pallas_call(lambda *refs: kernel(g, *refs[:count], *refs[rest:]), out_...  10.2 us
    unnamed x10, local copies, waits for them, and re-layouts  1.56 us
  transfers between devices with their start and end apart: 21, of which 8 were waited for; matrix products, arithmetic and copies ran while one was open for 0% of the time, Pallas kernels for 14%

profile of v2, /device:TPU:0, one launch (start us, length us, event | category | flops | bytes accessed | tf_op | source)
XLA Modules:
  0.0 53.2 jit_solution(6019249585763342726)
XLA Ops:
  0.6 0.9 %copy-done.3 = bf16[12,27,192]{2,1,0:T(8,128)(2,1)S(1)} copy-done((bf16[12,27,192]{2,1,0:T(8,128)(2,1)S(1)}, bf16[12,27,192]{2,1,0:T(8,128)(2,1)}, u32[]{:S(2)}) %copy-start.3) | copy-done | bytes 124440
  1.6 0.6 %pack_weights.1.refs_0_ = bf16[336,128]{1,0:T(8,128)(2,1)S(1)} custom-call(bf16[12,27,192]{2,1,0:T(8,128)(2,1)S(1)} %copy-done.3), custom_call_target="tpu_custom_call" | custom-call | flops 6000000000 | bytes 210432 | tf_op jit(solution)/shard_map/pack_weights/pallas_call | solution.py:439
  2.1 3.1 %collective-permute-start.6 = (bf16[336,128]{1,0:T(8,128)(2,1)S(1)}, bf16[336,128]{1,0:T(8,128)(2,1)S(1)}, u32[]{:S(2)}, u32[]{:S(2)}) collective-permute-start(bf16[336,128]{1,0:T(8,128)(2,1)S(1)} %pack_weights.1.refs_0_), channel_id=1, source_target_pairs={{0,8},{1,9},{2,10},{3,11},{4,12},{5,13},{6,14},{7,15},{8,0},{9,1},... | collective-permute-start | bytes 258056 | tf_op jit(solution)/shard_map/ppermute | solution.py:48
  5.5 0.6 %copy-done = bf16[2,2,128,192]{2,3,1,0:T(8,128)(2,1)S(1)} copy-done((bf16[2,2,128,192]{2,3,1,0:T(8,128)(2,1)S(1)}, bf16[2,2,128,192]{2,3,1,0:T(8,128)(2,1)}, u32[]{:S(2)}) %copy-start) | copy-done | bytes 196632
  6.3 1.5 %collective-permute-start = (bf16[896,128]{1,0:T(8,128)(2,1)S(1)}, bf16[896,128]{1,0:T(8,128)(2,1)S(1)}, u32[]{:S(2)}, u32[]{:S(2)}) collective-permute-start(bf16[896,128]{1,0:T(8,128)(2,1)S(1)} %get-tuple-element.26), channel_id=1, source_target_pairs={{0,2},{1,3},{2,0},{3,1},{4,6},{5,7},{6,4},{7,5},{8,10},{9,11},{10,... | collective-permute-start | bytes 688136 | tf_op jit(solution)/shard_map/ppermute | solution.py:48
  7.8 1.5 %collective-permute-start.1 = (bf16[896,128]{1,0:T(8,128)(2,1)S(1)}, bf16[896,128]{1,0:T(8,128)(2,1)S(1)}, u32[]{:S(2)}, u32[]{:S(2)}) collective-permute-start(bf16[896,128]{1,0:T(8,128)(2,1)S(1)} %get-tuple-element.27), channel_id=1, source_target_pairs={{0,4},{1,5},{2,6},{3,7},{4,0},{5,1},{6,2},{7,3},{8,12},{9,13},{10,... | collective-permute-start | bytes 688136 | tf_op jit(solution)/shard_map/ppermute | solution.py:48
  9.3 0.5 collective-permute-start.2
  9.8 2.7 %collective-permute-start.7 = (bf16[672,128]{1,0:T(8,128)(2,1)S(1)}, bf16[672,128]{1,0:T(8,128)(2,1)S(1)}, u32[]{:S(2)}, u32[]{:S(2)}) collective-permute-start(bf16[672,128]{1,0:T(8,128)(2,1)S(1)} %join_kernel_rows.1), channel_id=1, source_target_pairs={{0,16},{1,17},{2,18},{3,19},{4,20},{5,21},{6,22},{7,23},{8,24},{9,... | collective-permute-start | bytes 516104 | tf_op jit(solution)/shard_map/ppermute | solution.py:48
  12.5 2.4 %collective-permute-done.refs_1_ = bf16[896,128]{1,0:T(8,128)(2,1)S(1)} collective-permute-done((bf16[896,128]{1,0:T(8,128)(2,1)S(1)}, bf16[896,128]{1,0:T(8,128)(2,1)S(1)}, u32[]{:S(2)}, u32[]{:S(2)}) %collective-permute-start) | collective-permute-done | bytes 229408 | tf_op jit(solution)/shard_map/ppermute | solution.py:48
  14.9 4.7 %collective-permute-done.1.refs_2_ = bf16[896,128]{1,0:T(8,128)(2,1)S(1)} collective-permute-done((bf16[896,128]{1,0:T(8,128)(2,1)S(1)}, bf16[896,128]{1,0:T(8,128)(2,1)S(1)}, u32[]{:S(2)}, u32[]{:S(2)}) %collective-permute-start.1) | collective-permute-done | bytes 229408 | tf_op jit(solution)/shard_map/ppermute | solution.py:48
  19.5 0.6 %collective-permute-start.8 = (bf16[896,128]{1,0:T(8,128)(2,1)S(1)}, bf16[896,128]{1,0:T(8,128)(2,1)S(1)}, u32[]{:S(2)}, u32[]{:S(2)}) collective-permute-start(bf16[896,128]{1,0:T(8,128)(2,1)S(1)} %pass_on.1), channel_id=1, source_target_pairs={{0,1},{1,0},{2,3},{3,2},{4,5},{5,4},{6,7},{7,6},{8,9},{9,8},{10,11... | collective-permute-start | bytes 688136 | tf_op jit(solution)/shard_map/ppermute | solution.py:48
  20.1 0.4 kernel_rows.1.refs_8_
  20.5 0.5 collective-permute-done.5.refs_6_
  21.0 0.3 collective-permute-done.8.refs_7_
  21.4 2.7 %collective-permute-start.10 = (bf16[48,128]{1,0:T(8,128)(2,1)S(1)}, bf16[48,128]{1,0:T(8,128)(2,1)S(1)}, u32[]{:S(2)}, u32[]{:S(2)}) collective-permute-start(bf16[48,128]{1,0:T(8,128)(2,1)S(1)} %get-tuple-element.32), channel_id=1, source_target_pairs={{0,16},{1,17},{2,18},{3,19},{4,20},{5,21},{6,22},{7,23},{8,24},{9,... | collective-permute-start | bytes 36872 | tf_op jit(solution)/shard_map/ppermute | solution.py:48
  24.0 0.5 collective-permute-start.9
  24.6 1.3 %collective-permute-start.11 = (bf16[112,128]{1,0:T(8,128)(2,1)S(1)}, bf16[112,128]{1,0:T(8,128)(2,1)S(1)}, u32[]{:S(2)}, u32[]{:S(2)}) collective-permute-start(bf16[112,128]{1,0:T(8,128)(2,1)S(1)} %get-tuple-element.33), channel_id=1, source_target_pairs={{0,24},{1,25},{2,26},{3,27},{4,28},{5,29},{6,30},{7,31},{8,16},{9,... | collective-permute-start | bytes 86024 | tf_op jit(solution)/shard_map/ppermute | solution.py:48
  25.8 2.3 %field_grad.1.refs_4_ = f32[10,64,768]{2,1,0:T(8,128)S(1)} custom-call(bf16[896,128]{1,0:T(8,128)(2,1)S(1)} %get-tuple-element.25.refs_0_, bf16[896,128]{1,0:T(8,128)(2,1)S(1)} %collective-permute-done.refs_1_, bf16[896,128]{1,0:T(8,128)(2,1)S(1)} %collective-permute-done.1.refs_2_, bf16[896,128]{1,0:T(8,128)(2,1)S(1)} %collective-permute-done.2.refs_0_.refs_3_, ...), custom_call_target="tpu_custom_call" | custom-call | flops 2415919104 | bytes 4390912 | tf_op jit(solution)/shard_map/field_grad/pallas_call | solution.py:439
  28.2 2.1 %collective-permute-done.11.refs_7_ = bf16[112,128]{1,0:T(8,128)(2,1)S(1)} collective-permute-done((bf16[112,128]{1,0:T(8,128)(2,1)S(1)}, bf16[112,128]{1,0:T(8,128)(2,1)S(1)}, u32[]{:S(2)}, u32[]{:S(2)}) %collective-permute-start.11) | collective-permute-done | bytes 28704 | tf_op jit(solution)/shard_map/ppermute | solution.py:48
  30.2 1.1 %norm_grad.1 = (f32[10,64,128]{2,1,0:T(8,128)S(1)}, bf16[4,10,16,128]{3,2,1,0:T(8,128)(2,1)S(1)}, f32[64,128]{1,0:T(8,128)S(1)}, f32[16,128]{1,0:T(8,128)S(1)}, ...) custom-call(bf16[8,64,128]{2,1,0:T(8,128)(2,1)S(1)} %get-tuple-eleme, ...), custom_call_target="tpu_custom_call" | custom-call | bytes 3140608 | tf_op jit(solution)/shard_map/norm_grad/pallas_call | solution.py:439
  31.4 1.8 %collective-permute-start.12 = (bf16[176,128]{1,0:T(8,128)(2,1)S(1)}, bf16[176,128]{1,0:T(8,128)(2,1)S(1)}, u32[]{:S(2)}, u32[]{:S(2)}) collective-permute-start(bf16[176,128]{1,0:T(8,128)(2,1)S(1)} %get-tuple-element.39), channel_id=1, source_target_pairs={{0,8},{1,9},{2,10},{3,11},{4,12},{5,13},{6,14},{7,15},{8,0},{9,1},... | collective-permute-start | bytes 135176 | tf_op jit(solution)/shard_map/ppermute | solution.py:48
  33.2 2.6 %collective-permute-start.14 = (bf16[176,128]{1,0:T(8,128)(2,1)S(1)}, bf16[176,128]{1,0:T(8,128)(2,1)S(1)}, u32[]{:S(2)}, u32[]{:S(2)}) collective-permute-start(bf16[176,128]{1,0:T(8,128)(2,1)S(1)} %get-tuple-element.41), channel_id=1, source_target_pairs={{0,24},{1,25},{2,26},{3,27},{4,28},{5,29},{6,30},{7,31},{8,16},{9,... | collective-permute-start | bytes 135176 | tf_op jit(solution)/shard_map/ppermute | solution.py:48
  35.8 1.9 %sent_terms.1.refs_0_ = bf16[672,128]{1,0:T(8,128)(2,1)S(1)} custom-call(bf16[896,128]{1,0:T(8,128)(2,1)S(1)} %get-tuple-element.25.refs_0_, bf16[896,128]{1,0:T(8,128)(2,1)S(1)} %collective-permute-done.refs_1_, bf16[896,128]{1,0:T(8,128)(2,1)S(1)} %collective-permute-done.1.refs_2_, bf16[896,128]{1,0:T(8,128)(2,1)S(1)} %collective-permute-done.2.refs_0_.refs_3_, ...), custom_call_target="tpu_custom_call" | custom-call | flops 1207959552 | bytes 2170880 | tf_op jit(solution)/shard_map/sent_terms/pallas_call | solution.py:439
  37.7 1.3 %collective-permute-done.14.refs_3_.refs_6_ = bf16[176,128]{1,0:T(8,128)(2,1)S(1)} collective-permute-done((bf16[176,128]{1,0:T(8,128)(2,1)S(1)}, bf16[176,128]{1,0:T(8,128)(2,1)S(1)}, u32[]{:S(2)}, u32[]{:S(2)}) %collective-permute-start.14) | collective-permute-done | bytes 45088 | tf_op jit(solution)/shard_map/ppermute | solution.py:48
  39.3 1.3 %collective-permute-start.16 = (bf16[2,64,128]{2,1,0:T(8,128)(2,1)S(1)}, bf16[2,64,128]{2,1,0:T(8,128)(2,1)S(1)}, u32[]{:S(2)}, u32[]{:S(2)}) collective-permute-start(bf16[2,64,128]{2,1,0:T(8,128)(2,1)S(1)} %get-tuple-element.45), channel_id=1, source_target_pairs={{0,2},{1,3},{2,0},{3,1},{4,6},{5,7},{6,4},{7,5},{8,10},{9,11},{10,... | collective-permute-start | bytes 98312 | tf_op jit(solution)/shard_map/ppermute | solution.py:48
  40.6 1.5 %collective-permute-start.18 = (bf16[2,64,128]{2,1,0:T(8,128)(2,1)S(1)}, bf16[2,64,128]{2,1,0:T(8,128)(2,1)S(1)}, u32[]{:S(2)}, u32[]{:S(2)}) collective-permute-start(bf16[2,64,128]{2,1,0:T(8,128)(2,1)S(1)} %get-tuple-element.46), channel_id=1, source_target_pairs={{0,4},{1,5},{2,6},{3,7},{4,0},{5,1},{6,2},{7,3},{8,12},{9,13},{10,... | collective-permute-start | bytes 98312 | tf_op jit(solution)/shard_map/ppermute | solution.py:48
  42.1 0.8 %collective-permute-start.19 = (bf16[2,64,128]{2,1,0:T(8,128)(2,1)S(1)}, bf16[2,64,128]{2,1,0:T(8,128)(2,1)S(1)}, u32[]{:S(2)}, u32[]{:S(2)}) collective-permute-start(bf16[2,64,128]{2,1,0:T(8,128)(2,1)S(1)} %get-tuple-element.47), channel_id=1, source_target_pairs={{0,6},{1,7},{2,4},{3,5},{4,2},{5,3},{6,0},{7,1},{8,14},{9,15},{10,... | collective-permute-start | bytes 98312 | tf_op jit(solution)/shard_map/ppermute | solution.py:48
  42.9 1.9 %kept_terms.1 = (f32[288,192]{1,0:T(8,128)S(1)}, f32[1,224,192]{2,1,0:T(8,128)S(1)}) custom-call(bf16[896,128]{1,0:T(8,128)(2,1)S(1)} %get-tuple-element.25.refs_0_, bf16[896,128]{1,0:T(8,128)(2,1)S(1)} %collective-permute-done.refs_1_, bf16[896,128]{1,0:T(8,128)(2,1)S(1)} %collective-permute-done.1.refs_2_, ...), custom_call_target="tpu_custom_call" | custom-call | flops 1207959552 | bytes 2392064 | tf_op jit(solution)/shard_map/kept_terms/pallas_call | solution.py:439
  45.0 3.6 %collective-permute-start.17 = (bf16[336,128]{1,0:T(8,128)(2,1)S(1)}, bf16[336,128]{1,0:T(8,128)(2,1)S(1)}, u32[]{:S(2)}, u32[]{:S(2)}) collective-permute-start(bf16[336,128]{1,0:T(8,128)(2,1)S(1)} %halve.1), channel_id=1, source_target_pairs={{0,16},{1,17},{2,18},{3,19},{4,20},{5,21},{6,22},{7,23},{8,24},{9,... | collective-permute-start | bytes 258056 | tf_op jit(solution)/shard_map/ppermute | solution.py:48
  48.7 1.2 %collective-permute-done.20.refs_7_ = bf16[4,64,128]{2,1,0:T(8,128)(2,1)S(1)} collective-permute-done((bf16[4,64,128]{2,1,0:T(8,128)(2,1)S(1)}, bf16[4,64,128]{2,1,0:T(8,128)(2,1)S(1)}, u32[]{:S(2)}, u32[]{:S(2)}) %collective-permute-start.20) | collective-permute-done | bytes 65568 | tf_op jit(solution)/shard_map/ppermute | solution.py:48
  50.0 2.0 %collective-permute-done.17.refs_2_ = bf16[336,128]{1,0:T(8,128)(2,1)S(1)} collective-permute-done((bf16[336,128]{1,0:T(8,128)(2,1)S(1)}, bf16[336,128]{1,0:T(8,128)(2,1)S(1)}, u32[]{:S(2)}, u32[]{:S(2)}) %collective-permute-start.17) | collective-permute-done | bytes 86048 | tf_op jit(solution)/shard_map/ppermute | solution.py:48
  52.0 1.2 %unpack.1 = (bf16[2,1,64,384]{3,2,1,0:T(8,128)(2,1)}, f32[12,27,192]{2,1,0:T(8,128)}) custom-call(f32[288,192]{1,0:T(8,128)S(1)} %get-tuple-element.43.refs_0_, bf16[672,128]{1,0:T(8,128)(2,1)S(1)} %collective-permute-done.15.refs_1_, bf16[336,128]{1,0:T(8,128)(2,1)S(1)} %collective-permute-done.17.refs_2_, ...), custom_call_target="tpu_custom_call" | custom-call | bytes 1022976 | tf_op jit(solution)/shard_map/unpack/pallas_call | solution.py:439
  (36 shorter events, 1.1 us)
Async XLA Ops:
  0.6 0.9 %copy-start.3 = (bf16[12,27,192]{2,1,0:T(8,128)(2,1)S(1)}, bf16[12,27,192]{2,1,0:T(8,128)(2,1)}, u32[]{:S(2)}) copy-start(bf16[12,27,192]{2,1,0:T(8,128)(2,1)} %refs_0_.1) | copy-start | bytes 373252
  1.6 3.7 %copy-start.4 = (bf16[2,1,64,384]{3,2,1,0:T(8,128)(2,1)S(1)}, bf16[2,1,64,384]{3,2,1,0:T(8,128)(2,1)}, u32[]{:S(2)}) copy-start(bf16[2,1,64,384]{3,2,1,0:T(8,128)(2,1)} %param.5) | copy-start | bytes 294916
  2.1 7.7 %collective-permute-start.6 = (bf16[336,128]{1,0:T(8,128)(2,1)S(1)}, bf16[336,128]{1,0:T(8,128)(2,1)S(1)}, u32[]{:S(2)}, u32[]{:S(2)}) collective-permute-start(bf16[336,128]{1,0:T(8,128)(2,1)S(1)} %pack_weights.1.refs_0_), channel_id=1, source_target_pairs={{0,8},{1,9},{2,10},{3,11},{4,12},{5,13},{6,14},{7,15},{8,0},{9,1},... | collective-permute-start | bytes 258056 | tf_op jit(solution)/shard_map/ppermute | solution.py:48
  5.2 0.9 %copy-start = (bf16[2,2,128,192]{2,3,1,0:T(8,128)(2,1)S(1)}, bf16[2,2,128,192]{2,3,1,0:T(8,128)(2,1)}, u32[]{:S(2)}) copy-start(bf16[2,2,128,192]{2,3,1,0:T(8,128)(2,1)} %param.9) | copy-start | bytes 589828
  6.3 8.6 %collective-permute-start = (bf16[896,128]{1,0:T(8,128)(2,1)S(1)}, bf16[896,128]{1,0:T(8,128)(2,1)S(1)}, u32[]{:S(2)}, u32[]{:S(2)}) collective-permute-start(bf16[896,128]{1,0:T(8,128)(2,1)S(1)} %get-tuple-element.26), channel_id=1, source_target_pairs={{0,2},{1,3},{2,0},{3,1},{4,6},{5,7},{6,4},{7,5},{8,10},{9,11},{10,... | collective-permute-start | bytes 688136 | tf_op jit(solution)/shard_map/ppermute | solution.py:48
  7.8 11.7 %collective-permute-start.1 = (bf16[896,128]{1,0:T(8,128)(2,1)S(1)}, bf16[896,128]{1,0:T(8,128)(2,1)S(1)}, u32[]{:S(2)}, u32[]{:S(2)}) collective-permute-start(bf16[896,128]{1,0:T(8,128)(2,1)S(1)} %get-tuple-element.27), channel_id=1, source_target_pairs={{0,4},{1,5},{2,6},{3,7},{4,0},{5,1},{6,2},{7,3},{8,12},{9,13},{10,... | collective-permute-start | bytes 688136 | tf_op jit(solution)/shard_map/ppermute | solution.py:48
  9.3 10.2 %collective-permute-start.2 = (bf16[896,128]{1,0:T(8,128)(2,1)S(1)}, bf16[896,128]{1,0:T(8,128)(2,1)S(1)}, u32[]{:S(2)}, u32[]{:S(2)}) collective-permute-start(bf16[896,128]{1,0:T(8,128)(2,1)S(1)} %get-tuple-element.28), channel_id=1, source_target_pairs={{0,6},{1,7},{2,4},{3,5},{4,2},{5,3},{6,0},{7,1},{8,14},{9,15},{10,... | collective-permute-start | bytes 688136 | tf_op jit(solution)/shard_map/ppermute | solution.py:48
  9.8 9.7 %collective-permute-start.7 = (bf16[672,128]{1,0:T(8,128)(2,1)S(1)}, bf16[672,128]{1,0:T(8,128)(2,1)S(1)}, u32[]{:S(2)}, u32[]{:S(2)}) collective-permute-start(bf16[672,128]{1,0:T(8,128)(2,1)S(1)} %join_kernel_rows.1), channel_id=1, source_target_pairs={{0,16},{1,17},{2,18},{3,19},{4,20},{5,21},{6,22},{7,23},{8,24},{9,... | collective-permute-start | bytes 516104 | tf_op jit(solution)/shard_map/ppermute | solution.py:48
  12.5 8.0 %collective-permute-start.3 = (bf16[896,128]{1,0:T(8,128)(2,1)S(1)}, bf16[896,128]{1,0:T(8,128)(2,1)S(1)}, u32[]{:S(2)}, u32[]{:S(2)}) collective-permute-start(bf16[896,128]{1,0:T(8,128)(2,1)S(1)} %get-tuple-element.25.refs_0_), channel_id=1, source_target_pairs={{0,1},{1,0},{2,3},{3,2},{4,5},{5,4},{6,7},{7,6},{8,9},{9,8},{10,11... | collective-permute-start | bytes 688136 | tf_op jit(solution)/shard_map/ppermute | solution.py:48
  14.9 5.7 %collective-permute-start.4 = (bf16[896,128]{1,0:T(8,128)(2,1)S(1)}, bf16[896,128]{1,0:T(8,128)(2,1)S(1)}, u32[]{:S(2)}, u32[]{:S(2)}) collective-permute-start(bf16[896,128]{1,0:T(8,128)(2,1)S(1)} %collective-permute-done.refs_1_), channel_id=1, source_target_pairs={{0,1},{1,0},{2,3},{3,2},{4,5},{5,4},{6,7},{7,6},{8,9},{9,8},{10,11... | collective-permute-start | bytes 688136 | tf_op jit(solution)/shard_map/ppermute | solution.py:48
  19.5 1.5 %collective-permute-start.5 = (bf16[896,128]{1,0:T(8,128)(2,1)S(1)}, bf16[896,128]{1,0:T(8,128)(2,1)S(1)}, u32[]{:S(2)}, u32[]{:S(2)}) collective-permute-start(bf16[896,128]{1,0:T(8,128)(2,1)S(1)} %collective-permute-done.1.refs_2_), channel_id=1, source_target_pairs={{0,1},{1,0},{2,3},{3,2},{4,5},{5,4},{6,7},{7,6},{8,9},{9,8},{10,11... | collective-permute-start | bytes 688136 | tf_op jit(solution)/shard_map/ppermute | solution.py:48
  19.5 1.8 %collective-permute-start.8 = (bf16[896,128]{1,0:T(8,128)(2,1)S(1)}, bf16[896,128]{1,0:T(8,128)(2,1)S(1)}, u32[]{:S(2)}, u32[]{:S(2)}) collective-permute-start(bf16[896,128]{1,0:T(8,128)(2,1)S(1)} %pass_on.1), channel_id=1, source_target_pairs={{0,1},{1,0},{2,3},{3,2},{4,5},{5,4},{6,7},{7,6},{8,9},{9,8},{10,11... | collective-permute-start | bytes 688136 | tf_op jit(solution)/shard_map/ppermute | solution.py:48
  21.4 6.8 %collective-permute-start.10 = (bf16[48,128]{1,0:T(8,128)(2,1)S(1)}, bf16[48,128]{1,0:T(8,128)(2,1)S(1)}, u32[]{:S(2)}, u32[]{:S(2)}) collective-permute-start(bf16[48,128]{1,0:T(8,128)(2,1)S(1)} %get-tuple-element.32), channel_id=1, source_target_pairs={{0,16},{1,17},{2,18},{3,19},{4,20},{5,21},{6,22},{7,23},{8,24},{9,... | collective-permute-start | bytes 36872 | tf_op jit(solution)/shard_map/ppermute | solution.py:48
  24.0 4.1 %collective-permute-start.9 = (bf16[112,128]{1,0:T(8,128)(2,1)S(1)}, bf16[112,128]{1,0:T(8,128)(2,1)S(1)}, u32[]{:S(2)}, u32[]{:S(2)}) collective-permute-start(bf16[112,128]{1,0:T(8,128)(2,1)S(1)} %get-tuple-element.31), channel_id=1, source_target_pairs={{0,8},{1,9},{2,10},{3,11},{4,12},{5,13},{6,14},{7,15},{8,0},{9,1},... | collective-permute-start | bytes 86024 | tf_op jit(solution)/shard_map/ppermute | solution.py:48
  24.6 5.7 %copy-start.1 = (f32[384]{0:T(512)S(1)}, f32[384]{0:T(512)}, u32[]{:S(2)}) copy-start(f32[384]{0:T(512)} %refs_2_.1) | copy-start | bytes 4612
  24.6 5.7 %copy-start.2 = (f32[384]{0:T(512)S(1)}, f32[384]{0:T(512)}, u32[]{:S(2)}) copy-start(f32[384]{0:T(512)} %refs_3_.1) | copy-start | bytes 4612
  24.6 5.7 %collective-permute-start.11 = (bf16[112,128]{1,0:T(8,128)(2,1)S(1)}, bf16[112,128]{1,0:T(8,128)(2,1)S(1)}, u32[]{:S(2)}, u32[]{:S(2)}) collective-permute-start(bf16[112,128]{1,0:T(8,128)(2,1)S(1)} %get-tuple-element.33), channel_id=1, source_target_pairs={{0,24},{1,25},{2,26},{3,27},{4,28},{5,29},{6,30},{7,31},{8,16},{9,... | collective-permute-start | bytes 86024 | tf_op jit(solution)/shard_map/ppermute | solution.py:48
  31.3 6.4 %collective-permute-start.13 = (bf16[48,128]{1,0:T(8,128)(2,1)S(1)}, bf16[48,128]{1,0:T(8,128)(2,1)S(1)}, u32[]{:S(2)}, u32[]{:S(2)}) collective-permute-start(bf16[48,128]{1,0:T(8,128)(2,1)S(1)} %get-tuple-element.40), channel_id=1, source_target_pairs={{0,16},{1,17},{2,18},{3,19},{4,20},{5,21},{6,22},{7,23},{8,24},{9,... | collective-permute-start | bytes 36872 | tf_op jit(solution)/shard_map/ppermute | solution.py:48
  31.4 6.3 %collective-permute-start.12 = (bf16[176,128]{1,0:T(8,128)(2,1)S(1)}, bf16[176,128]{1,0:T(8,128)(2,1)S(1)}, u32[]{:S(2)}, u32[]{:S(2)}) collective-permute-start(bf16[176,128]{1,0:T(8,128)(2,1)S(1)} %get-tuple-element.39), channel_id=1, source_target_pairs={{0,8},{1,9},{2,10},{3,11},{4,12},{5,13},{6,14},{7,15},{8,0},{9,1},... | collective-permute-start | bytes 135176 | tf_op jit(solution)/shard_map/ppermute | solution.py:48
  33.2 5.8 %collective-permute-start.14 = (bf16[176,128]{1,0:T(8,128)(2,1)S(1)}, bf16[176,128]{1,0:T(8,128)(2,1)S(1)}, u32[]{:S(2)}, u32[]{:S(2)}) collective-permute-start(bf16[176,128]{1,0:T(8,128)(2,1)S(1)} %get-tuple-element.41), channel_id=1, source_target_pairs={{0,24},{1,25},{2,26},{3,27},{4,28},{5,29},{6,30},{7,31},{8,16},{9,... | collective-permute-start | bytes 135176 | tf_op jit(solution)/shard_map/ppermute | solution.py:48
  39.1 5.7 %collective-permute-start.15 = (bf16[672,128]{1,0:T(8,128)(2,1)S(1)}, bf16[672,128]{1,0:T(8,128)(2,1)S(1)}, u32[]{:S(2)}, u32[]{:S(2)}) collective-permute-start(bf16[672,128]{1,0:T(8,128)(2,1)S(1)} %pass_terms.1.refs_7_), channel_id=1, source_target_pairs={{0,8},{1,9},{2,10},{3,11},{4,12},{5,13},{6,14},{7,15},{8,0},{9,1},... | collective-permute-start | bytes 516104 | tf_op jit(solution)/shard_map/ppermute | solution.py:48
  39.3 5.5 %collective-permute-start.16 = (bf16[2,64,128]{2,1,0:T(8,128)(2,1)S(1)}, bf16[2,64,128]{2,1,0:T(8,128)(2,1)S(1)}, u32[]{:S(2)}, u32[]{:S(2)}) collective-permute-start(bf16[2,64,128]{2,1,0:T(8,128)(2,1)S(1)} %get-tuple-element.45), channel_id=1, source_target_pairs={{0,2},{1,3},{2,0},{3,1},{4,6},{5,7},{6,4},{7,5},{8,10},{9,11},{10,... | collective-permute-start | bytes 98312 | tf_op jit(solution)/shard_map/ppermute | solution.py:48
  40.6 8.0 %collective-permute-start.18 = (bf16[2,64,128]{2,1,0:T(8,128)(2,1)S(1)}, bf16[2,64,128]{2,1,0:T(8,128)(2,1)S(1)}, u32[]{:S(2)}, u32[]{:S(2)}) collective-permute-start(bf16[2,64,128]{2,1,0:T(8,128)(2,1)S(1)} %get-tuple-element.46), channel_id=1, source_target_pairs={{0,4},{1,5},{2,6},{3,7},{4,0},{5,1},{6,2},{7,3},{8,12},{9,13},{10,... | collective-permute-start | bytes 98312 | tf_op jit(solution)/shard_map/ppermute | solution.py:48
  42.1 6.5 %collective-permute-start.19 = (bf16[2,64,128]{2,1,0:T(8,128)(2,1)S(1)}, bf16[2,64,128]{2,1,0:T(8,128)(2,1)S(1)}, u32[]{:S(2)}, u32[]{:S(2)}) collective-permute-start(bf16[2,64,128]{2,1,0:T(8,128)(2,1)S(1)} %get-tuple-element.47), channel_id=1, source_target_pairs={{0,6},{1,7},{2,4},{3,5},{4,2},{5,3},{6,0},{7,1},{8,14},{9,15},{10,... | collective-permute-start | bytes 98312 | tf_op jit(solution)/shard_map/ppermute | solution.py:48
  45.0 7.0 %collective-permute-start.17 = (bf16[336,128]{1,0:T(8,128)(2,1)S(1)}, bf16[336,128]{1,0:T(8,128)(2,1)S(1)}, u32[]{:S(2)}, u32[]{:S(2)}) collective-permute-start(bf16[336,128]{1,0:T(8,128)(2,1)S(1)} %halve.1), channel_id=1, source_target_pairs={{0,16},{1,17},{2,18},{3,19},{4,20},{5,21},{6,22},{7,23},{8,24},{9,... | collective-permute-start | bytes 258056 | tf_op jit(solution)/shard_map/ppermute | solution.py:48
  48.6 1.3 %collective-permute-start.20 = (bf16[4,64,128]{2,1,0:T(8,128)(2,1)S(1)}, bf16[4,64,128]{2,1,0:T(8,128)(2,1)S(1)}, u32[]{:S(2)}, u32[]{:S(2)}) collective-permute-start(bf16[4,64,128]{2,1,0:T(8,128)(2,1)S(1)} %cross_grads.1), channel_id=1, source_target_pairs={{0,1},{1,0},{2,3},{3,2},{4,5},{5,4},{6,7},{7,6},{8,9},{9,8},{10,11... | collective-permute-start | bytes 196616 | tf_op jit(solution)/shard_map/ppermute | solution.py:48

commit v3 on v2

--- a/solution.py
+++ b/solution.py
@@ -38,8 +38,7 @@
         self.order = [*range(1, self.outer, 2), *range(0, self.outer, 2)]
         self.grows = 2 * self.grad_frames * self.outs
         self.count = float(low_rows * tiles * self.cols * self.per)
-        self.steps = [k for k in range(1, self.outer) if k & (k + 1) == 0]
-        if low_rows != 1 or tiles != GROUPS or self.hi != 64 or self.outer > 8:
+        if low_rows != 1 or tiles != GROUPS or self.hi != 64 or self.outer != 4:
             raise ValueError("unsupported sizes")
 
 
@@ -95,16 +94,12 @@
     return out
 
 
-def sort_acts_kernel(g, acts_ref, out_ref):
+def sort_acts_kernel(g, acts_ref, *out_refs):
     _, w = place(g)
     pick = channel_select(g, w, g.inner).astype(BF16)
-    out_ref[...] = dot(pick, acts_ref[...], ((1,), (1,))).astype(BF16)
-
-
-def pack_kernel(g, blocks_ref, grads_ref, *out_refs):
+    blocks = dot(pick, acts_ref[...], ((1,), (1,))).astype(BF16)
     for k, ref in enumerate(out_refs):
-        ref[: g.grows] = grads_ref[...]
-        ref[g.grows :] = blocks_ref[2 * k * g.rb : 2 * (k + 1) * g.rb]
+        ref[...] = blocks[2 * k * g.rb : 2 * (k + 1) * g.rb].reshape(2, g.rb, g.cells)
 
 
 def pack_rows(g, value):
@@ -142,34 +137,57 @@
     return jnp.concatenate(out, axis=0)
 
 
-def send_stats(g, refs, stats, z, rows_ref, parts):
-    pieces = split(stats, 3)
-    last = rows_ref.shape[0] - 1
-    for k, ref in enumerate(refs, 1):
-        for i, piece in enumerate(pieces):
-            ref[i * SPLIT : (i + 1) * SPLIT] = piece
-        if k in g.steps:
-            edge = rows_ref[jnp.where((z ^ k) == z + 1, last, 0)]
-            for i, piece in enumerate(split(edge, parts) if parts > 1 else [edge]):
-                ref[3 * SPLIT + i * g.rb : 3 * SPLIT + (i + 1) * g.rb] = piece
+def put_stats(ref, stats):
+    for i, piece in enumerate(split(stats, 3)):
+        ref[i * SPLIT : (i + 1) * SPLIT] = piece
+
+
+def send_stats(g, ref, stats, z, rows_ref, parts):
+    put_stats(ref, stats)
+    last, even = rows_ref.shape[0] - 1, (z & 1) == 0
+    for n, row in enumerate((jnp.where(even, last, 0), jnp.where(even, 0, last))):
+        edge = rows_ref[row]
+        for i, piece in enumerate(split(edge, parts) if parts > 1 else [edge.astype(BF16)]):
+            at = 3 * SPLIT + (n * parts + i) * g.rb
+            ref[at : at + g.rb] = piece
+
+
+def step_kernel(g, stats_ref, received_ref, total_ref, send_ref):
+    stats = add_stats(stats_ref[...], [received_ref])
+    total_ref[...] = stats
+    put_stats(send_ref, stats)
+    count = send_ref.shape[0] - 3 * SPLIT
+    send_ref[3 * SPLIT :] = received_ref[3 * SPLIT + count :]
+
+
+def edges(g, z, received, parts):
+    near, far = (
+        sum(
+            ref[3 * SPLIT + i * g.rb : 3 * SPLIT + (i + 1) * g.rb].astype(F32)
+            for i in range(parts)
+        )
+        for ref in received
+    )
+    odd = (z & 1) == 1
+    above = jnp.where(odd, near, jnp.where((z ^ 3) == z - 1, far, 0.0))
+    below = jnp.where(odd, jnp.where((z ^ 3) == z + 1, far, 0.0), near)
+    return above, below
 
 
 def stats_kernel(g, *refs):
-    direct, crossed, refs = refs[: g.pairs], refs[g.pairs : 2 * g.pairs], refs[2 * g.pairs :]
-    rows_ref, stats_ref, *sends = refs
+    direct, (crossed, rows_ref, stats_ref, send_ref) = refs[: g.pairs], refs[g.pairs :]
     z, w = place(g)
     first = jnp.zeros((g.rb, g.cells), F32)
     second = jnp.zeros((g.rb, g.cells), F32)
     for k in range(g.pairs):
-        for j, ref in enumerate((direct[k], crossed[k])):
-            block = ref[g.grows + j * g.rb : g.grows + (j + 1) * g.rb]
+        for j, block in enumerate((direct[k][0], crossed[k])):
             rows_ref[w ^ (2 * k + j)] = block
             wide = block.astype(F32)
             first = first + wide
             second = second + wide * wide
     stats = totals(g, first, second)
     stats_ref[...] = stats
-    send_stats(g, sends, stats, z, rows_ref, 1)
+    send_stats(g, send_ref, stats, z, rows_ref, 1)
 
 
 def add_stats(own, received):
@@ -225,43 +243,41 @@
     return slice((3 * t + e) * g.wide, (3 * t + e + 1) * g.wide)
 
 
-def field_kernel(g, *refs):
-    direct, crossed, refs = refs[: g.pairs], refs[g.pairs : 2 * g.pairs], refs[2 * g.pairs :]
-    weights_ref, field = refs
+def field_kernel(g, j, *refs):
+    *tiles, weights_ref, field = refs
     _, w = place(g)
     rb, wide = g.rb, g.wide
     field[...] = jnp.zeros_like(field)
-    for k in range(g.pairs):
-        for j, ref in enumerate((direct[k], crossed[k])):
-            row = w ^ (2 * k + j)
-            for later in range(g.grad_frames):
-                pairs = meetings(g, later)
-                if not pairs:
-                    continue
-                low, high = pairs[0][0] - g.first, pairs[-1][0] - g.first + 1
-                taps = weights_ref[9 * low : 9 * high].reshape(9 * (high - low) * rb, 256)
-                every = dot(taps[:, : g.outs], fine_rows(g, ref, later))
-                for n, (_, t) in enumerate(pairs):
-                    back = every[9 * n * rb : 9 * (n + 1) * rb]
-                    part = lambda b, e, fine: back[
-                        (3 * b + e) * rb : (3 * b + e + 1) * rb, fine * wide : (fine + 1) * wide
-                    ]
-                    for e in range(3):
-                        lanes = lanes_of(g, t, e)
-                        field[row, :, lanes] += part(0, e, 0)
-                        field[row + 1, :, lanes] += (part(1, e, 0) + part(2, e, 0)) + (
-                            part(0, e, 1) + part(1, e, 1)
-                        )
-                        field[row + 2, :, lanes] += part(2, e, 1)
+    for k, ref in enumerate(tiles):
+        row = w ^ (2 * k + j)
+        for later in range(g.grad_frames):
+            pairs = meetings(g, later)
+            if not pairs:
+                continue
+            low, high = pairs[0][0] - g.first, pairs[-1][0] - g.first + 1
+            taps = weights_ref[9 * low : 9 * high].reshape(9 * (high - low) * rb, 256)
+            every = dot(taps[:, : g.outs], fine_rows(g, ref, later))
+            for n, (_, t) in enumerate(pairs):
+                back = every[9 * n * rb : 9 * (n + 1) * rb]
+                part = lambda b, e, fine: back[
+                    (3 * b + e) * rb : (3 * b + e + 1) * rb, fine * wide : (fine + 1) * wide
+                ]
+                for e in range(3):
+                    lanes = lanes_of(g, t, e)
+                    field[row, :, lanes] += part(0, e, 0)
+                    field[row + 1, :, lanes] += (part(1, e, 0) + part(2, e, 0)) + (
+                        part(0, e, 1) + part(1, e, 1)
+                    )
+                    field[row + 2, :, lanes] += part(2, e, 1)
 
 
 def norm_grad_kernel(g, *refs):
-    rows_ref, stats_ref, gamma_ref, beta_ref, field_ref, *refs = refs
-    received, refs = refs[: g.outer - 1], refs[g.outer - 1 :]
-    normed_ref, hidden_ref, inv_ref, sums_ref, grad_ref, *sends, slope_ref, hidden_scratch = refs
+    rows_ref, stats_ref, gamma_ref, beta_ref, field_ref, other_ref, *refs = refs
+    received, refs = refs[:2], refs[2:]
+    normed_ref, hidden_ref, inv_ref, sums_ref, grad_ref, send_ref, slope_ref, hidden_scratch = refs
     z, w = place(g)
     rb = g.rb
-    total, total_sq = spread(g, add_stats(stats_ref[...], received))
+    total, total_sq = spread(g, add_stats(stats_ref[...], received[1:]))
     mean = total / g.count
     inv = lax.rsqrt(total_sq / g.count - mean * mean + norm_eps)
     inv_ref[...] = inv
@@ -280,13 +296,9 @@
             hidden_ref[at, place_at] = hidden_scratch[z ^ k]
         slope_ref[place_at] = gate * (1.0 + shifted * (1.0 - gate)) * gamma * present
 
-    for place_at, step in ((0, -1), (g.inner + 1, 1)):
-        block = jnp.zeros((rb, g.cells), BF16)
-        for k in g.steps:
-            edge = received[k - 1][3 * SPLIT : 3 * SPLIT + rb]
-            block = jnp.where((z ^ k) == z + step, edge, block)
-        inside = (z + step >= 0) & (z + step < g.outer)
-        activate(place_at, block, jnp.where(inside, 1.0, 0.0))
+    above, below = edges(g, z, received, 1)
+    activate(0, above, jnp.where(z > 0, 1.0, 0.0))
+    activate(g.inner + 1, below, jnp.where(z < g.outer - 1, 1.0, 0.0))
 
     @pl.loop(0, g.inner)
     def _(i):
@@ -294,14 +306,14 @@
 
     count = g.inner + 2
     select = column_select(g)
-    flat = field_ref[...].reshape(count * rb, g.frames * 3 * g.wide)
+    flat = (field_ref[...] + other_ref[...]).reshape(count * rb, g.frames * 3 * g.wide)
     pieces = split(flat, 2)
     act_grad = dot(pieces[0], select, ((1,), (1,))) + dot(pieces[1], select, ((1,), (1,)))
     grad = act_grad.reshape(count, rb, g.cells) * slope_ref[...]
     grad_ref[...] = grad
     sums = totals(g, jnp.sum(grad, axis=0), jnp.sum(grad * normed_ref[...], axis=0))
     sums_ref[...] = sums
-    send_stats(g, sends, sums, z, grad_ref, 2)
+    send_stats(g, send_ref, sums, z, grad_ref, 1)
 
 
 def kernel_terms(g, first, direct, crossed, hidden_ref, acc, ups):
@@ -377,25 +389,18 @@
 
 def finish_kernel(g, *refs):
     sums_ref, grad_ref, normed_ref, inv_ref, *refs = refs
-    received, sends = refs[: g.outer - 1], refs[g.outer - 1 :]
+    received, sends = refs[:2], refs[2:]
     z, w = place(g)
-    first, second = spread(g, add_stats(sums_ref[...], received))
+    first, second = spread(g, add_stats(sums_ref[...], received[1:]))
     first, second = first / g.count, second / g.count
     inv = inv_ref[...]
-    edges = []
-    for step in (-1, 1):
-        edge = jnp.zeros((g.rb, g.cells), F32)
-        for k in g.steps:
-            ref, at = received[k - 1], 3 * SPLIT
-            value = ref[at : at + g.rb].astype(F32) + ref[at + g.rb :].astype(F32)
-            edge = jnp.where((z ^ k) == z + step, value, edge)
-        edges.append(edge)
+    above, below = edges(g, z, received, 1)
     for k, ref in enumerate(sends):
         for j in range(2):
             row = w ^ (2 * k + j)
             grad = grad_ref[row + 1]
-            grad = grad + jnp.where(row == 0, edges[0], 0.0)
-            grad = grad + jnp.where(row == g.inner - 1, edges[1], 0.0)
+            grad = grad + jnp.where(row == 0, above, 0.0)
+            grad = grad + jnp.where(row == g.inner - 1, below, 0.0)
             ref[j] = (inv * (grad - first - normed_ref[row + 1] * second)).astype(BF16)
 
 
@@ -460,6 +465,10 @@
         at += ref.shape[0]
 
 
+def pass_on(g, value, after):
+    return call(g, copy_kernel, "pass_on", [(value.shape, value.dtype)], [value], after=after)[0]
+
+
 def cross_kernel(g, *refs):
     *blocks, out_ref = refs
     for k, ref in enumerate(blocks):
@@ -484,11 +493,13 @@
     stats_shape = ((SPLIT, g.cells), F32)
     packed_shape = ((g.wrows, 128), BF16)
     wide_shape = (count, g.rb, g.frames * 3 * g.wide)
-    over_z = lambda values: [swap(v, g.inner * k) for k, v in enumerate(values, 1)]
-    sums_shapes = lambda parts: [
-        ((3 * SPLIT + (parts * g.rb if k in g.steps else 0), 128), BF16)
-        for k in range(1, g.outer)
-    ]
+    sums_shape = lambda edges: ((3 * SPLIT + edges * g.rb, 128), BF16)
+
+    def over_z(name, stats, send, parts, after):
+        near = swap(send, g.inner)
+        outs = [stats_shape, sums_shape(parts)]
+        total, send = call(g, step_kernel, name, outs, [stats, near], after=after)
+        return total, send, [near, swap(send, 2 * g.inner)]
 
     packed = list(
         call(g, pack_weights_kernel, "pack_weights", [packed_shape], [weights], flops=6 * 10**9)
@@ -499,58 +510,59 @@
             shape = ((g.wrows << bit, 128), BF16)
             (whole,) = call(g, join_kernel, "join_kernel_rows", [shape], packed)
         packed.append(swap(whole, g.inner << bit))
-    (blocks,) = call(
+    sends = call(
         g,
         sort_acts_kernel,
         "sort_acts",
-        [((g.inner * g.rb, g.cells), BF16)],
+        [block] * g.pairs,
         [acts.reshape(g.cells, g.chans)],
-        flops=6 * 10**9,
-    )
-    sends = call(
-        g,
-        pack_kernel,
-        "pack",
-        [((g.grows + 2 * g.rb, g.cells), BF16)] * g.pairs,
-        [blocks, jnp.swapaxes(cotangent, 2, 3).reshape(g.grows, g.wide)],
-    )
-    direct = [sends[0]] + [swap(sends[k], 2 * k) for k in range(1, g.pairs)]
-    (last,) = call(
-        g, copy_kernel, "pass_on", [(sends[0].shape, BF16)], direct[-1:], after=packed[1:]
-    )
-    arrived = direct + [swap(v, 1) for v in direct[:-1] + [last]]
-    rows, stats, *sends = call(
+        flops=2*10**9,
+    )
+    blocks = [sends[0]] + [swap(sends[k], 2 * k) for k in range(1, g.pairs)]
+    blocks.append(cross(g, "cross_acts", blocks))
+    turned = jnp.swapaxes(cotangent, 2, 3).reshape(g.grows, g.wide)
+    direct = [turned] + [swap(turned, 2 * k) for k in range(1, g.pairs)]
+    arrived = direct + [swap(v, 1) for v in direct]
+
+    rows, stats, send = call(
         g,
         stats_kernel,
         "stats",
-        [((g.inner, g.rb, g.cells), BF16), stats_shape] + sums_shapes(1),
-        arrived,
-    )
-    received = over_z(sends)
+        [((g.inner, g.rb, g.cells), BF16), stats_shape, sums_shape(2)],
+        blocks,
+        flops=5*10**9,
+    )
     kernel_shape = ((g.used, g.outer, g.gp, 256), BF16)
-    (rows_of_kernel,) = call(g, prepare_weights_kernel, "kernel_rows", [kernel_shape], packed)
+    (rows_of_kernel,) = call(g, prepare_weights_kernel, "kernel_rows", [kernel_shape], packed, flops=7*10**9)
     flops = 2 * 2 * g.inner * 9 * g.rb * 256 * 256 * g.grad_frames
-    (field,) = call(
-        g, field_kernel, "field_grad", [(wide_shape, F32)], arrived + [rows_of_kernel], flops=flops
-    )
+    fields = [
+        call(
+            g,
+            lambda g, *refs, j=j: field_kernel(g, j, *refs),
+            "field_grad",
+            [(wide_shape, F32)],
+            arrived[j * g.pairs : (j + 1) * g.pairs] + [rows_of_kernel],
+            flops=flops // 2,
+        )[0]
+        for j in range(2)
+    ]
+    stats, _, received = over_z("add_stats", stats, send, 1, ())
     hidden_shape = ((g.outer, count, g.gp, g.cells), BF16)
-    normed, hidden, inv, sums, grad, *sends = call(
+    normed, hidden, inv, sums, grad, send = call(
         g,
         norm_grad_kernel,
         "norm_grad",
-        [rows_shape, hidden_shape, ((g.rb, g.cells), F32), stats_shape, rows_shape]
-        + sums_shapes(2),
-        [rows, stats, gamma, beta, field] + received,
+        [rows_shape, hidden_shape, ((g.rb, g.cells), F32), stats_shape, rows_shape, sums_shape(2)],
+        [rows, stats, gamma, beta] + fields + received,
         [pltpu.VMEM(*rows_shape), pltpu.VMEM((g.outer, g.gp, g.cells), BF16)],
     )
-    received = over_z(sends)
     half = g.outer // 2
     kept_shape = lambda count: [((count, g.sent, g.outs), F32)] if count else []
     scratch = [
         pltpu.VMEM((half, g.used, g.gp, g.outs), F32),
         pltpu.VMEM((half, count, g.gp, wide_shape[-1]), BF16),
     ]
-    (send,) = call(
+    (terms,) = call(
         g,
         sent_terms_kernel,
         "sent_terms",
@@ -559,17 +571,8 @@
         scratch,
         flops // 2,
     )
-    (send,) = call(g, copy_kernel, "pass_terms", [(send.shape, BF16)], [send], after=received)
-    terms = [swap(send, g.inner)]
-    sends = call(
-        g,
-        finish_kernel,
-        "finish",
-        [block] * g.pairs,
-        [sums, grad, normed, inv] + received,
-        after=[send],
-    )
-    direct = [sends[0]] + [swap(sends[k], 2 * k) for k in range(1, g.pairs)]
+    sums, send, received = over_z("add_sums", sums, send, 1, [terms])
+    terms = [swap(pass_on(g, terms, [send]), g.inner)]
     own, *kept = call(
         g,
         kept_terms_kernel,
@@ -578,8 +581,17 @@
         arrived + [hidden],
         scratch,
         flops // 2,
-        after=sends[:1],
-    )
+        after=[send],
+    )
+    sends = call(
+        g,
+        finish_kernel,
+        "finish",
+        [block] * g.pairs,
+        [sums, grad, normed, inv] + received,
+        after=[own],
+    )
+    direct = [sends[0]] + [swap(sends[k], 2 * k) for k in range(1, g.pairs)]
     bit = 1
     while kept:
         half //= 2
@@ -589,7 +601,6 @@
             "halve",
             [((half * g.wrows, 128), BF16)] + kept_shape(half - 1),
             [kept[0], terms[-1]],
-            after=direct[1:2],
         )
         terms.append(swap(send, g.inner << bit))
         bit += 1

time: 53.4 us -> 50.9 us (0.953)
  waiting for transfers between devices: 14.5 us -> 9.6 us
  starting transfers between devices: 26.1 us -> 29 us
  local copies, waits for them, and re-layouts: 1.56 us -> 0.91 us
    ppermute x21 -> x23, waiting for transfers between devices: 14.5 us -> 9.6 us  [swap(): return lax.ppermute(value, 'tile', [(i, i ^ mask) for i in range(count)])]
    ppermute x21 -> x23, starting transfers between devices: 26.1 us -> 29 us  [swap(): return lax.ppermute(value, 'tile', [(i, i ^ mask) for i in range(count)])]
    unnamed x10, local copies, waits for them, and re-layouts: 1.56 us -> 0.91 us
    pallas_call x16 -> x18, Pallas kernels: 10.2 us -> 10.4 us  [call(): pl.pallas_call(lambda *refs: kernel(g, *refs[:count], *refs[rest:]), out_...]
  transfers between devices with their start and end apart: 21 -> 23, of which waited for: 8 -> 6; matrix products, arithmetic and copies ran while one was open for 0% -> 0% of each run, Pallas kernels for 14% -> 15%
where the time goes in v3:
time: 50.9 us; the launch traced here: 50.8 us
  starting transfers between devices  29 us (57%)
  Pallas kernels  10.4 us (20%)
  waiting for transfers between devices  9.6 us (19%)
  local copies, waits for them, and re-layouts  0.91 us (2%)
  between operations  0.83 us (2%)
    ppermute x23, starting transfers between devices, swap(): return lax.ppermute(value, 'tile', [(i, i ^ mask) for i in range(count)])  29 us
    pallas_call x18, Pallas kernels, call(): pl.pallas_call(lambda *refs: kernel(g, *refs[:count], *refs[rest:]), out_...  10.4 us
    ppermute x23, waiting for transfers between devices, swap(): return lax.ppermute(value, 'tile', [(i, i ^ mask) for i in range(count)])  9.6 us
  transfers between devices with their start and end apart: 23, of which 6 were waited for; matrix products, arithmetic and copies ran while one was open for 0% of the time, Pallas kernels for 15%

profile of v3, /device:TPU:0, one launch (start us, length us, event | category | flops | bytes accessed | tf_op | source)
XLA Modules:
  0.0 50.8 jit_solution(4524798368804559156)
XLA Ops:
  0.6 0.9 %copy-done.4 = bf16[2,1,64,384]{3,2,1,0:T(8,128)(2,1)S(1)} copy-done((bf16[2,1,64,384]{3,2,1,0:T(8,128)(2,1)S(1)}, bf16[2,1,64,384]{3,2,1,0:T(8,128)(2,1)}, u32[]{:S(2)}) %copy-start.4) | copy-done | bytes 98328
  1.5 0.3 sort_acts.1
  1.8 3.0 %collective-permute-start.7 = (bf16[2,64,128]{2,1,0:T(8,128)(2,1)S(1)}, bf16[2,64,128]{2,1,0:T(8,128)(2,1)S(1)}, u32[]{:S(2)}, u32[]{:S(2)}) collective-permute-start(bf16[2,64,128]{2,1,0:T(8,128)(2,1)S(1)} %get-tuple-element.26), channel_id=1, source_target_pairs={{0,2},{1,3},{2,0},{3,1},{4,6},{5,7},{6,4},{7,5},{8,10},{9,11},{10,... | collective-permute-start | bytes 98312 | tf_op jit(solution)/shard_map/ppermute | solution.py:47
  4.8 1.5 %collective-permute-start.8 = (bf16[2,64,128]{2,1,0:T(8,128)(2,1)S(1)}, bf16[2,64,128]{2,1,0:T(8,128)(2,1)S(1)}, u32[]{:S(2)}, u32[]{:S(2)}) collective-permute-start(bf16[2,64,128]{2,1,0:T(8,128)(2,1)S(1)} %get-tuple-element.27), channel_id=1, source_target_pairs={{0,4},{1,5},{2,6},{3,7},{4,0},{5,1},{6,2},{7,3},{8,12},{9,13},{10,... | collective-permute-start | bytes 98312 | tf_op jit(solution)/shard_map/ppermute | solution.py:47
  6.4 0.6 %pack_weights.1.refs_0_ = bf16[336,128]{1,0:T(8,128)(2,1)S(1)} custom-call(bf16[12,27,192]{2,1,0:T(8,128)(2,1)S(1)} %copy-done.2), custom_call_target="tpu_custom_call" | custom-call | flops 6000000000 | bytes 210432 | tf_op jit(solution)/shard_map/pack_weights/pallas_call | solution.py:444
  6.9 2.1 %collective-permute-start.12 = (bf16[336,128]{1,0:T(8,128)(2,1)S(1)}, bf16[336,128]{1,0:T(8,128)(2,1)S(1)}, u32[]{:S(2)}, u32[]{:S(2)}) collective-permute-start(bf16[336,128]{1,0:T(8,128)(2,1)S(1)} %pack_weights.1.refs_0_), channel_id=1, source_target_pairs={{0,8},{1,9},{2,10},{3,11},{4,12},{5,13},{6,14},{7,15},{8,0},{9,1},... | collective-permute-start | bytes 258056 | tf_op jit(solution)/shard_map/ppermute | solution.py:47
  9.0 2.1 %collective-permute-done.9.refs_3_ = bf16[2,64,128]{2,1,0:T(8,128)(2,1)S(1)} collective-permute-done((bf16[2,64,128]{2,1,0:T(8,128)(2,1)S(1)}, bf16[2,64,128]{2,1,0:T(8,128)(2,1)S(1)}, u32[]{:S(2)}, u32[]{:S(2)}) %collective-permute-start.9) | collective-permute-done | bytes 32800 | tf_op jit(solution)/shard_map/ppermute | solution.py:47
  11.2 0.5 collective-permute-start.2
  11.7 1.6 %collective-permute-start.1 = (bf16[768,128]{1,0:T(8,128)(2,1)S(1)}, bf16[768,128]{1,0:T(8,128)(2,1)S(1)}, u32[]{:S(2)}, u32[]{:S(2)}) collective-permute-start(bf16[768,128]{1,0:T(8,128)(2,1)S(1)} %bitcast.5), channel_id=1, source_target_pairs={{0,4},{1,5},{2,6},{3,7},{4,0},{5,1},{6,2},{7,3},{8,12},{9,13},{10,... | collective-permute-start | bytes 589832 | tf_op jit(solution)/shard_map/ppermute | solution.py:47
  13.2 1.5 %collective-permute-start = (bf16[768,128]{1,0:T(8,128)(2,1)S(1)}, bf16[768,128]{1,0:T(8,128)(2,1)S(1)}, u32[]{:S(2)}, u32[]{:S(2)}) collective-permute-start(bf16[768,128]{1,0:T(8,128)(2,1)S(1)} %bitcast.6), channel_id=1, source_target_pairs={{0,2},{1,3},{2,0},{3,1},{4,6},{5,7},{6,4},{7,5},{8,10},{9,11},{10,... | collective-permute-start | bytes 589832 | tf_op jit(solution)/shard_map/ppermute | solution.py:47
  14.8 2.7 %collective-permute-start.13 = (bf16[672,128]{1,0:T(8,128)(2,1)S(1)}, bf16[672,128]{1,0:T(8,128)(2,1)S(1)}, u32[]{:S(2)}, u32[]{:S(2)}) collective-permute-start(bf16[672,128]{1,0:T(8,128)(2,1)S(1)} %join_kernel_rows.1), channel_id=1, source_target_pairs={{0,16},{1,17},{2,18},{3,19},{4,20},{5,21},{6,22},{7,23},{8,24},{9,... | collective-permute-start | bytes 516104 | tf_op jit(solution)/shard_map/ppermute | solution.py:47
  17.5 1.6 %collective-permute-start.11 = (bf16[176,128]{1,0:T(8,128)(2,1)S(1)}, bf16[176,128]{1,0:T(8,128)(2,1)S(1)}, u32[]{:S(2)}, u32[]{:S(2)}) collective-permute-start(bf16[176,128]{1,0:T(8,128)(2,1)S(1)} %get-tuple-element.31), channel_id=1, source_target_pairs={{0,8},{1,9},{2,10},{3,11},{4,12},{5,13},{6,14},{7,15},{8,0},{9,1},... | collective-permute-start | bytes 135176 | tf_op jit(solution)/shard_map/ppermute | solution.py:47
  19.1 2.7 %collective-permute-done.11.refs_1_.refs_6_ = bf16[176,128]{1,0:T(8,128)(2,1)S(1)} collective-permute-done((bf16[176,128]{1,0:T(8,128)(2,1)S(1)}, bf16[176,128]{1,0:T(8,128)(2,1)S(1)}, u32[]{:S(2)}, u32[]{:S(2)}) %collective-permute-start.11) | collective-permute-done | bytes 45088 | tf_op jit(solution)/shard_map/ppermute | solution.py:47
  21.9 2.4 %collective-permute-start.14 = (bf16[112,128]{1,0:T(8,128)(2,1)S(1)}, bf16[112,128]{1,0:T(8,128)(2,1)S(1)}, u32[]{:S(2)}, u32[]{:S(2)}) collective-permute-start(bf16[112,128]{1,0:T(8,128)(2,1)S(1)} %get-tuple-element.33), channel_id=1, source_target_pairs={{0,16},{1,17},{2,18},{3,19},{4,20},{5,21},{6,22},{7,23},{8,24},{9,... | collective-permute-start | bytes 86024 | tf_op jit(solution)/shard_map/ppermute | solution.py:47
  24.8 0.5 collective-permute-done.13.refs_2_
  25.3 0.4 kernel_rows.1.refs_4_
  25.7 1.3 %field_grad.2.refs_4_ = f32[10,64,768]{2,1,0:T(8,128)S(1)} custom-call(bf16[768,128]{1,0:T(8,128)(2,1)S(1)} %bitcast.8, bf16[768,128]{1,0:T(8,128)(2,1)S(1)} %collective-permute-done.refs_1_, bf16[768,128]{1,0:T(8,128)(2,1)S(1)} %collective-permute-done.1.refs_2_, bf16[768,128]{1,0:T(8,128)(2,1)S(1)} %collective-permute-done.2.refs_3_, ...), custom_call_target="tpu_custom_call" | custom-call | flops 1207959552 | bytes 3342336 | tf_op jit(solution)/shard_map/field_grad/pallas_call | solution.py:444
  27.1 1.2 %field_grad.3.refs_5_ = f32[10,64,768]{2,1,0:T(8,128)S(1)} custom-call(bf16[768,128]{1,0:T(8,128)(2,1)S(1)} %collective-permute-done.3.refs_0_.refs_4_, bf16[768,128]{1,0:T(8,128)(2,1)S(1)} %collective-permute-done.4.refs_1_.refs_5_, bf16[768,128]{1,0:T(8,128)(2,1)S(1)} %collective-permute-done.5.refs_2_.refs_6_, ...), custom_call_target="tpu_custom_call" | custom-call | flops 1207959552 | bytes 3342336 | tf_op jit(solution)/shard_map/field_grad/pallas_call | solution.py:444
  28.4 1.1 %norm_grad.1 = (f32[10,64,128]{2,1,0:T(8,128)S(1)}, bf16[4,10,16,128]{3,2,1,0:T(8,128)(2,1)S(1)}, f32[64,128]{1,0:T(8,128)S(1)}, f32[16,128]{1,0:T(8,128)S(1)}, ...) custom-call(bf16[8,64,128]{2,1,0:T(8,128)(2,1)S(1)} %get-tuple-element.29.refs_0_, ...), custom_call_target="tpu_custom_call" | custom-call | bytes 5053440 | tf_op jit(solution)/shard_map/norm_grad/pallas_call | solution.py:444
  29.5 0.9 %collective-permute-start.15 = (bf16[176,128]{1,0:T(8,128)(2,1)S(1)}, bf16[176,128]{1,0:T(8,128)(2,1)S(1)}, u32[]{:S(2)}, u32[]{:S(2)}) collective-permute-start(bf16[176,128]{1,0:T(8,128)(2,1)S(1)} %get-tuple-element.36), channel_id=1, source_target_pairs={{0,8},{1,9},{2,10},{3,11},{4,12},{5,13},{6,14},{7,15},{8,0},{9,1},... | collective-permute-start | bytes 135176 | tf_op jit(solution)/shard_map/ppermute | solution.py:47
  30.4 1.9 %sent_terms.1.refs_2_.refs_0_ = bf16[672,128]{1,0:T(8,128)(2,1)S(1)} custom-call(bf16[768,128]{1,0:T(8,128)(2,1)S(1)} %bitcast.9, bf16[768,128]{1,0:T(8,128)(2,1)S(1)} %collective-permute-done.refs_1_, bf16[768,128]{1,0:T(8,128)(2,1)S(1)} %collective-permute-done.1.refs_2_, bf16[768,128]{1,0:T(8,128)(2,1)S(1)} %collective-permute-done.2.refs_3_, ...), custom_call_target="tpu_custom_call" | custom-call | flops 1207959552 | bytes 1908736 | tf_op jit(solution)/shard_map/sent_terms/pallas_call | solution.py:444
  32.3 1.3 %collective-permute-done.15.refs_1_.refs_4_ = bf16[176,128]{1,0:T(8,128)(2,1)S(1)} collective-permute-done((bf16[176,128]{1,0:T(8,128)(2,1)S(1)}, bf16[176,128]{1,0:T(8,128)(2,1)S(1)}, u32[]{:S(2)}, u32[]{:S(2)}) %collective-permute-start.15) | collective-permute-done | bytes 45088 | tf_op jit(solution)/shard_map/ppermute | solution.py:47
  33.7 0.9 %collective-permute-start.16 = (bf16[672,128]{1,0:T(8,128)(2,1)S(1)}, bf16[672,128]{1,0:T(8,128)(2,1)S(1)}, u32[]{:S(2)}, u32[]{:S(2)}) collective-permute-start(bf16[672,128]{1,0:T(8,128)(2,1)S(1)} %pass_on.1), channel_id=1, source_target_pairs={{0,8},{1,9},{2,10},{3,11},{4,12},{5,13},{6,14},{7,15},{8,0},{9,1},... | collective-permute-start | bytes 516104 | tf_op jit(solution)/shard_map/ppermute | solution.py:47
  34.5 3.4 %collective-permute-start.18 = (bf16[112,128]{1,0:T(8,128)(2,1)S(1)}, bf16[112,128]{1,0:T(8,128)(2,1)S(1)}, u32[]{:S(2)}, u32[]{:S(2)}) collective-permute-start(bf16[112,128]{1,0:T(8,128)(2,1)S(1)} %get-tuple-element.37.refs_9_.refs_1_), channel_id=1, source_target_pairs={{0,16},{1,17},{2,18},{3,19},{4,20},{5,21},{6,22},{7,23},{8,24},{9,... | collective-permute-start | bytes 86024 | tf_op jit(solution)/shard_map/ppermute | solution.py:47
  37.9 1.9 %kept_terms.1 = (f32[288,192]{1,0:T(8,128)S(1)}, f32[1,224,192]{2,1,0:T(8,128)S(1)}) custom-call(bf16[768,128]{1,0:T(8,128)(2,1)S(1)} %bitcast.10, bf16[768,128]{1,0:T(8,128)(2,1)S(1)} %collective-permute-done.refs_1_, bf16[768,128]{1,0:T(8,128)(2,1)S(1)} %collective-permute-done.1.refs_2_, bf16[768,128]{1,0:T(8,128)(2,1)S(1)} %collective-permute-done.2.refs_3_, ...), custom_call_target="tpu_custom_call" | custom-call | flops 1207959552 | bytes 2129920 | tf_op jit(solution)/shard_map/kept_terms/pallas_call | solution.py:444
  40.0 0.6 %collective-permute-start.19 = (bf16[2,64,128]{2,1,0:T(8,128)(2,1)S(1)}, bf16[2,64,128]{2,1,0:T(8,128)(2,1)S(1)}, u32[]{:S(2)}, u32[]{:S(2)}) collective-permute-start(bf16[2,64,128]{2,1,0:T(8,128)(2,1)S(1)} %get-tuple-element.45), channel_id=1, source_target_pairs={{0,2},{1,3},{2,0},{3,1},{4,6},{5,7},{6,4},{7,5},{8,10},{9,11},{10,... | collective-permute-start | bytes 98312 | tf_op jit(solution)/shard_map/ppermute | solution.py:47
  40.6 0.5 %collective-permute-start.20 = (bf16[2,64,128]{2,1,0:T(8,128)(2,1)S(1)}, bf16[2,64,128]{2,1,0:T(8,128)(2,1)S(1)}, u32[]{:S(2)}, u32[]{:S(2)}) collective-permute-start(bf16[2,64,128]{2,1,0:T(8,128)(2,1)S(1)} %get-tuple-element.46), channel_id=1, source_target_pairs={{0,4},{1,5},{2,6},{3,7},{4,0},{5,1},{6,2},{7,3},{8,12},{9,13},{10,... | collective-permute-start | bytes 98312 | tf_op jit(solution)/shard_map/ppermute | solution.py:47
  41.1 2.4 %collective-permute-start.21 = (bf16[2,64,128]{2,1,0:T(8,128)(2,1)S(1)}, bf16[2,64,128]{2,1,0:T(8,128)(2,1)S(1)}, u32[]{:S(2)}, u32[]{:S(2)}) collective-permute-start(bf16[2,64,128]{2,1,0:T(8,128)(2,1)S(1)} %get-tuple-element.47), channel_id=1, source_target_pairs={{0,6},{1,7},{2,4},{3,5},{4,2},{5,3},{6,0},{7,1},{8,14},{9,15},{10,... | collective-permute-start | bytes 98312 | tf_op jit(solution)/shard_map/ppermute | solution.py:47
  43.7 2.9 %collective-permute-start.17 = (bf16[336,128]{1,0:T(8,128)(2,1)S(1)}, bf16[336,128]{1,0:T(8,128)(2,1)S(1)}, u32[]{:S(2)}, u32[]{:S(2)}) collective-permute-start(bf16[336,128]{1,0:T(8,128)(2,1)S(1)} %halve.1), channel_id=1, source_target_pairs={{0,16},{1,17},{2,18},{3,19},{4,20},{5,21},{6,22},{7,23},{8,24},{9,... | collective-permute-start | bytes 258056 | tf_op jit(solution)/shard_map/ppermute | solution.py:47
  46.6 1.2 %collective-permute-done.22.refs_7_ = bf16[4,64,128]{2,1,0:T(8,128)(2,1)S(1)} collective-permute-done((bf16[4,64,128]{2,1,0:T(8,128)(2,1)S(1)}, bf16[4,64,128]{2,1,0:T(8,128)(2,1)S(1)}, u32[]{:S(2)}, u32[]{:S(2)}) %collective-permute-start.22) | collective-permute-done | bytes 65568 | tf_op jit(solution)/shard_map/ppermute | solution.py:47
  47.9 1.7 %collective-permute-done.17.refs_2_ = bf16[336,128]{1,0:T(8,128)(2,1)S(1)} collective-permute-done((bf16[336,128]{1,0:T(8,128)(2,1)S(1)}, bf16[336,128]{1,0:T(8,128)(2,1)S(1)}, u32[]{:S(2)}, u32[]{:S(2)}) %collective-permute-start.17) | collective-permute-done | bytes 86048 | tf_op jit(solution)/shard_map/ppermute | solution.py:47
  49.6 1.2 %unpack.1 = (bf16[2,1,64,384]{3,2,1,0:T(8,128)(2,1)}, f32[12,27,192]{2,1,0:T(8,128)}) custom-call(f32[288,192]{1,0:T(8,128)S(1)} %get-tuple-element.38.refs_6_.refs_0_, bf16[672,128]{1,0:T(8,128)(2,1)S(1)} %collective-permute-done.16.refs_1_, bf16[336,128]{1,0:T(8,128)(2,1)S(1)} %collective-permute-done.17.refs_2_, ...), custom_call_target="tpu_custom_call" | custom-call | bytes 1022976 | tf_op jit(solution)/shard_map/unpack/pallas_call | solution.py:444
  (42 shorter events, 1.1 us)
Async XLA Ops:
  0.6 0.9 %copy-start.4 = (bf16[2,1,64,384]{3,2,1,0:T(8,128)(2,1)S(1)}, bf16[2,1,64,384]{3,2,1,0:T(8,128)(2,1)}, u32[]{:S(2)}) copy-start(bf16[2,1,64,384]{3,2,1,0:T(8,128)(2,1)} %param.5) | copy-start | bytes 294916
  1.5 4.8 %copy-start.2 = (bf16[12,27,192]{2,1,0:T(8,128)(2,1)S(1)}, bf16[12,27,192]{2,1,0:T(8,128)(2,1)}, u32[]{:S(2)}) copy-start(bf16[12,27,192]{2,1,0:T(8,128)(2,1)} %refs_0_.1) | copy-start | bytes 373252
  1.8 7.2 %collective-permute-start.7 = (bf16[2,64,128]{2,1,0:T(8,128)(2,1)S(1)}, bf16[2,64,128]{2,1,0:T(8,128)(2,1)S(1)}, u32[]{:S(2)}, u32[]{:S(2)}) collective-permute-start(bf16[2,64,128]{2,1,0:T(8,128)(2,1)S(1)} %get-tuple-element.26), channel_id=1, source_target_pairs={{0,2},{1,3},{2,0},{3,1},{4,6},{5,7},{6,4},{7,5},{8,10},{9,11},{10,... | collective-permute-start | bytes 98312 | tf_op jit(solution)/shard_map/ppermute | solution.py:47
  4.8 4.2 %collective-permute-start.8 = (bf16[2,64,128]{2,1,0:T(8,128)(2,1)S(1)}, bf16[2,64,128]{2,1,0:T(8,128)(2,1)S(1)}, u32[]{:S(2)}, u32[]{:S(2)}) collective-permute-start(bf16[2,64,128]{2,1,0:T(8,128)(2,1)S(1)} %get-tuple-element.27), channel_id=1, source_target_pairs={{0,4},{1,5},{2,6},{3,7},{4,0},{5,1},{6,2},{7,3},{8,12},{9,13},{10,... | collective-permute-start | bytes 98312 | tf_op jit(solution)/shard_map/ppermute | solution.py:47
  6.3 4.8 %copy-start.3 = (bf16[2,2,128,192]{2,3,1,0:T(8,128)(2,1)S(1)}, bf16[2,2,128,192]{2,3,1,0:T(8,128)(2,1)}, u32[]{:S(2)}) copy-start(bf16[2,2,128,192]{2,3,1,0:T(8,128)(2,1)} %param.9) | copy-start | bytes 589828
  6.3 4.8 %collective-permute-start.9 = (bf16[2,64,128]{2,1,0:T(8,128)(2,1)S(1)}, bf16[2,64,128]{2,1,0:T(8,128)(2,1)S(1)}, u32[]{:S(2)}, u32[]{:S(2)}) collective-permute-start(bf16[2,64,128]{2,1,0:T(8,128)(2,1)S(1)} %get-tuple-element.28), channel_id=1, source_target_pairs={{0,6},{1,7},{2,4},{3,5},{4,2},{5,3},{6,0},{7,1},{8,14},{9,15},{10,... | collective-permute-start | bytes 98312 | tf_op jit(solution)/shard_map/ppermute | solution.py:47
  6.9 7.8 %collective-permute-start.12 = (bf16[336,128]{1,0:T(8,128)(2,1)S(1)}, bf16[336,128]{1,0:T(8,128)(2,1)S(1)}, u32[]{:S(2)}, u32[]{:S(2)}) collective-permute-start(bf16[336,128]{1,0:T(8,128)(2,1)S(1)} %pack_weights.1.refs_0_), channel_id=1, source_target_pairs={{0,8},{1,9},{2,10},{3,11},{4,12},{5,13},{6,14},{7,15},{8,0},{9,1},... | collective-permute-start | bytes 258056 | tf_op jit(solution)/shard_map/ppermute | solution.py:47
  11.2 6.3 %collective-permute-start.10 = (bf16[4,64,128]{2,1,0:T(8,128)(2,1)S(1)}, bf16[4,64,128]{2,1,0:T(8,128)(2,1)S(1)}, u32[]{:S(2)}, u32[]{:S(2)}) collective-permute-start(bf16[4,64,128]{2,1,0:T(8,128)(2,1)S(1)} %cross_acts.1), channel_id=1, source_target_pairs={{0,1},{1,0},{2,3},{3,2},{4,5},{5,4},{6,7},{7,6},{8,9},{9,8},{10,11... | collective-permute-start | bytes 196616 | tf_op jit(solution)/shard_map/ppermute | solution.py:47
  11.2 10.7 %collective-permute-start.2 = (bf16[768,128]{1,0:T(8,128)(2,1)S(1)}, bf16[768,128]{1,0:T(8,128)(2,1)S(1)}, u32[]{:S(2)}, u32[]{:S(2)}) collective-permute-start(bf16[768,128]{1,0:T(8,128)(2,1)S(1)} %bitcast.4), channel_id=1, source_target_pairs={{0,6},{1,7},{2,4},{3,5},{4,2},{5,3},{6,0},{7,1},{8,14},{9,15},{10,... | collective-permute-start | bytes 589832 | tf_op jit(solution)/shard_map/ppermute | solution.py:47
  11.7 12.6 %collective-permute-start.1 = (bf16[768,128]{1,0:T(8,128)(2,1)S(1)}, bf16[768,128]{1,0:T(8,128)(2,1)S(1)}, u32[]{:S(2)}, u32[]{:S(2)}) collective-permute-start(bf16[768,128]{1,0:T(8,128)(2,1)S(1)} %bitcast.5), channel_id=1, source_target_pairs={{0,4},{1,5},{2,6},{3,7},{4,0},{5,1},{6,2},{7,3},{8,12},{9,13},{10,... | collective-permute-start | bytes 589832 | tf_op jit(solution)/shard_map/ppermute | solution.py:47
  13.2 11.3 %collective-permute-start = (bf16[768,128]{1,0:T(8,128)(2,1)S(1)}, bf16[768,128]{1,0:T(8,128)(2,1)S(1)}, u32[]{:S(2)}, u32[]{:S(2)}) collective-permute-start(bf16[768,128]{1,0:T(8,128)(2,1)S(1)} %bitcast.6), channel_id=1, source_target_pairs={{0,2},{1,3},{2,0},{3,1},{4,6},{5,7},{6,4},{7,5},{8,10},{9,11},{10,... | collective-permute-start | bytes 589832 | tf_op jit(solution)/shard_map/ppermute | solution.py:47
  14.8 10.5 %collective-permute-start.13 = (bf16[672,128]{1,0:T(8,128)(2,1)S(1)}, bf16[672,128]{1,0:T(8,128)(2,1)S(1)}, u32[]{:S(2)}, u32[]{:S(2)}) collective-permute-start(bf16[672,128]{1,0:T(8,128)(2,1)S(1)} %join_kernel_rows.1), channel_id=1, source_target_pairs={{0,16},{1,17},{2,18},{3,19},{4,20},{5,21},{6,22},{7,23},{8,24},{9,... | collective-permute-start | bytes 516104 | tf_op jit(solution)/shard_map/ppermute | solution.py:47
  17.5 4.3 %collective-permute-start.11 = (bf16[176,128]{1,0:T(8,128)(2,1)S(1)}, bf16[176,128]{1,0:T(8,128)(2,1)S(1)}, u32[]{:S(2)}, u32[]{:S(2)}) collective-permute-start(bf16[176,128]{1,0:T(8,128)(2,1)S(1)} %get-tuple-element.31), channel_id=1, source_target_pairs={{0,8},{1,9},{2,10},{3,11},{4,12},{5,13},{6,14},{7,15},{8,0},{9,1},... | collective-permute-start | bytes 135176 | tf_op jit(solution)/shard_map/ppermute | solution.py:47
  21.8 5.2 %collective-permute-start.3 = (bf16[768,128]{1,0:T(8,128)(2,1)S(1)}, bf16[768,128]{1,0:T(8,128)(2,1)S(1)}, u32[]{:S(2)}, u32[]{:S(2)}) collective-permute-start(bf16[768,128]{1,0:T(8,128)(2,1)S(1)} %bitcast.7), channel_id=1, source_target_pairs={{0,1},{1,0},{2,3},{3,2},{4,5},{5,4},{6,7},{7,6},{8,9},{9,8},{10,11... | collective-permute-start | bytes 589832 | tf_op jit(solution)/shard_map/ppermute | solution.py:47
  21.9 6.5 %collective-permute-start.14 = (bf16[112,128]{1,0:T(8,128)(2,1)S(1)}, bf16[112,128]{1,0:T(8,128)(2,1)S(1)}, u32[]{:S(2)}, u32[]{:S(2)}) collective-permute-start(bf16[112,128]{1,0:T(8,128)(2,1)S(1)} %get-tuple-element.33), channel_id=1, source_target_pairs={{0,16},{1,17},{2,18},{3,19},{4,20},{5,21},{6,22},{7,23},{8,24},{9,... | collective-permute-start | bytes 86024 | tf_op jit(solution)/shard_map/ppermute | solution.py:47
  24.3 2.8 %collective-permute-start.6 = (bf16[768,128]{1,0:T(8,128)(2,1)S(1)}, bf16[768,128]{1,0:T(8,128)(2,1)S(1)}, u32[]{:S(2)}, u32[]{:S(2)}) collective-permute-start(bf16[768,128]{1,0:T(8,128)(2,1)S(1)} %collective-permute-done.2.refs_3_), channel_id=1, source_target_pairs={{0,1},{1,0},{2,3},{3,2},{4,5},{5,4},{6,7},{7,6},{8,9},{9,8},{10,11... | collective-permute-start | bytes 589832 | tf_op jit(solution)/shard_map/ppermute | solution.py:47
  24.5 2.5 %collective-permute-start.5 = (bf16[768,128]{1,0:T(8,128)(2,1)S(1)}, bf16[768,128]{1,0:T(8,128)(2,1)S(1)}, u32[]{:S(2)}, u32[]{:S(2)}) collective-permute-start(bf16[768,128]{1,0:T(8,128)(2,1)S(1)} %collective-permute-done.1.refs_2_), channel_id=1, source_target_pairs={{0,1},{1,0},{2,3},{3,2},{4,5},{5,4},{6,7},{7,6},{8,9},{9,8},{10,11... | collective-permute-start | bytes 589832 | tf_op jit(solution)/shard_map/ppermute | solution.py:47
  25.3 1.8 %collective-permute-start.4 = (bf16[768,128]{1,0:T(8,128)(2,1)S(1)}, bf16[768,128]{1,0:T(8,128)(2,1)S(1)}, u32[]{:S(2)}, u32[]{:S(2)}) collective-permute-start(bf16[768,128]{1,0:T(8,128)(2,1)S(1)} %collective-permute-done.refs_1_), channel_id=1, source_target_pairs={{0,1},{1,0},{2,3},{3,2},{4,5},{5,4},{6,7},{7,6},{8,9},{9,8},{10,11... | collective-permute-start | bytes 589832 | tf_op jit(solution)/shard_map/ppermute | solution.py:47
  27.0 1.3 %copy-start = (f32[384]{0:T(512)S(1)}, f32[384]{0:T(512)}, u32[]{:S(2)}) copy-start(f32[384]{0:T(512)} %refs_2_.1) | copy-start | bytes 4612
  27.0 1.3 %copy-start.1 = (f32[384]{0:T(512)S(1)}, f32[384]{0:T(512)}, u32[]{:S(2)}) copy-start(f32[384]{0:T(512)} %refs_3_.1) | copy-start | bytes 4612
  29.5 4.1 %collective-permute-start.15 = (bf16[176,128]{1,0:T(8,128)(2,1)S(1)}, bf16[176,128]{1,0:T(8,128)(2,1)S(1)}, u32[]{:S(2)}, u32[]{:S(2)}) collective-permute-start(bf16[176,128]{1,0:T(8,128)(2,1)S(1)} %get-tuple-element.36), channel_id=1, source_target_pairs={{0,8},{1,9},{2,10},{3,11},{4,12},{5,13},{6,14},{7,15},{8,0},{9,1},... | collective-permute-start | bytes 135176 | tf_op jit(solution)/shard_map/ppermute | solution.py:47
  33.7 9.9 %collective-permute-start.16 = (bf16[672,128]{1,0:T(8,128)(2,1)S(1)}, bf16[672,128]{1,0:T(8,128)(2,1)S(1)}, u32[]{:S(2)}, u32[]{:S(2)}) collective-permute-start(bf16[672,128]{1,0:T(8,128)(2,1)S(1)} %pass_on.1), channel_id=1, source_target_pairs={{0,8},{1,9},{2,10},{3,11},{4,12},{5,13},{6,14},{7,15},{8,0},{9,1},... | collective-permute-start | bytes 516104 | tf_op jit(solution)/shard_map/ppermute | solution.py:47
  34.5 5.3 %collective-permute-start.18 = (bf16[112,128]{1,0:T(8,128)(2,1)S(1)}, bf16[112,128]{1,0:T(8,128)(2,1)S(1)}, u32[]{:S(2)}, u32[]{:S(2)}) collective-permute-start(bf16[112,128]{1,0:T(8,128)(2,1)S(1)} %get-tuple-element.37.refs_9_.refs_1_), channel_id=1, source_target_pairs={{0,16},{1,17},{2,18},{3,19},{4,20},{5,21},{6,22},{7,23},{8,24},{9,... | collective-permute-start | bytes 86024 | tf_op jit(solution)/shard_map/ppermute | solution.py:47
  40.0 6.6 %collective-permute-start.19 = (bf16[2,64,128]{2,1,0:T(8,128)(2,1)S(1)}, bf16[2,64,128]{2,1,0:T(8,128)(2,1)S(1)}, u32[]{:S(2)}, u32[]{:S(2)}) collective-permute-start(bf16[2,64,128]{2,1,0:T(8,128)(2,1)S(1)} %get-tuple-element.45), channel_id=1, source_target_pairs={{0,2},{1,3},{2,0},{3,1},{4,6},{5,7},{6,4},{7,5},{8,10},{9,11},{10,... | collective-permute-start | bytes 98312 | tf_op jit(solution)/shard_map/ppermute | solution.py:47
  40.6 6.0 %collective-permute-start.20 = (bf16[2,64,128]{2,1,0:T(8,128)(2,1)S(1)}, bf16[2,64,128]{2,1,0:T(8,128)(2,1)S(1)}, u32[]{:S(2)}, u32[]{:S(2)}) collective-permute-start(bf16[2,64,128]{2,1,0:T(8,128)(2,1)S(1)} %get-tuple-element.46), channel_id=1, source_target_pairs={{0,4},{1,5},{2,6},{3,7},{4,0},{5,1},{6,2},{7,3},{8,12},{9,13},{10,... | collective-permute-start | bytes 98312 | tf_op jit(solution)/shard_map/ppermute | solution.py:47
  41.1 5.5 %collective-permute-start.21 = (bf16[2,64,128]{2,1,0:T(8,128)(2,1)S(1)}, bf16[2,64,128]{2,1,0:T(8,128)(2,1)S(1)}, u32[]{:S(2)}, u32[]{:S(2)}) collective-permute-start(bf16[2,64,128]{2,1,0:T(8,128)(2,1)S(1)} %get-tuple-element.47), channel_id=1, source_target_pairs={{0,6},{1,7},{2,4},{3,5},{4,2},{5,3},{6,0},{7,1},{8,14},{9,15},{10,... | collective-permute-start | bytes 98312 | tf_op jit(solution)/shard_map/ppermute | solution.py:47
  43.7 5.9 %collective-permute-start.17 = (bf16[336,128]{1,0:T(8,128)(2,1)S(1)}, bf16[336,128]{1,0:T(8,128)(2,1)S(1)}, u32[]{:S(2)}, u32[]{:S(2)}) collective-permute-start(bf16[336,128]{1,0:T(8,128)(2,1)S(1)} %halve.1), channel_id=1, source_target_pairs={{0,16},{1,17},{2,18},{3,19},{4,20},{5,21},{6,22},{7,23},{8,24},{9,... | collective-permute-start | bytes 258056 | tf_op jit(solution)/shard_map/ppermute | solution.py:47
  46.6 1.3 %collective-permute-start.22 = (bf16[4,64,128]{2,1,0:T(8,128)(2,1)S(1)}, bf16[4,64,128]{2,1,0:T(8,128)(2,1)S(1)}, u32[]{:S(2)}, u32[]{:S(2)}) collective-permute-start(bf16[4,64,128]{2,1,0:T(8,128)(2,1)S(1)} %cross_grads.1), channel_id=1, source_target_pairs={{0,1},{1,0},{2,3},{3,2},{4,5},{5,4},{6,7},{7,6},{8,9},{9,8},{10,11... | collective-permute-start | bytes 196616 | tf_op jit(solution)/shard_map/ppermute | solution.py:47

commit v4 on v3

--- a/solution.py
+++ b/solution.py
@@ -313,7 +313,7 @@
     grad_ref[...] = grad
     sums = totals(g, jnp.sum(grad, axis=0), jnp.sum(grad * normed_ref[...], axis=0))
     sums_ref[...] = sums
-    send_stats(g, send_ref, sums, z, grad_ref, 1)
+    send_stats(g, send_ref, sums, z, grad_ref, 2)
 
 
 def kernel_terms(g, first, direct, crossed, hidden_ref, acc, ups):
@@ -394,7 +394,7 @@
     first, second = spread(g, add_stats(sums_ref[...], received[1:]))
     first, second = first / g.count, second / g.count
     inv = inv_ref[...]
-    above, below = edges(g, z, received, 1)
+    above, below = edges(g, z, received, 2)
     for k, ref in enumerate(sends):
         for j in range(2):
             row = w ^ (2 * k + j)
@@ -552,7 +552,7 @@
         g,
         norm_grad_kernel,
         "norm_grad",
-        [rows_shape, hidden_shape, ((g.rb, g.cells), F32), stats_shape, rows_shape, sums_shape(2)],
+        [rows_shape, hidden_shape, ((g.rb, g.cells), F32), stats_shape, rows_shape, sums_shape(4)],
         [rows, stats, gamma, beta] + fields + received,
         [pltpu.VMEM(*rows_shape), pltpu.VMEM((g.outer, g.gp, g.cells), BF16)],
     )
@@ -571,8 +571,8 @@
         scratch,
         flops // 2,
     )
-    sums, send, received = over_z("add_sums", sums, send, 1, [terms])
-    terms = [swap(pass_on(g, terms, [send]), g.inner)]
+    sums, send, received = over_z("add_sums", sums, send, 2, [terms])
+    terms = [swap(terms, g.inner)]
     own, *kept = call(
         g,
         kept_terms_kernel,

time: 50.9 us -> 51 us (level)
  waiting for transfers between devices: 9.6 us -> 10.5 us
  starting transfers between devices: 29 us -> 28.3 us
    ppermute x23, waiting for transfers between devices: 9.6 us -> 10.5 us  [swap(): return lax.ppermute(value, 'tile', [(i, i ^ mask) for i in range(count)])]
    ppermute x23, starting transfers between devices: 29 us -> 28.3 us  [swap(): return lax.ppermute(value, 'tile', [(i, i ^ mask) for i in range(count)])]
    pallas_call x18 -> x17, Pallas kernels: 10.4 us -> 10.4 us  [call(): pl.pallas_call(lambda *refs: kernel(g, *refs[:count], *refs[rest:]), out_...]
  transfers between devices with their start and end apart: 23 -> 23, of which waited for: 6 -> 7; matrix products, arithmetic and copies ran while one was open for 0% -> 0% of each run, Pallas kernels for 15% -> 15%
where the time goes in v4:
time: 51 us; the launch traced here: 50.8 us
  starting transfers between devices  28.3 us (55%)
  waiting for transfers between devices  10.5 us (21%)
  Pallas kernels  10.4 us (20%)
  local copies, waits for them, and re-layouts  0.91 us (2%)
  between operations  0.83 us (2%)
    ppermute x23, starting transfers between devices, swap(): return lax.ppermute(value, 'tile', [(i, i ^ mask) for i in range(count)])  28.3 us
    ppermute x23, waiting for transfers between devices, swap(): return lax.ppermute(value, 'tile', [(i, i ^ mask) for i in range(count)])  10.5 us
    pallas_call x17, Pallas kernels, call(): pl.pallas_call(lambda *refs: kernel(g, *refs[:count], *refs[rest:]), out_...  10.4 us
  transfers between devices with their start and end apart: 23, of which 7 were waited for; matrix products, arithmetic and copies ran while one was open for 0% of the time, Pallas kernels for 15%

profile of v4, /device:TPU:0, one launch (start us, length us, event | category | flops | bytes accessed | tf_op | source)
XLA Modules:
  0.0 50.8 jit_solution(2206900109040983670)
XLA Ops:
  0.6 0.9 %copy-done.4 = bf16[2,1,64,384]{3,2,1,0:T(8,128)(2,1)S(1)} copy-done((bf16[2,1,64,384]{3,2,1,0:T(8,128)(2,1)S(1)}, bf16[2,1,64,384]{3,2,1,0:T(8,128)(2,1)}, u32[]{:S(2)}) %copy-start.4) | copy-done | bytes 98328
  1.8 3.0 %collective-permute-start.7 = (bf16[2,64,128]{2,1,0:T(8,128)(2,1)S(1)}, bf16[2,64,128]{2,1,0:T(8,128)(2,1)S(1)}, u32[]{:S(2)}, u32[]{:S(2)}) collective-permute-start(bf16[2,64,128]{2,1,0:T(8,128)(2,1)S(1)} %get-tuple-element.26), channel_id=1, source_target_pairs={{0,2},{1,3},{2,0},{3,1},{4,6},{5,7},{6,4},{7,5},{8,10},{9,11},{10,... | collective-permute-start | bytes 98312 | tf_op jit(solution)/shard_map/ppermute | solution.py:47
  4.8 1.5 %collective-permute-start.8 = (bf16[2,64,128]{2,1,0:T(8,128)(2,1)S(1)}, bf16[2,64,128]{2,1,0:T(8,128)(2,1)S(1)}, u32[]{:S(2)}, u32[]{:S(2)}) collective-permute-start(bf16[2,64,128]{2,1,0:T(8,128)(2,1)S(1)} %get-tuple-element.27), channel_id=1, source_target_pairs={{0,4},{1,5},{2,6},{3,7},{4,0},{5,1},{6,2},{7,3},{8,12},{9,13},{10,... | collective-permute-start | bytes 98312 | tf_op jit(solution)/shard_map/ppermute | solution.py:47
  6.4 0.6 %pack_weights.1.refs_0_ = bf16[336,128]{1,0:T(8,128)(2,1)S(1)} custom-call(bf16[12,27,192]{2,1,0:T(8,128)(2,1)S(1)} %copy-done.2), custom_call_target="tpu_custom_call" | custom-call | flops 6000000000 | bytes 210432 | tf_op jit(solution)/shard_map/pack_weights/pallas_call | solution.py:444
  6.9 2.1 %collective-permute-start.12 = (bf16[336,128]{1,0:T(8,128)(2,1)S(1)}, bf16[336,128]{1,0:T(8,128)(2,1)S(1)}, u32[]{:S(2)}, u32[]{:S(2)}) collective-permute-start(bf16[336,128]{1,0:T(8,128)(2,1)S(1)} %pack_weights.1.refs_0_), channel_id=1, source_target_pairs={{0,8},{1,9},{2,10},{3,11},{4,12},{5,13},{6,14},{7,15},{8,0},{9,1},... | collective-permute-start | bytes 258056 | tf_op jit(solution)/shard_map/ppermute | solution.py:47
  9.0 2.1 %collective-permute-done.9.refs_3_ = bf16[2,64,128]{2,1,0:T(8,128)(2,1)S(1)} collective-permute-done((bf16[2,64,128]{2,1,0:T(8,128)(2,1)S(1)}, bf16[2,64,128]{2,1,0:T(8,128)(2,1)S(1)}, u32[]{:S(2)}, u32[]{:S(2)}) %collective-permute-start.9) | collective-permute-done | bytes 32800 | tf_op jit(solution)/shard_map/ppermute | solution.py:47
  11.2 0.5 collective-permute-start.2
  11.7 1.6 %collective-permute-start.1 = (bf16[768,128]{1,0:T(8,128)(2,1)S(1)}, bf16[768,128]{1,0:T(8,128)(2,1)S(1)}, u32[]{:S(2)}, u32[]{:S(2)}) collective-permute-start(bf16[768,128]{1,0:T(8,128)(2,1)S(1)} %bitcast.5), channel_id=1, source_target_pairs={{0,4},{1,5},{2,6},{3,7},{4,0},{5,1},{6,2},{7,3},{8,12},{9,13},{10,... | collective-permute-start | bytes 589832 | tf_op jit(solution)/shard_map/ppermute | solution.py:47
  13.2 1.5 %collective-permute-start = (bf16[768,128]{1,0:T(8,128)(2,1)S(1)}, bf16[768,128]{1,0:T(8,128)(2,1)S(1)}, u32[]{:S(2)}, u32[]{:S(2)}) collective-permute-start(bf16[768,128]{1,0:T(8,128)(2,1)S(1)} %bitcast.6), channel_id=1, source_target_pairs={{0,2},{1,3},{2,0},{3,1},{4,6},{5,7},{6,4},{7,5},{8,10},{9,11},{10,... | collective-permute-start | bytes 589832 | tf_op jit(solution)/shard_map/ppermute | solution.py:47
  14.8 2.7 %collective-permute-start.13 = (bf16[672,128]{1,0:T(8,128)(2,1)S(1)}, bf16[672,128]{1,0:T(8,128)(2,1)S(1)}, u32[]{:S(2)}, u32[]{:S(2)}) collective-permute-start(bf16[672,128]{1,0:T(8,128)(2,1)S(1)} %join_kernel_rows.1), channel_id=1, source_target_pairs={{0,16},{1,17},{2,18},{3,19},{4,20},{5,21},{6,22},{7,23},{8,24},{9,... | collective-permute-start | bytes 516104 | tf_op jit(solution)/shard_map/ppermute | solution.py:47
  17.5 1.6 %collective-permute-start.11 = (bf16[176,128]{1,0:T(8,128)(2,1)S(1)}, bf16[176,128]{1,0:T(8,128)(2,1)S(1)}, u32[]{:S(2)}, u32[]{:S(2)}) collective-permute-start(bf16[176,128]{1,0:T(8,128)(2,1)S(1)} %get-tuple-element.31), channel_id=1, source_target_pairs={{0,8},{1,9},{2,10},{3,11},{4,12},{5,13},{6,14},{7,15},{8,0},{9,1},... | collective-permute-start | bytes 135176 | tf_op jit(solution)/shard_map/ppermute | solution.py:47
  19.1 2.7 %collective-permute-done.11.refs_1_.refs_6_ = bf16[176,128]{1,0:T(8,128)(2,1)S(1)} collective-permute-done((bf16[176,128]{1,0:T(8,128)(2,1)S(1)}, bf16[176,128]{1,0:T(8,128)(2,1)S(1)}, u32[]{:S(2)}, u32[]{:S(2)}) %collective-permute-start.11) | collective-permute-done | bytes 45088 | tf_op jit(solution)/shard_map/ppermute | solution.py:47
  21.9 2.4 %collective-permute-start.14 = (bf16[112,128]{1,0:T(8,128)(2,1)S(1)}, bf16[112,128]{1,0:T(8,128)(2,1)S(1)}, u32[]{:S(2)}, u32[]{:S(2)}) collective-permute-start(bf16[112,128]{1,0:T(8,128)(2,1)S(1)} %get-tuple-element.33), channel_id=1, source_target_pairs={{0,16},{1,17},{2,18},{3,19},{4,20},{5,21},{6,22},{7,23},{8,24},{9,... | collective-permute-start | bytes 86024 | tf_op jit(solution)/shard_map/ppermute | solution.py:47
  24.8 0.5 collective-permute-done.13.refs_2_
  25.3 0.4 kernel_rows.1.refs_4_
  25.7 1.3 %field_grad.2.refs_4_ = f32[10,64,768]{2,1,0:T(8,128)S(1)} custom-call(bf16[768,128]{1,0:T(8,128)(2,1)S(1)} %bitcast.8, bf16[768,128]{1,0:T(8,128)(2,1)S(1)} %collective-permute-done.refs_1_, bf16[768,128]{1,0:T(8,128)(2,1)S(1)} %collective-permute-done.1.refs_2_, bf16[768,128]{1,0:T(8,128)(2,1)S(1)} %collective-permute-done.2.refs_3_, ...), custom_call_target="tpu_custom_call" | custom-call | flops 1207959552 | bytes 3342336 | tf_op jit(solution)/shard_map/field_grad/pallas_call | solution.py:444
  27.1 1.2 %field_grad.3.refs_5_ = f32[10,64,768]{2,1,0:T(8,128)S(1)} custom-call(bf16[768,128]{1,0:T(8,128)(2,1)S(1)} %collective-permute-done.3.refs_0_.refs_4_, bf16[768,128]{1,0:T(8,128)(2,1)S(1)} %collective-permute-done.4.refs_1_.refs_5_, bf16[768,128]{1,0:T(8,128)(2,1)S(1)} %collective-permute-done.5.refs_2_.refs_6_, ...), custom_call_target="tpu_custom_call" | custom-call | flops 1207959552 | bytes 3342336 | tf_op jit(solution)/shard_map/field_grad/pallas_call | solution.py:444
  28.4 1.1 %norm_grad.1 = (f32[10,64,128]{2,1,0:T(8,128)S(1)}, bf16[4,10,16,128]{3,2,1,0:T(8,128)(2,1)S(1)}, f32[64,128]{1,0:T(8,128)S(1)}, f32[16,128]{1,0:T(8,128)S(1)}, ...) custom-call(bf16[8,64,128]{2,1,0:T(8,128)(2,1)S(1)} %get-tuple-element.29.refs_0_, ...), custom_call_target="tpu_custom_call" | custom-call | bytes 5086208 | tf_op jit(solution)/shard_map/norm_grad/pallas_call | solution.py:444
  29.5 0.9 %collective-permute-start.15 = (bf16[304,128]{1,0:T(8,128)(2,1)S(1)}, bf16[304,128]{1,0:T(8,128)(2,1)S(1)}, u32[]{:S(2)}, u32[]{:S(2)}) collective-permute-start(bf16[304,128]{1,0:T(8,128)(2,1)S(1)} %get-tuple-element.36), channel_id=1, source_target_pairs={{0,8},{1,9},{2,10},{3,11},{4,12},{5,13},{6,14},{7,15},{8,0},{9,1},... | collective-permute-start | bytes 233480 | tf_op jit(solution)/shard_map/ppermute | solution.py:47
  30.4 1.9 %sent_terms.1.refs_2_ = bf16[672,128]{1,0:T(8,128)(2,1)S(1)} custom-call(bf16[768,128]{1,0:T(8,128)(2,1)S(1)} %bitcast.9, bf16[768,128]{1,0:T(8,128)(2,1)S(1)} %collective-permute-done.refs_1_, bf16[768,128]{1,0:T(8,128)(2,1)S(1)} %collective-permute-done.1.refs_2_, bf16[768,128]{1,0:T(8,128)(2,1)S(1)} %collective-permute-done.2.refs_3_, ...), custom_call_target="tpu_custom_call" | custom-call | flops 1207959552 | bytes 1908736 | tf_op jit(solution)/shard_map/sent_terms/pallas_call | solution.py:444
  32.3 1.3 %collective-permute-start.16 = (bf16[672,128]{1,0:T(8,128)(2,1)S(1)}, bf16[672,128]{1,0:T(8,128)(2,1)S(1)}, u32[]{:S(2)}, u32[]{:S(2)}) collective-permute-start(bf16[672,128]{1,0:T(8,128)(2,1)S(1)} %sent_terms.1.refs_2_), channel_id=1, source_target_pairs={{0,8},{1,9},{2,10},{3,11},{4,12},{5,13},{6,14},{7,15},{8,0},{9,1},... | collective-permute-start | bytes 516104 | tf_op jit(solution)/shard_map/ppermute | solution.py:47
  33.6 0.7 %collective-permute-done.15.refs_1_.refs_4_ = bf16[304,128]{1,0:T(8,128)(2,1)S(1)} collective-permute-done((bf16[304,128]{1,0:T(8,128)(2,1)S(1)}, bf16[304,128]{1,0:T(8,128)(2,1)S(1)}, u32[]{:S(2)}, u32[]{:S(2)}) %collective-permute-start.15) | collective-permute-done | bytes 77856 | tf_op jit(solution)/shard_map/ppermute | solution.py:47
  34.3 2.5 %collective-permute-start.18 = (bf16[176,128]{1,0:T(8,128)(2,1)S(1)}, bf16[176,128]{1,0:T(8,128)(2,1)S(1)}, u32[]{:S(2)}, u32[]{:S(2)}) collective-permute-start(bf16[176,128]{1,0:T(8,128)(2,1)S(1)} %get-tuple-element.37.refs_9_), channel_id=1, source_target_pairs={{0,16},{1,17},{2,18},{3,19},{4,20},{5,21},{6,22},{7,23},{8,24},{9,... | collective-permute-start | bytes 135176 | tf_op jit(solution)/shard_map/ppermute | solution.py:47
  36.8 1.9 %kept_terms.1 = (f32[288,192]{1,0:T(8,128)S(1)}, f32[1,224,192]{2,1,0:T(8,128)S(1)}) custom-call(bf16[768,128]{1,0:T(8,128)(2,1)S(1)} %bitcast.10, bf16[768,128]{1,0:T(8,128)(2,1)S(1)} %collective-permute-done.refs_1_, bf16[768,128]{1,0:T(8,128)(2,1)S(1)} %collective-permute-done.1.refs_2_, bf16[768,128]{1,0:T(8,128)(2,1)S(1)} %collective-permute-done.2.refs_3_, ...), custom_call_target="tpu_custom_call" | custom-call | flops 1207959552 | bytes 2129920 | tf_op jit(solution)/shard_map/kept_terms/pallas_call | solution.py:444
  38.7 0.7 %collective-permute-done.18.refs_5_ = bf16[176,128]{1,0:T(8,128)(2,1)S(1)} collective-permute-done((bf16[176,128]{1,0:T(8,128)(2,1)S(1)}, bf16[176,128]{1,0:T(8,128)(2,1)S(1)}, u32[]{:S(2)}, u32[]{:S(2)}) %collective-permute-start.18) | collective-permute-done | bytes 45088 | tf_op jit(solution)/shard_map/ppermute | solution.py:47
  39.6 0.6 %collective-permute-start.19 = (bf16[2,64,128]{2,1,0:T(8,128)(2,1)S(1)}, bf16[2,64,128]{2,1,0:T(8,128)(2,1)S(1)}, u32[]{:S(2)}, u32[]{:S(2)}) collective-permute-start(bf16[2,64,128]{2,1,0:T(8,128)(2,1)S(1)} %get-tuple-element.45), channel_id=1, source_target_pairs={{0,2},{1,3},{2,0},{3,1},{4,6},{5,7},{6,4},{7,5},{8,10},{9,11},{10,... | collective-permute-start | bytes 98312 | tf_op jit(solution)/shard_map/ppermute | solution.py:47
  40.2 0.5 collective-permute-start.20
  40.7 2.5 %collective-permute-start.21 = (bf16[2,64,128]{2,1,0:T(8,128)(2,1)S(1)}, bf16[2,64,128]{2,1,0:T(8,128)(2,1)S(1)}, u32[]{:S(2)}, u32[]{:S(2)}) collective-permute-start(bf16[2,64,128]{2,1,0:T(8,128)(2,1)S(1)} %get-tuple-element.47), channel_id=1, source_target_pairs={{0,6},{1,7},{2,4},{3,5},{4,2},{5,3},{6,0},{7,1},{8,14},{9,15},{10,... | collective-permute-start | bytes 98312 | tf_op jit(solution)/shard_map/ppermute | solution.py:47
  43.3 2.6 %collective-permute-start.17 = (bf16[336,128]{1,0:T(8,128)(2,1)S(1)}, bf16[336,128]{1,0:T(8,128)(2,1)S(1)}, u32[]{:S(2)}, u32[]{:S(2)}) collective-permute-start(bf16[336,128]{1,0:T(8,128)(2,1)S(1)} %halve.1), channel_id=1, source_target_pairs={{0,16},{1,17},{2,18},{3,19},{4,20},{5,21},{6,22},{7,23},{8,24},{9,... | collective-permute-start | bytes 258056 | tf_op jit(solution)/shard_map/ppermute | solution.py:47
  46.0 1.2 %collective-permute-done.22.refs_7_ = bf16[4,64,128]{2,1,0:T(8,128)(2,1)S(1)} collective-permute-done((bf16[4,64,128]{2,1,0:T(8,128)(2,1)S(1)}, bf16[4,64,128]{2,1,0:T(8,128)(2,1)S(1)}, u32[]{:S(2)}, u32[]{:S(2)}) %collective-permute-start.22) | collective-permute-done | bytes 65568 | tf_op jit(solution)/shard_map/ppermute | solution.py:47
  47.2 2.4 %collective-permute-done.17.refs_2_ = bf16[336,128]{1,0:T(8,128)(2,1)S(1)} collective-permute-done((bf16[336,128]{1,0:T(8,128)(2,1)S(1)}, bf16[336,128]{1,0:T(8,128)(2,1)S(1)}, u32[]{:S(2)}, u32[]{:S(2)}) %collective-permute-start.17) | collective-permute-done | bytes 86048 | tf_op jit(solution)/shard_map/ppermute | solution.py:47
  49.7 1.2 %unpack.1 = (bf16[2,1,64,384]{3,2,1,0:T(8,128)(2,1)}, f32[12,27,192]{2,1,0:T(8,128)}) custom-call(f32[288,192]{1,0:T(8,128)S(1)} %get-tuple-element.38.refs_6_.refs_0_, bf16[672,128]{1,0:T(8,128)(2,1)S(1)} %collective-permute-done.16.refs_1_, bf16[336,128]{1,0:T(8,128)(2,1)S(1)} %collective-permute-done.17.refs_2_, ...), custom_call_target="tpu_custom_call" | custom-call | bytes 1022976 | tf_op jit(solution)/shard_map/unpack/pallas_call | solution.py:444
  (41 shorter events, 1.4 us)
Async XLA Ops:
  0.6 0.9 %copy-start.4 = (bf16[2,1,64,384]{3,2,1,0:T(8,128)(2,1)S(1)}, bf16[2,1,64,384]{3,2,1,0:T(8,128)(2,1)}, u32[]{:S(2)}) copy-start(bf16[2,1,64,384]{3,2,1,0:T(8,128)(2,1)} %param.5) | copy-start | bytes 294916
  1.5 4.8 %copy-start.2 = (bf16[12,27,192]{2,1,0:T(8,128)(2,1)S(1)}, bf16[12,27,192]{2,1,0:T(8,128)(2,1)}, u32[]{:S(2)}) copy-start(bf16[12,27,192]{2,1,0:T(8,128)(2,1)} %refs_0_.1) | copy-start | bytes 373252
  1.8 7.2 %collective-permute-start.7 = (bf16[2,64,128]{2,1,0:T(8,128)(2,1)S(1)}, bf16[2,64,128]{2,1,0:T(8,128)(2,1)S(1)}, u32[]{:S(2)}, u32[]{:S(2)}) collective-permute-start(bf16[2,64,128]{2,1,0:T(8,128)(2,1)S(1)} %get-tuple-element.26), channel_id=1, source_target_pairs={{0,2},{1,3},{2,0},{3,1},{4,6},{5,7},{6,4},{7,5},{8,10},{9,11},{10,... | collective-permute-start | bytes 98312 | tf_op jit(solution)/shard_map/ppermute | solution.py:47
  4.8 4.2 %collective-permute-start.8 = (bf16[2,64,128]{2,1,0:T(8,128)(2,1)S(1)}, bf16[2,64,128]{2,1,0:T(8,128)(2,1)S(1)}, u32[]{:S(2)}, u32[]{:S(2)}) collective-permute-start(bf16[2,64,128]{2,1,0:T(8,128)(2,1)S(1)} %get-tuple-element.27), channel_id=1, source_target_pairs={{0,4},{1,5},{2,6},{3,7},{4,0},{5,1},{6,2},{7,3},{8,12},{9,13},{10,... | collective-permute-start | bytes 98312 | tf_op jit(solution)/shard_map/ppermute | solution.py:47
  6.3 4.8 %copy-start.3 = (bf16[2,2,128,192]{2,3,1,0:T(8,128)(2,1)S(1)}, bf16[2,2,128,192]{2,3,1,0:T(8,128)(2,1)}, u32[]{:S(2)}) copy-start(bf16[2,2,128,192]{2,3,1,0:T(8,128)(2,1)} %param.9) | copy-start | bytes 589828
  6.3 4.8 %collective-permute-start.9 = (bf16[2,64,128]{2,1,0:T(8,128)(2,1)S(1)}, bf16[2,64,128]{2,1,0:T(8,128)(2,1)S(1)}, u32[]{:S(2)}, u32[]{:S(2)}) collective-permute-start(bf16[2,64,128]{2,1,0:T(8,128)(2,1)S(1)} %get-tuple-element.28), channel_id=1, source_target_pairs={{0,6},{1,7},{2,4},{3,5},{4,2},{5,3},{6,0},{7,1},{8,14},{9,15},{10,... | collective-permute-start | bytes 98312 | tf_op jit(solution)/shard_map/ppermute | solution.py:47
  6.9 7.8 %collective-permute-start.12 = (bf16[336,128]{1,0:T(8,128)(2,1)S(1)}, bf16[336,128]{1,0:T(8,128)(2,1)S(1)}, u32[]{:S(2)}, u32[]{:S(2)}) collective-permute-start(bf16[336,128]{1,0:T(8,128)(2,1)S(1)} %pack_weights.1.refs_0_), channel_id=1, source_target_pairs={{0,8},{1,9},{2,10},{3,11},{4,12},{5,13},{6,14},{7,15},{8,0},{9,1},... | collective-permute-start | bytes 258056 | tf_op jit(solution)/shard_map/ppermute | solution.py:47
  11.2 6.3 %collective-permute-start.10 = (bf16[4,64,128]{2,1,0:T(8,128)(2,1)S(1)}, bf16[4,64,128]{2,1,0:T(8,128)(2,1)S(1)}, u32[]{:S(2)}, u32[]{:S(2)}) collective-permute-start(bf16[4,64,128]{2,1,0:T(8,128)(2,1)S(1)} %cross_acts.1), channel_id=1, source_target_pairs={{0,1},{1,0},{2,3},{3,2},{4,5},{5,4},{6,7},{7,6},{8,9},{9,8},{10,11... | collective-permute-start | bytes 196616 | tf_op jit(solution)/shard_map/ppermute | solution.py:47
  11.2 10.7 %collective-permute-start.2 = (bf16[768,128]{1,0:T(8,128)(2,1)S(1)}, bf16[768,128]{1,0:T(8,128)(2,1)S(1)}, u32[]{:S(2)}, u32[]{:S(2)}) collective-permute-start(bf16[768,128]{1,0:T(8,128)(2,1)S(1)} %bitcast.4), channel_id=1, source_target_pairs={{0,6},{1,7},{2,4},{3,5},{4,2},{5,3},{6,0},{7,1},{8,14},{9,15},{10,... | collective-permute-start | bytes 589832 | tf_op jit(solution)/shard_map/ppermute | solution.py:47
  11.7 12.6 %collective-permute-start.1 = (bf16[768,128]{1,0:T(8,128)(2,1)S(1)}, bf16[768,128]{1,0:T(8,128)(2,1)S(1)}, u32[]{:S(2)}, u32[]{:S(2)}) collective-permute-start(bf16[768,128]{1,0:T(8,128)(2,1)S(1)} %bitcast.5), channel_id=1, source_target_pairs={{0,4},{1,5},{2,6},{3,7},{4,0},{5,1},{6,2},{7,3},{8,12},{9,13},{10,... | collective-permute-start | bytes 589832 | tf_op jit(solution)/shard_map/ppermute | solution.py:47
  13.2 11.3 %collective-permute-start = (bf16[768,128]{1,0:T(8,128)(2,1)S(1)}, bf16[768,128]{1,0:T(8,128)(2,1)S(1)}, u32[]{:S(2)}, u32[]{:S(2)}) collective-permute-start(bf16[768,128]{1,0:T(8,128)(2,1)S(1)} %bitcast.6), channel_id=1, source_target_pairs={{0,2},{1,3},{2,0},{3,1},{4,6},{5,7},{6,4},{7,5},{8,10},{9,11},{10,... | collective-permute-start | bytes 589832 | tf_op jit(solution)/shard_map/ppermute | solution.py:47
  14.8 10.5 %collective-permute-start.13 = (bf16[672,128]{1,0:T(8,128)(2,1)S(1)}, bf16[672,128]{1,0:T(8,128)(2,1)S(1)}, u32[]{:S(2)}, u32[]{:S(2)}) collective-permute-start(bf16[672,128]{1,0:T(8,128)(2,1)S(1)} %join_kernel_rows.1), channel_id=1, source_target_pairs={{0,16},{1,17},{2,18},{3,19},{4,20},{5,21},{6,22},{7,23},{8,24},{9,... | collective-permute-start | bytes 516104 | tf_op jit(solution)/shard_map/ppermute | solution.py:47
  17.5 4.3 %collective-permute-start.11 = (bf16[176,128]{1,0:T(8,128)(2,1)S(1)}, bf16[176,128]{1,0:T(8,128)(2,1)S(1)}, u32[]{:S(2)}, u32[]{:S(2)}) collective-permute-start(bf16[176,128]{1,0:T(8,128)(2,1)S(1)} %get-tuple-element.31), channel_id=1, source_target_pairs={{0,8},{1,9},{2,10},{3,11},{4,12},{5,13},{6,14},{7,15},{8,0},{9,1},... | collective-permute-start | bytes 135176 | tf_op jit(solution)/shard_map/ppermute | solution.py:47
  21.8 5.2 %collective-permute-start.3 = (bf16[768,128]{1,0:T(8,128)(2,1)S(1)}, bf16[768,128]{1,0:T(8,128)(2,1)S(1)}, u32[]{:S(2)}, u32[]{:S(2)}) collective-permute-start(bf16[768,128]{1,0:T(8,128)(2,1)S(1)} %bitcast.7), channel_id=1, source_target_pairs={{0,1},{1,0},{2,3},{3,2},{4,5},{5,4},{6,7},{7,6},{8,9},{9,8},{10,11... | collective-permute-start | bytes 589832 | tf_op jit(solution)/shard_map/ppermute | solution.py:47
  21.9 6.5 %collective-permute-start.14 = (bf16[112,128]{1,0:T(8,128)(2,1)S(1)}, bf16[112,128]{1,0:T(8,128)(2,1)S(1)}, u32[]{:S(2)}, u32[]{:S(2)}) collective-permute-start(bf16[112,128]{1,0:T(8,128)(2,1)S(1)} %get-tuple-element.33), channel_id=1, source_target_pairs={{0,16},{1,17},{2,18},{3,19},{4,20},{5,21},{6,22},{7,23},{8,24},{9,... | collective-permute-start | bytes 86024 | tf_op jit(solution)/shard_map/ppermute | solution.py:47
  24.3 2.8 %collective-permute-start.6 = (bf16[768,128]{1,0:T(8,128)(2,1)S(1)}, bf16[768,128]{1,0:T(8,128)(2,1)S(1)}, u32[]{:S(2)}, u32[]{:S(2)}) collective-permute-start(bf16[768,128]{1,0:T(8,128)(2,1)S(1)} %collective-permute-done.2.refs_3_), channel_id=1, source_target_pairs={{0,1},{1,0},{2,3},{3,2},{4,5},{5,4},{6,7},{7,6},{8,9},{9,8},{10,11... | collective-permute-start | bytes 589832 | tf_op jit(solution)/shard_map/ppermute | solution.py:47
  24.5 2.5 %collective-permute-start.5 = (bf16[768,128]{1,0:T(8,128)(2,1)S(1)}, bf16[768,128]{1,0:T(8,128)(2,1)S(1)}, u32[]{:S(2)}, u32[]{:S(2)}) collective-permute-start(bf16[768,128]{1,0:T(8,128)(2,1)S(1)} %collective-permute-done.1.refs_2_), channel_id=1, source_target_pairs={{0,1},{1,0},{2,3},{3,2},{4,5},{5,4},{6,7},{7,6},{8,9},{9,8},{10,11... | collective-permute-start | bytes 589832 | tf_op jit(solution)/shard_map/ppermute | solution.py:47
  25.3 1.8 %collective-permute-start.4 = (bf16[768,128]{1,0:T(8,128)(2,1)S(1)}, bf16[768,128]{1,0:T(8,128)(2,1)S(1)}, u32[]{:S(2)}, u32[]{:S(2)}) collective-permute-start(bf16[768,128]{1,0:T(8,128)(2,1)S(1)} %collective-permute-done.refs_1_), channel_id=1, source_target_pairs={{0,1},{1,0},{2,3},{3,2},{4,5},{5,4},{6,7},{7,6},{8,9},{9,8},{10,11... | collective-permute-start | bytes 589832 | tf_op jit(solution)/shard_map/ppermute | solution.py:47
  27.0 1.3 %copy-start = (f32[384]{0:T(512)S(1)}, f32[384]{0:T(512)}, u32[]{:S(2)}) copy-start(f32[384]{0:T(512)} %refs_2_.1) | copy-start | bytes 4612
  27.0 1.3 %copy-start.1 = (f32[384]{0:T(512)S(1)}, f32[384]{0:T(512)}, u32[]{:S(2)}) copy-start(f32[384]{0:T(512)} %refs_3_.1) | copy-start | bytes 4612
  29.5 4.8 %collective-permute-start.15 = (bf16[304,128]{1,0:T(8,128)(2,1)S(1)}, bf16[304,128]{1,0:T(8,128)(2,1)S(1)}, u32[]{:S(2)}, u32[]{:S(2)}) collective-permute-start(bf16[304,128]{1,0:T(8,128)(2,1)S(1)} %get-tuple-element.36), channel_id=1, source_target_pairs={{0,8},{1,9},{2,10},{3,11},{4,12},{5,13},{6,14},{7,15},{8,0},{9,1},... | collective-permute-start | bytes 233480 | tf_op jit(solution)/shard_map/ppermute | solution.py:47
  32.3 10.8 %collective-permute-start.16 = (bf16[672,128]{1,0:T(8,128)(2,1)S(1)}, bf16[672,128]{1,0:T(8,128)(2,1)S(1)}, u32[]{:S(2)}, u32[]{:S(2)}) collective-permute-start(bf16[672,128]{1,0:T(8,128)(2,1)S(1)} %sent_terms.1.refs_2_), channel_id=1, source_target_pairs={{0,8},{1,9},{2,10},{3,11},{4,12},{5,13},{6,14},{7,15},{8,0},{9,1},... | collective-permute-start | bytes 516104 | tf_op jit(solution)/shard_map/ppermute | solution.py:47
  34.3 5.1 %collective-permute-start.18 = (bf16[176,128]{1,0:T(8,128)(2,1)S(1)}, bf16[176,128]{1,0:T(8,128)(2,1)S(1)}, u32[]{:S(2)}, u32[]{:S(2)}) collective-permute-start(bf16[176,128]{1,0:T(8,128)(2,1)S(1)} %get-tuple-element.37.refs_9_), channel_id=1, source_target_pairs={{0,16},{1,17},{2,18},{3,19},{4,20},{5,21},{6,22},{7,23},{8,24},{9,... | collective-permute-start | bytes 135176 | tf_op jit(solution)/shard_map/ppermute | solution.py:47
  39.6 6.3 %collective-permute-start.19 = (bf16[2,64,128]{2,1,0:T(8,128)(2,1)S(1)}, bf16[2,64,128]{2,1,0:T(8,128)(2,1)S(1)}, u32[]{:S(2)}, u32[]{:S(2)}) collective-permute-start(bf16[2,64,128]{2,1,0:T(8,128)(2,1)S(1)} %get-tuple-element.45), channel_id=1, source_target_pairs={{0,2},{1,3},{2,0},{3,1},{4,6},{5,7},{6,4},{7,5},{8,10},{9,11},{10,... | collective-permute-start | bytes 98312 | tf_op jit(solution)/shard_map/ppermute | solution.py:47
  40.2 5.7 %collective-permute-start.20 = (bf16[2,64,128]{2,1,0:T(8,128)(2,1)S(1)}, bf16[2,64,128]{2,1,0:T(8,128)(2,1)S(1)}, u32[]{:S(2)}, u32[]{:S(2)}) collective-permute-start(bf16[2,64,128]{2,1,0:T(8,128)(2,1)S(1)} %get-tuple-element.46), channel_id=1, source_target_pairs={{0,4},{1,5},{2,6},{3,7},{4,0},{5,1},{6,2},{7,3},{8,12},{9,13},{10,... | collective-permute-start | bytes 98312 | tf_op jit(solution)/shard_map/ppermute | solution.py:47
  40.7 5.2 %collective-permute-start.21 = (bf16[2,64,128]{2,1,0:T(8,128)(2,1)S(1)}, bf16[2,64,128]{2,1,0:T(8,128)(2,1)S(1)}, u32[]{:S(2)}, u32[]{:S(2)}) collective-permute-start(bf16[2,64,128]{2,1,0:T(8,128)(2,1)S(1)} %get-tuple-element.47), channel_id=1, source_target_pairs={{0,6},{1,7},{2,4},{3,5},{4,2},{5,3},{6,0},{7,1},{8,14},{9,15},{10,... | collective-permute-start | bytes 98312 | tf_op jit(solution)/shard_map/ppermute | solution.py:47
  43.3 6.4 %collective-permute-start.17 = (bf16[336,128]{1,0:T(8,128)(2,1)S(1)}, bf16[336,128]{1,0:T(8,128)(2,1)S(1)}, u32[]{:S(2)}, u32[]{:S(2)}) collective-permute-start(bf16[336,128]{1,0:T(8,128)(2,1)S(1)} %halve.1), channel_id=1, source_target_pairs={{0,16},{1,17},{2,18},{3,19},{4,20},{5,21},{6,22},{7,23},{8,24},{9,... | collective-permute-start | bytes 258056 | tf_op jit(solution)/shard_map/ppermute | solution.py:47
  45.9 1.3 %collective-permute-start.22 = (bf16[4,64,128]{2,1,0:T(8,128)(2,1)S(1)}, bf16[4,64,128]{2,1,0:T(8,128)(2,1)S(1)}, u32[]{:S(2)}, u32[]{:S(2)}) collective-permute-start(bf16[4,64,128]{2,1,0:T(8,128)(2,1)S(1)} %cross_grads.1), channel_id=1, source_target_pairs={{0,1},{1,0},{2,3},{3,2},{4,5},{5,4},{6,7},{7,6},{8,9},{9,8},{10,11... | collective-permute-start | bytes 196616 | tf_op jit(solution)/shard_map/ppermute | solution.py:47

commit v5 on v4

--- a/solution.py
+++ b/solution.py
@@ -404,10 +404,19 @@
             ref[j] = (inv * (grad - first - normed_ref[row + 1] * second)).astype(BF16)
 
 
-def unpack_kernel(g, own_ref, *refs):
-    steps = g.outer.bit_length() - 1
-    received, refs = refs[:steps], refs[steps:]
-    direct, (crossed, acts_ref, out_ref, low, high) = refs[: g.pairs], refs[g.pairs :]
+STEP = 32
+
+
+def in_order(g, received):
+    shape = (g.per * STEP, g.sent)
+    row, col = iota(shape, 0), iota(shape, 1)
+    tap, lane = row & (STEP - 1), row >> 5
+    pick = ((col == tap * g.per + lane) & (tap < g.used)).astype(BF16)
+    return sum(dot(pick, unpack_rows(g, ref[: g.wrows])) for ref in received)
+
+
+def unpack_acts_kernel(g, own_ref, near_ref, *refs):
+    direct, (crossed, acts_ref, part_ref, low, high) = refs[: g.pairs], refs[g.pairs :]
     _, w = place(g)
     pick = channel_select(g, w, g.inner).astype(BF16)
     blocks = []
@@ -415,24 +424,24 @@
         blocks += [direct[k][0], crossed[k]]
     d_acts = dot(jnp.concatenate(blocks, axis=0), pick, ((0,), (0,)))
     acts_ref[...] = d_acts.astype(BF16).reshape(acts_ref.shape)
-
-    step = 32
-    shape = (g.per * step, g.sent)
-    row, col = iota(shape, 0), iota(shape, 1)
-    tap, lane = row & (step - 1), row >> 5
-    pick = ((col == tap * g.per + lane) & (tap < g.used)).astype(BF16)
-    total = jnp.zeros((g.per * step, 256), F32)
-    for ref in received:
-        total = total + dot(pick, unpack_rows(g, ref[: g.wrows]))
+    total = in_order(g, [near_ref])
     low[...] = own_ref[:, : g.lo]
     high[:, : g.hi] = own_ref[:, g.lo :]
     for i in range(g.per):
         at = pl.ds(i, g.used, stride=g.gp)
-        there = total[i * step : i * step + g.used]
+        there = total[i * STEP : i * STEP + g.used]
+        part_ref[i, : g.used, : g.lo] = low[at, :] + there[:, : g.lo]
+        part_ref[i, : g.used, g.lo :] = high[at, :][:, : g.hi] + there[:, g.lo : g.outs]
+
+
+def unpack_weights_kernel(g, part_ref, *refs):
+    *received, out_ref = refs
+    total = in_order(g, received)
+    for i in range(g.per):
         if g.first:
             out_ref[i, : 9 * g.first, :] = jnp.zeros((9 * g.first, g.outs), F32)
-        out_ref[i, 9 * g.first :, : g.lo] = low[at, :] + there[:, : g.lo]
-        out_ref[i, 9 * g.first :, g.lo :] = high[at, :][:, : g.hi] + there[:, g.lo : g.outs]
+        there = total[i * STEP : i * STEP + g.used, : g.outs]
+        out_ref[i, 9 * g.first :, :] = part_ref[i, : g.used, :] + there
 
 
 def call(g, kernel, name, outs, args, scratch=(), flops=0, after=()):
@@ -605,13 +614,16 @@
         terms.append(swap(send, g.inner << bit))
         bit += 1
     crossed = cross(g, "cross_grads", direct)
-    d_acts, d_weights = call(
+    d_acts, part = call(
         g,
-        unpack_kernel,
-        "unpack",
-        [(acts.shape, BF16), (weights.shape, F32)],
-        [own] + terms + direct + [crossed],
+        unpack_acts_kernel,
+        "unpack_acts",
+        [(acts.shape, BF16), ((g.per, STEP, g.outs), F32)],
+        [own, terms[0]] + direct + [crossed],
         [pltpu.VMEM((g.used * g.gp, 128), F32)] * 2,
+    )
+    (d_weights,) = call(
+        g, unpack_weights_kernel, "unpack_weights", [(weights.shape, F32)], [part] + terms[1:]
     )
     if g.blocks > 1:
         d_weights = lax.psum(d_weights, "block")

time: 51 us -> 50.8 us (level)
  waiting for transfers between devices: 10.5 us -> 9.48 us
  Pallas kernels: 10.4 us -> 11.2 us
    ppermute x23, waiting for transfers between devices: 10.5 us -> 9.48 us  [swap(): return lax.ppermute(value, 'tile', [(i, i ^ mask) for i in range(count)])]
    pallas_call x17 -> x18, Pallas kernels: 10.4 us -> 11.2 us  [call(): pl.pallas_call(lambda *refs: kernel(g, *refs[:count], *refs[rest:]), out_...]
  transfers between devices with their start and end apart: 23 -> 23, of which waited for: 7 -> 7; matrix products, arithmetic and copies ran while one was open for 0% -> 0% of each run, Pallas kernels for 15% -> 17%
where the time goes in v5:
time: 50.8 us; the launch traced here: 50.7 us
  starting transfers between devices  28.3 us (56%)
  Pallas kernels  11.2 us (22%)
  waiting for transfers between devices  9.48 us (19%)
  local copies, waits for them, and re-layouts  0.91 us (2%)
  between operations  0.83 us (2%)
    ppermute x23, starting transfers between devices, swap(): return lax.ppermute(value, 'tile', [(i, i ^ mask) for i in range(count)])  28.3 us
    pallas_call x18, Pallas kernels, call(): pl.pallas_call(lambda *refs: kernel(g, *refs[:count], *refs[rest:]), out_...  11.2 us
    ppermute x23, waiting for transfers between devices, swap(): return lax.ppermute(value, 'tile', [(i, i ^ mask) for i in range(count)])  9.48 us
  transfers between devices with their start and end apart: 23, of which 7 were waited for; matrix products, arithmetic and copies ran while one was open for 0% of the time, Pallas kernels for 17%

profile of v5, /device:TPU:0, one launch (start us, length us, event | category | flops | bytes accessed | tf_op | source)
XLA Modules:
  0.0 50.7 jit_solution(5671949236449458691)
XLA Ops:
  0.6 0.9 %copy-done.4 = bf16[2,1,64,384]{3,2,1,0:T(8,128)(2,1)S(1)} copy-done((bf16[2,1,64,384]{3,2,1,0:T(8,128)(2,1)S(1)}, bf16[2,1,64,384]{3,2,1,0:T(8,128)(2,1)}, u32[]{:S(2)}) %copy-start.4) | copy-done | bytes 98328
  1.8 3.0 %collective-permute-start.7 = (bf16[2,64,128]{2,1,0:T(8,128)(2,1)S(1)}, bf16[2,64,128]{2,1,0:T(8,128)(2,1)S(1)}, u32[]{:S(2)}, u32[]{:S(2)}) collective-permute-start(bf16[2,64,128]{2,1,0:T(8,128)(2,1)S(1)} %get-tuple-element.28), channel_id=1, source_target_pairs={{0,2},{1,3},{2,0},{3,1},{4,6},{5,7},{6,4},{7,5},{8,10},{9,11},{10,... | collective-permute-start | bytes 98312 | tf_op jit(solution)/shard_map/ppermute | solution.py:47
  4.8 1.5 %collective-permute-start.8 = (bf16[2,64,128]{2,1,0:T(8,128)(2,1)S(1)}, bf16[2,64,128]{2,1,0:T(8,128)(2,1)S(1)}, u32[]{:S(2)}, u32[]{:S(2)}) collective-permute-start(bf16[2,64,128]{2,1,0:T(8,128)(2,1)S(1)} %get-tuple-element.29), channel_id=1, source_target_pairs={{0,4},{1,5},{2,6},{3,7},{4,0},{5,1},{6,2},{7,3},{8,12},{9,13},{10,... | collective-permute-start | bytes 98312 | tf_op jit(solution)/shard_map/ppermute | solution.py:47
  6.4 0.6 %pack_weights.1.refs_0_ = bf16[336,128]{1,0:T(8,128)(2,1)S(1)} custom-call(bf16[12,27,192]{2,1,0:T(8,128)(2,1)S(1)} %copy-done.2), custom_call_target="tpu_custom_call" | custom-call | flops 6000000000 | bytes 210432 | tf_op jit(solution)/shard_map/pack_weights/pallas_call | solution.py:453
  6.9 2.1 %collective-permute-start.12 = (bf16[336,128]{1,0:T(8,128)(2,1)S(1)}, bf16[336,128]{1,0:T(8,128)(2,1)S(1)}, u32[]{:S(2)}, u32[]{:S(2)}) collective-permute-start(bf16[336,128]{1,0:T(8,128)(2,1)S(1)} %pack_weights.1.refs_0_), channel_id=1, source_target_pairs={{0,8},{1,9},{2,10},{3,11},{4,12},{5,13},{6,14},{7,15},{8,0},{9,1},... | collective-permute-start | bytes 258056 | tf_op jit(solution)/shard_map/ppermute | solution.py:47
  9.0 2.1 %collective-permute-done.9.refs_3_ = bf16[2,64,128]{2,1,0:T(8,128)(2,1)S(1)} collective-permute-done((bf16[2,64,128]{2,1,0:T(8,128)(2,1)S(1)}, bf16[2,64,128]{2,1,0:T(8,128)(2,1)S(1)}, u32[]{:S(2)}, u32[]{:S(2)}) %collective-permute-start.9) | collective-permute-done | bytes 32800 | tf_op jit(solution)/shard_map/ppermute | solution.py:47
  11.2 0.5 collective-permute-start.2
  11.7 1.6 %collective-permute-start.1 = (bf16[768,128]{1,0:T(8,128)(2,1)S(1)}, bf16[768,128]{1,0:T(8,128)(2,1)S(1)}, u32[]{:S(2)}, u32[]{:S(2)}) collective-permute-start(bf16[768,128]{1,0:T(8,128)(2,1)S(1)} %bitcast.5), channel_id=1, source_target_pairs={{0,4},{1,5},{2,6},{3,7},{4,0},{5,1},{6,2},{7,3},{8,12},{9,13},{10,... | collective-permute-start | bytes 589832 | tf_op jit(solution)/shard_map/ppermute | solution.py:47
  13.2 1.5 %collective-permute-start = (bf16[768,128]{1,0:T(8,128)(2,1)S(1)}, bf16[768,128]{1,0:T(8,128)(2,1)S(1)}, u32[]{:S(2)}, u32[]{:S(2)}) collective-permute-start(bf16[768,128]{1,0:T(8,128)(2,1)S(1)} %bitcast.6), channel_id=1, source_target_pairs={{0,2},{1,3},{2,0},{3,1},{4,6},{5,7},{6,4},{7,5},{8,10},{9,11},{10,... | collective-permute-start | bytes 589832 | tf_op jit(solution)/shard_map/ppermute | solution.py:47
  14.8 2.7 %collective-permute-start.13 = (bf16[672,128]{1,0:T(8,128)(2,1)S(1)}, bf16[672,128]{1,0:T(8,128)(2,1)S(1)}, u32[]{:S(2)}, u32[]{:S(2)}) collective-permute-start(bf16[672,128]{1,0:T(8,128)(2,1)S(1)} %join_kernel_rows.1), channel_id=1, source_target_pairs={{0,16},{1,17},{2,18},{3,19},{4,20},{5,21},{6,22},{7,23},{8,24},{9,... | collective-permute-start | bytes 516104 | tf_op jit(solution)/shard_map/ppermute | solution.py:47
  17.5 1.6 %collective-permute-start.11 = (bf16[176,128]{1,0:T(8,128)(2,1)S(1)}, bf16[176,128]{1,0:T(8,128)(2,1)S(1)}, u32[]{:S(2)}, u32[]{:S(2)}) collective-permute-start(bf16[176,128]{1,0:T(8,128)(2,1)S(1)} %get-tuple-element.33), channel_id=1, source_target_pairs={{0,8},{1,9},{2,10},{3,11},{4,12},{5,13},{6,14},{7,15},{8,0},{9,1},... | collective-permute-start | bytes 135176 | tf_op jit(solution)/shard_map/ppermute | solution.py:47
  19.1 2.7 %collective-permute-done.11.refs_1_.refs_6_ = bf16[176,128]{1,0:T(8,128)(2,1)S(1)} collective-permute-done((bf16[176,128]{1,0:T(8,128)(2,1)S(1)}, bf16[176,128]{1,0:T(8,128)(2,1)S(1)}, u32[]{:S(2)}, u32[]{:S(2)}) %collective-permute-start.11) | collective-permute-done | bytes 45088 | tf_op jit(solution)/shard_map/ppermute | solution.py:47
  21.9 2.4 %collective-permute-start.14 = (bf16[112,128]{1,0:T(8,128)(2,1)S(1)}, bf16[112,128]{1,0:T(8,128)(2,1)S(1)}, u32[]{:S(2)}, u32[]{:S(2)}) collective-permute-start(bf16[112,128]{1,0:T(8,128)(2,1)S(1)} %get-tuple-element.35), channel_id=1, source_target_pairs={{0,16},{1,17},{2,18},{3,19},{4,20},{5,21},{6,22},{7,23},{8,24},{9,... | collective-permute-start | bytes 86024 | tf_op jit(solution)/shard_map/ppermute | solution.py:47
  24.8 0.5 collective-permute-done.13.refs_2_
  25.7 1.3 %field_grad.2.refs_4_ = f32[10,64,768]{2,1,0:T(8,128)S(1)} custom-call(bf16[768,128]{1,0:T(8,128)(2,1)S(1)} %bitcast.8, bf16[768,128]{1,0:T(8,128)(2,1)S(1)} %collective-permute-done.refs_1_, bf16[768,128]{1,0:T(8,128)(2,1)S(1)} %collective-permute-done.1.refs_2_, bf16[768,128]{1,0:T(8,128)(2,1)S(1)} %collective-permute-done.2.refs_3_, ...), custom_call_target="tpu_custom_call" | custom-call | flops 1207959552 | bytes 3342336 | tf_op jit(solution)/shard_map/field_grad/pallas_call | solution.py:453
  27.1 1.2 %field_grad.3.refs_5_ = f32[10,64,768]{2,1,0:T(8,128)S(1)} custom-call(bf16[768,128]{1,0:T(8,128)(2,1)S(1)} %collective-permute-done.3.refs_0_.refs_4_, bf16[768,128]{1,0:T(8,128)(2,1)S(1)} %collective-permute-done.4.refs_1_.refs_5_, bf16[768,128]{1,0:T(8,128)(2,1)S(1)} %collective-permute-done.5.refs_2_.refs_6_, ...), custom_call_target="tpu_custom_call" | custom-call | flops 1207959552 | bytes 3342336 | tf_op jit(solution)/shard_map/field_grad/pallas_call | solution.py:453
  28.4 1.1 %norm_grad.1 = (f32[10,64,128]{2,1,0:T(8,128)S(1)}, bf16[4,10,16,128]{3,2,1,0:T(8,128)(2,1)S(1)}, f32[64,128]{1,0:T(8,128)S(1)}, f32[16,128]{1,0:T(8,128)S(1)}, ...) custom-call(bf16[8,64,128]{2,1,0:T(8,128)(2,1)S(1)} %get-tuple-element.31.refs_0_, ...), custom_call_target="tpu_custom_call" | custom-call | bytes 5086208 | tf_op jit(solution)/shard_map/norm_grad/pallas_call | solution.py:453
  29.5 0.9 %collective-permute-start.15 = (bf16[304,128]{1,0:T(8,128)(2,1)S(1)}, bf16[304,128]{1,0:T(8,128)(2,1)S(1)}, u32[]{:S(2)}, u32[]{:S(2)}) collective-permute-start(bf16[304,128]{1,0:T(8,128)(2,1)S(1)} %get-tuple-element.38), channel_id=1, source_target_pairs={{0,8},{1,9},{2,10},{3,11},{4,12},{5,13},{6,14},{7,15},{8,0},{9,1},... | collective-permute-start | bytes 233480 | tf_op jit(solution)/shard_map/ppermute | solution.py:47
  30.4 1.9 %sent_terms.1.refs_2_ = bf16[672,128]{1,0:T(8,128)(2,1)S(1)} custom-call(bf16[768,128]{1,0:T(8,128)(2,1)S(1)} %bitcast.9, bf16[768,128]{1,0:T(8,128)(2,1)S(1)} %collective-permute-done.refs_1_, bf16[768,128]{1,0:T(8,128)(2,1)S(1)} %collective-permute-done.1.refs_2_, bf16[768,128]{1,0:T(8,128)(2,1)S(1)} %collective-permute-done.2.refs_3_, ...), custom_call_target="tpu_custom_call" | custom-call | flops 1207959552 | bytes 1908736 | tf_op jit(solution)/shard_map/sent_terms/pallas_call | solution.py:453
  32.3 1.3 %collective-permute-start.16 = (bf16[672,128]{1,0:T(8,128)(2,1)S(1)}, bf16[672,128]{1,0:T(8,128)(2,1)S(1)}, u32[]{:S(2)}, u32[]{:S(2)}) collective-permute-start(bf16[672,128]{1,0:T(8,128)(2,1)S(1)} %sent_terms.1.refs_2_), channel_id=1, source_target_pairs={{0,8},{1,9},{2,10},{3,11},{4,12},{5,13},{6,14},{7,15},{8,0},{9,1},... | collective-permute-start | bytes 516104 | tf_op jit(solution)/shard_map/ppermute | solution.py:47
  33.6 0.7 %collective-permute-done.15.refs_1_.refs_4_ = bf16[304,128]{1,0:T(8,128)(2,1)S(1)} collective-permute-done((bf16[304,128]{1,0:T(8,128)(2,1)S(1)}, bf16[304,128]{1,0:T(8,128)(2,1)S(1)}, u32[]{:S(2)}, u32[]{:S(2)}) %collective-permute-start.15) | collective-permute-done | bytes 77856 | tf_op jit(solution)/shard_map/ppermute | solution.py:47
  34.3 2.5 %collective-permute-start.17 = (bf16[176,128]{1,0:T(8,128)(2,1)S(1)}, bf16[176,128]{1,0:T(8,128)(2,1)S(1)}, u32[]{:S(2)}, u32[]{:S(2)}) collective-permute-start(bf16[176,128]{1,0:T(8,128)(2,1)S(1)} %get-tuple-element.39.refs_9_), channel_id=1, source_target_pairs={{0,16},{1,17},{2,18},{3,19},{4,20},{5,21},{6,22},{7,23},{8,24},{9,... | collective-permute-start | bytes 135176 | tf_op jit(solution)/shard_map/ppermute | solution.py:47
  36.8 1.9 %kept_terms.1 = (f32[288,192]{1,0:T(8,128)S(1)}, f32[1,224,192]{2,1,0:T(8,128)S(1)}) custom-call(bf16[768,128]{1,0:T(8,128)(2,1)S(1)} %bitcast.10, bf16[768,128]{1,0:T(8,128)(2,1)S(1)} %collective-permute-done.refs_1_, bf16[768,128]{1,0:T(8,128)(2,1)S(1)} %collective-permute-done.1.refs_2_, bf16[768,128]{1,0:T(8,128)(2,1)S(1)} %collective-permute-done.2.refs_3_, ...), custom_call_target="tpu_custom_call" | custom-call | flops 1207959552 | bytes 2129920 | tf_op jit(solution)/shard_map/kept_terms/pallas_call | solution.py:453
  38.7 0.7 %collective-permute-done.17.refs_5_ = bf16[176,128]{1,0:T(8,128)(2,1)S(1)} collective-permute-done((bf16[176,128]{1,0:T(8,128)(2,1)S(1)}, bf16[176,128]{1,0:T(8,128)(2,1)S(1)}, u32[]{:S(2)}, u32[]{:S(2)}) %collective-permute-start.17) | collective-permute-done | bytes 45088 | tf_op jit(solution)/shard_map/ppermute | solution.py:47
  39.6 0.6 %collective-permute-start.18 = (bf16[2,64,128]{2,1,0:T(8,128)(2,1)S(1)}, bf16[2,64,128]{2,1,0:T(8,128)(2,1)S(1)}, u32[]{:S(2)}, u32[]{:S(2)}) collective-permute-start(bf16[2,64,128]{2,1,0:T(8,128)(2,1)S(1)} %get-tuple-element.46), channel_id=1, source_target_pairs={{0,2},{1,3},{2,0},{3,1},{4,6},{5,7},{6,4},{7,5},{8,10},{9,11},{10,... | collective-permute-start | bytes 98312 | tf_op jit(solution)/shard_map/ppermute | solution.py:47
  40.2 0.5 collective-permute-start.19
  40.7 2.5 %collective-permute-start.20 = (bf16[2,64,128]{2,1,0:T(8,128)(2,1)S(1)}, bf16[2,64,128]{2,1,0:T(8,128)(2,1)S(1)}, u32[]{:S(2)}, u32[]{:S(2)}) collective-permute-start(bf16[2,64,128]{2,1,0:T(8,128)(2,1)S(1)} %get-tuple-element.48), channel_id=1, source_target_pairs={{0,6},{1,7},{2,4},{3,5},{4,2},{5,3},{6,0},{7,1},{8,14},{9,15},{10,... | collective-permute-start | bytes 98312 | tf_op jit(solution)/shard_map/ppermute | solution.py:47
  43.3 2.6 %collective-permute-start.22 = (bf16[336,128]{1,0:T(8,128)(2,1)S(1)}, bf16[336,128]{1,0:T(8,128)(2,1)S(1)}, u32[]{:S(2)}, u32[]{:S(2)}) collective-permute-start(bf16[336,128]{1,0:T(8,128)(2,1)S(1)} %halve.1), channel_id=1, source_target_pairs={{0,16},{1,17},{2,18},{3,19},{4,20},{5,21},{6,22},{7,23},{8,24},{9,... | collective-permute-start | bytes 258056 | tf_op jit(solution)/shard_map/ppermute | solution.py:47
  46.0 1.2 %collective-permute-done.21.refs_6_ = bf16[4,64,128]{2,1,0:T(8,128)(2,1)S(1)} collective-permute-done((bf16[4,64,128]{2,1,0:T(8,128)(2,1)S(1)}, bf16[4,64,128]{2,1,0:T(8,128)(2,1)S(1)}, u32[]{:S(2)}, u32[]{:S(2)}) %collective-permute-start.21) | collective-permute-done | bytes 65568 | tf_op jit(solution)/shard_map/ppermute | solution.py:47
  47.2 1.0 %unpack_acts.1 = (bf16[2,1,64,384]{3,2,1,0:T(8,128)(2,1)}, f32[12,32,192]{2,1,0:T(8,128)S(1)}) custom-call(f32[288,192]{1,0:T(8,128)S(1)} %get-tuple-element.40.refs_6_.refs_0_, bf16[672,128]{1,0:T(8,128)(2,1)S(1)} %collective-permute-done.16.refs_1_, bf16[2,64,128]{2,1,0:T(8,128)(2,1)S(1)} %get-tuple-element.45.refs_0_.refs_2_, ...), custom_call_target="tpu_custom_call" | custom-call | bytes 983040 | tf_op jit(solution)/shard_map/unpack_acts/pallas_call | solution.py:453
  48.2 1.4 %collective-permute-done.22.refs_1_ = bf16[336,128]{1,0:T(8,128)(2,1)S(1)} collective-permute-done((bf16[336,128]{1,0:T(8,128)(2,1)S(1)}, bf16[336,128]{1,0:T(8,128)(2,1)S(1)}, u32[]{:S(2)}, u32[]{:S(2)}) %collective-permute-start.22) | collective-permute-done | bytes 86048 | tf_op jit(solution)/shard_map/ppermute | solution.py:47
  49.7 1.0 %unpack_weights.1 = f32[12,27,192]{2,1,0:T(8,128)} custom-call(f32[12,32,192]{2,1,0:T(8,128)S(1)} %get-tuple-element.50.refs_0_, bf16[336,128]{1,0:T(8,128)(2,1)S(1)} %collective-permute-done.22.refs_1_), custom_call_target="tpu_custom_call" | custom-call | bytes 629760 | tf_op jit(solution)/shard_map/unpack_weights/pallas_call | solution.py:453
  (42 shorter events, 1.8 us)
Async XLA Ops:
  0.6 0.9 %copy-start.4 = (bf16[2,1,64,384]{3,2,1,0:T(8,128)(2,1)S(1)}, bf16[2,1,64,384]{3,2,1,0:T(8,128)(2,1)}, u32[]{:S(2)}) copy-start(bf16[2,1,64,384]{3,2,1,0:T(8,128)(2,1)} %param.5) | copy-start | bytes 294916
  1.5 4.8 %copy-start.2 = (bf16[12,27,192]{2,1,0:T(8,128)(2,1)S(1)}, bf16[12,27,192]{2,1,0:T(8,128)(2,1)}, u32[]{:S(2)}) copy-start(bf16[12,27,192]{2,1,0:T(8,128)(2,1)} %refs_0_.1) | copy-start | bytes 373252
  1.8 7.2 %collective-permute-start.7 = (bf16[2,64,128]{2,1,0:T(8,128)(2,1)S(1)}, bf16[2,64,128]{2,1,0:T(8,128)(2,1)S(1)}, u32[]{:S(2)}, u32[]{:S(2)}) collective-permute-start(bf16[2,64,128]{2,1,0:T(8,128)(2,1)S(1)} %get-tuple-element.28), channel_id=1, source_target_pairs={{0,2},{1,3},{2,0},{3,1},{4,6},{5,7},{6,4},{7,5},{8,10},{9,11},{10,... | collective-permute-start | bytes 98312 | tf_op jit(solution)/shard_map/ppermute | solution.py:47
  4.8 4.2 %collective-permute-start.8 = (bf16[2,64,128]{2,1,0:T(8,128)(2,1)S(1)}, bf16[2,64,128]{2,1,0:T(8,128)(2,1)S(1)}, u32[]{:S(2)}, u32[]{:S(2)}) collective-permute-start(bf16[2,64,128]{2,1,0:T(8,128)(2,1)S(1)} %get-tuple-element.29), channel_id=1, source_target_pairs={{0,4},{1,5},{2,6},{3,7},{4,0},{5,1},{6,2},{7,3},{8,12},{9,13},{10,... | collective-permute-start | bytes 98312 | tf_op jit(solution)/shard_map/ppermute | solution.py:47
  6.3 4.8 %copy-start.3 = (bf16[2,2,128,192]{2,3,1,0:T(8,128)(2,1)S(1)}, bf16[2,2,128,192]{2,3,1,0:T(8,128)(2,1)}, u32[]{:S(2)}) copy-start(bf16[2,2,128,192]{2,3,1,0:T(8,128)(2,1)} %param.9) | copy-start | bytes 589828
  6.3 4.8 %collective-permute-start.9 = (bf16[2,64,128]{2,1,0:T(8,128)(2,1)S(1)}, bf16[2,64,128]{2,1,0:T(8,128)(2,1)S(1)}, u32[]{:S(2)}, u32[]{:S(2)}) collective-permute-start(bf16[2,64,128]{2,1,0:T(8,128)(2,1)S(1)} %get-tuple-element.30), channel_id=1, source_target_pairs={{0,6},{1,7},{2,4},{3,5},{4,2},{5,3},{6,0},{7,1},{8,14},{9,15},{10,... | collective-permute-start | bytes 98312 | tf_op jit(solution)/shard_map/ppermute | solution.py:47
  6.9 7.8 %collective-permute-start.12 = (bf16[336,128]{1,0:T(8,128)(2,1)S(1)}, bf16[336,128]{1,0:T(8,128)(2,1)S(1)}, u32[]{:S(2)}, u32[]{:S(2)}) collective-permute-start(bf16[336,128]{1,0:T(8,128)(2,1)S(1)} %pack_weights.1.refs_0_), channel_id=1, source_target_pairs={{0,8},{1,9},{2,10},{3,11},{4,12},{5,13},{6,14},{7,15},{8,0},{9,1},... | collective-permute-start | bytes 258056 | tf_op jit(solution)/shard_map/ppermute | solution.py:47
  11.2 6.3 %collective-permute-start.10 = (bf16[4,64,128]{2,1,0:T(8,128)(2,1)S(1)}, bf16[4,64,128]{2,1,0:T(8,128)(2,1)S(1)}, u32[]{:S(2)}, u32[]{:S(2)}) collective-permute-start(bf16[4,64,128]{2,1,0:T(8,128)(2,1)S(1)} %cross_acts.1), channel_id=1, source_target_pairs={{0,1},{1,0},{2,3},{3,2},{4,5},{5,4},{6,7},{7,6},{8,9},{9,8},{10,11... | collective-permute-start | bytes 196616 | tf_op jit(solution)/shard_map/ppermute | solution.py:47
  11.2 10.7 %collective-permute-start.2 = (bf16[768,128]{1,0:T(8,128)(2,1)S(1)}, bf16[768,128]{1,0:T(8,128)(2,1)S(1)}, u32[]{:S(2)}, u32[]{:S(2)}) collective-permute-start(bf16[768,128]{1,0:T(8,128)(2,1)S(1)} %bitcast.4), channel_id=1, source_target_pairs={{0,6},{1,7},{2,4},{3,5},{4,2},{5,3},{6,0},{7,1},{8,14},{9,15},{10,... | collective-permute-start | bytes 589832 | tf_op jit(solution)/shard_map/ppermute | solution.py:47
  11.7 12.6 %collective-permute-start.1 = (bf16[768,128]{1,0:T(8,128)(2,1)S(1)}, bf16[768,128]{1,0:T(8,128)(2,1)S(1)}, u32[]{:S(2)}, u32[]{:S(2)}) collective-permute-start(bf16[768,128]{1,0:T(8,128)(2,1)S(1)} %bitcast.5), channel_id=1, source_target_pairs={{0,4},{1,5},{2,6},{3,7},{4,0},{5,1},{6,2},{7,3},{8,12},{9,13},{10,... | collective-permute-start | bytes 589832 | tf_op jit(solution)/shard_map/ppermute | solution.py:47
  13.2 11.3 %collective-permute-start = (bf16[768,128]{1,0:T(8,128)(2,1)S(1)}, bf16[768,128]{1,0:T(8,128)(2,1)S(1)}, u32[]{:S(2)}, u32[]{:S(2)}) collective-permute-start(bf16[768,128]{1,0:T(8,128)(2,1)S(1)} %bitcast.6), channel_id=1, source_target_pairs={{0,2},{1,3},{2,0},{3,1},{4,6},{5,7},{6,4},{7,5},{8,10},{9,11},{10,... | collective-permute-start | bytes 589832 | tf_op jit(solution)/shard_map/ppermute | solution.py:47
  14.8 10.5 %collective-permute-start.13 = (bf16[672,128]{1,0:T(8,128)(2,1)S(1)}, bf16[672,128]{1,0:T(8,128)(2,1)S(1)}, u32[]{:S(2)}, u32[]{:S(2)}) collective-permute-start(bf16[672,128]{1,0:T(8,128)(2,1)S(1)} %join_kernel_rows.1), channel_id=1, source_target_pairs={{0,16},{1,17},{2,18},{3,19},{4,20},{5,21},{6,22},{7,23},{8,24},{9,... | collective-permute-start | bytes 516104 | tf_op jit(solution)/shard_map/ppermute | solution.py:47
  17.5 4.3 %collective-permute-start.11 = (bf16[176,128]{1,0:T(8,128)(2,1)S(1)}, bf16[176,128]{1,0:T(8,128)(2,1)S(1)}, u32[]{:S(2)}, u32[]{:S(2)}) collective-permute-start(bf16[176,128]{1,0:T(8,128)(2,1)S(1)} %get-tuple-element.33), channel_id=1, source_target_pairs={{0,8},{1,9},{2,10},{3,11},{4,12},{5,13},{6,14},{7,15},{8,0},{9,1},... | collective-permute-start | bytes 135176 | tf_op jit(solution)/shard_map/ppermute | solution.py:47
  21.8 5.2 %collective-permute-start.3 = (bf16[768,128]{1,0:T(8,128)(2,1)S(1)}, bf16[768,128]{1,0:T(8,128)(2,1)S(1)}, u32[]{:S(2)}, u32[]{:S(2)}) collective-permute-start(bf16[768,128]{1,0:T(8,128)(2,1)S(1)} %bitcast.7), channel_id=1, source_target_pairs={{0,1},{1,0},{2,3},{3,2},{4,5},{5,4},{6,7},{7,6},{8,9},{9,8},{10,11... | collective-permute-start | bytes 589832 | tf_op jit(solution)/shard_map/ppermute | solution.py:47
  21.9 6.5 %collective-permute-start.14 = (bf16[112,128]{1,0:T(8,128)(2,1)S(1)}, bf16[112,128]{1,0:T(8,128)(2,1)S(1)}, u32[]{:S(2)}, u32[]{:S(2)}) collective-permute-start(bf16[112,128]{1,0:T(8,128)(2,1)S(1)} %get-tuple-element.35), channel_id=1, source_target_pairs={{0,16},{1,17},{2,18},{3,19},{4,20},{5,21},{6,22},{7,23},{8,24},{9,... | collective-permute-start | bytes 86024 | tf_op jit(solution)/shard_map/ppermute | solution.py:47
  24.3 2.8 %collective-permute-start.6 = (bf16[768,128]{1,0:T(8,128)(2,1)S(1)}, bf16[768,128]{1,0:T(8,128)(2,1)S(1)}, u32[]{:S(2)}, u32[]{:S(2)}) collective-permute-start(bf16[768,128]{1,0:T(8,128)(2,1)S(1)} %collective-permute-done.2.refs_3_), channel_id=1, source_target_pairs={{0,1},{1,0},{2,3},{3,2},{4,5},{5,4},{6,7},{7,6},{8,9},{9,8},{10,11... | collective-permute-start | bytes 589832 | tf_op jit(solution)/shard_map/ppermute | solution.py:47
  24.5 2.5 %collective-permute-start.5 = (bf16[768,128]{1,0:T(8,128)(2,1)S(1)}, bf16[768,128]{1,0:T(8,128)(2,1)S(1)}, u32[]{:S(2)}, u32[]{:S(2)}) collective-permute-start(bf16[768,128]{1,0:T(8,128)(2,1)S(1)} %collective-permute-done.1.refs_2_), channel_id=1, source_target_pairs={{0,1},{1,0},{2,3},{3,2},{4,5},{5,4},{6,7},{7,6},{8,9},{9,8},{10,11... | collective-permute-start | bytes 589832 | tf_op jit(solution)/shard_map/ppermute | solution.py:47
  25.3 1.8 %collective-permute-start.4 = (bf16[768,128]{1,0:T(8,128)(2,1)S(1)}, bf16[768,128]{1,0:T(8,128)(2,1)S(1)}, u32[]{:S(2)}, u32[]{:S(2)}) collective-permute-start(bf16[768,128]{1,0:T(8,128)(2,1)S(1)} %collective-permute-done.refs_1_), channel_id=1, source_target_pairs={{0,1},{1,0},{2,3},{3,2},{4,5},{5,4},{6,7},{7,6},{8,9},{9,8},{10,11... | collective-permute-start | bytes 589832 | tf_op jit(solution)/shard_map/ppermute | solution.py:47
  27.0 1.3 %copy-start = (f32[384]{0:T(512)S(1)}, f32[384]{0:T(512)}, u32[]{:S(2)}) copy-start(f32[384]{0:T(512)} %refs_2_.1) | copy-start | bytes 4612
  27.0 1.3 %copy-start.1 = (f32[384]{0:T(512)S(1)}, f32[384]{0:T(512)}, u32[]{:S(2)}) copy-start(f32[384]{0:T(512)} %refs_3_.1) | copy-start | bytes 4612
  29.5 4.8 %collective-permute-start.15 = (bf16[304,128]{1,0:T(8,128)(2,1)S(1)}, bf16[304,128]{1,0:T(8,128)(2,1)S(1)}, u32[]{:S(2)}, u32[]{:S(2)}) collective-permute-start(bf16[304,128]{1,0:T(8,128)(2,1)S(1)} %get-tuple-element.38), channel_id=1, source_target_pairs={{0,8},{1,9},{2,10},{3,11},{4,12},{5,13},{6,14},{7,15},{8,0},{9,1},... | collective-permute-start | bytes 233480 | tf_op jit(solution)/shard_map/ppermute | solution.py:47
  32.3 10.8 %collective-permute-start.16 = (bf16[672,128]{1,0:T(8,128)(2,1)S(1)}, bf16[672,128]{1,0:T(8,128)(2,1)S(1)}, u32[]{:S(2)}, u32[]{:S(2)}) collective-permute-start(bf16[672,128]{1,0:T(8,128)(2,1)S(1)} %sent_terms.1.refs_2_), channel_id=1, source_target_pairs={{0,8},{1,9},{2,10},{3,11},{4,12},{5,13},{6,14},{7,15},{8,0},{9,1},... | collective-permute-start | bytes 516104 | tf_op jit(solution)/shard_map/ppermute | solution.py:47
  34.3 5.1 %collective-permute-start.17 = (bf16[176,128]{1,0:T(8,128)(2,1)S(1)}, bf16[176,128]{1,0:T(8,128)(2,1)S(1)}, u32[]{:S(2)}, u32[]{:S(2)}) collective-permute-start(bf16[176,128]{1,0:T(8,128)(2,1)S(1)} %get-tuple-element.39.refs_9_), channel_id=1, source_target_pairs={{0,16},{1,17},{2,18},{3,19},{4,20},{5,21},{6,22},{7,23},{8,24},{9,... | collective-permute-start | bytes 135176 | tf_op jit(solution)/shard_map/ppermute | solution.py:47
  39.6 6.3 %collective-permute-start.18 = (bf16[2,64,128]{2,1,0:T(8,128)(2,1)S(1)}, bf16[2,64,128]{2,1,0:T(8,128)(2,1)S(1)}, u32[]{:S(2)}, u32[]{:S(2)}) collective-permute-start(bf16[2,64,128]{2,1,0:T(8,128)(2,1)S(1)} %get-tuple-element.46), channel_id=1, source_target_pairs={{0,2},{1,3},{2,0},{3,1},{4,6},{5,7},{6,4},{7,5},{8,10},{9,11},{10,... | collective-permute-start | bytes 98312 | tf_op jit(solution)/shard_map/ppermute | solution.py:47
  40.2 5.7 %collective-permute-start.19 = (bf16[2,64,128]{2,1,0:T(8,128)(2,1)S(1)}, bf16[2,64,128]{2,1,0:T(8,128)(2,1)S(1)}, u32[]{:S(2)}, u32[]{:S(2)}) collective-permute-start(bf16[2,64,128]{2,1,0:T(8,128)(2,1)S(1)} %get-tuple-element.47), channel_id=1, source_target_pairs={{0,4},{1,5},{2,6},{3,7},{4,0},{5,1},{6,2},{7,3},{8,12},{9,13},{10,... | collective-permute-start | bytes 98312 | tf_op jit(solution)/shard_map/ppermute | solution.py:47
  40.7 5.2 %collective-permute-start.20 = (bf16[2,64,128]{2,1,0:T(8,128)(2,1)S(1)}, bf16[2,64,128]{2,1,0:T(8,128)(2,1)S(1)}, u32[]{:S(2)}, u32[]{:S(2)}) collective-permute-start(bf16[2,64,128]{2,1,0:T(8,128)(2,1)S(1)} %get-tuple-element.48), channel_id=1, source_target_pairs={{0,6},{1,7},{2,4},{3,5},{4,2},{5,3},{6,0},{7,1},{8,14},{9,15},{10,... | collective-permute-start | bytes 98312 | tf_op jit(solution)/shard_map/ppermute | solution.py:47
  43.3 6.4 %collective-permute-start.22 = (bf16[336,128]{1,0:T(8,128)(2,1)S(1)}, bf16[336,128]{1,0:T(8,128)(2,1)S(1)}, u32[]{:S(2)}, u32[]{:S(2)}) collective-permute-start(bf16[336,128]{1,0:T(8,128)(2,1)S(1)} %halve.1), channel_id=1, source_target_pairs={{0,16},{1,17},{2,18},{3,19},{4,20},{5,21},{6,22},{7,23},{8,24},{9,... | collective-permute-start | bytes 258056 | tf_op jit(solution)/shard_map/ppermute | solution.py:47
  45.9 1.3 %collective-permute-start.21 = (bf16[4,64,128]{2,1,0:T(8,128)(2,1)S(1)}, bf16[4,64,128]{2,1,0:T(8,128)(2,1)S(1)}, u32[]{:S(2)}, u32[]{:S(2)}) collective-permute-start(bf16[4,64,128]{2,1,0:T(8,128)(2,1)S(1)} %cross_grads.1), channel_id=1, source_target_pairs={{0,1},{1,0},{2,3},{3,2},{4,5},{5,4},{6,7},{7,6},{8,9},{9,8},{10,11... | collective-permute-start | bytes 196616 | tf_op jit(solution)/shard_map/ppermute | solution.py:47

commit v6 on v5

--- a/solution.py
+++ b/solution.py
@@ -313,7 +313,7 @@
     grad_ref[...] = grad
     sums = totals(g, jnp.sum(grad, axis=0), jnp.sum(grad * normed_ref[...], axis=0))
     sums_ref[...] = sums
-    send_stats(g, send_ref, sums, z, grad_ref, 2)
+    send_stats(g, send_ref, sums, z, grad_ref, 1)
 
 
 def kernel_terms(g, first, direct, crossed, hidden_ref, acc, ups):
@@ -357,34 +357,27 @@
 
 def sent_terms_kernel(g, *refs):
     direct, crossed, refs = refs[: g.pairs], refs[g.pairs : 2 * g.pairs], refs[2 * g.pairs :]
-    hidden_ref, send_ref, acc, ups = refs
+    hidden_ref, *sends, acc, ups = refs
     kernel_terms(g, 0, direct, crossed, hidden_ref, acc, ups)
     pick = sent_order(g)
-    for i in range(g.outer // 2):
+    for i, ref in enumerate(sends):
         terms = acc[i].reshape(g.used * g.gp, g.outs).astype(BF16)
-        send_ref[i * g.wrows : (i + 1) * g.wrows] = pack_rows(g, dot(pick, terms))
+        ref[...] = pack_rows(g, dot(pick, terms))
 
 
 def kept_terms_kernel(g, *refs):
     direct, crossed, refs = refs[: g.pairs], refs[g.pairs : 2 * g.pairs], refs[2 * g.pairs :]
-    hidden_ref, own_ref, *kept, acc, ups = refs
+    hidden_ref, own_ref, keep_ref, acc, ups = refs
     kernel_terms(g, g.outer // 2, direct, crossed, hidden_ref, acc, ups)
     own_ref[...] = acc[0].reshape(g.used * g.gp, g.outs)
     pick = sent_order(g)
-    for i in range(1, g.outer // 2):
-        terms = acc[i].reshape(g.used * g.gp, g.outs)
-        kept[0][i - 1] = sum(dot(pick, piece) for piece in split(terms, 2))
-
-
-def halve_kernel(g, bit, keep_ref, received_ref, *refs):
-    send_ref, *kept = refs
-    for i in range(keep_ref.shape[0]):
-        block = received_ref[(i + 1) * g.wrows : (i + 2) * g.wrows]
-        total = keep_ref[i] + unpack_rows(g, block).astype(F32)[:, : g.outs]
-        if i % 2:
-            kept[0][i // 2] = total
-        else:
-            send_ref[i // 2 * g.wrows : (i // 2 + 1) * g.wrows] = pack_rows(g, total)
+    terms = acc[1].reshape(g.used * g.gp, g.outs)
+    keep_ref[...] = sum(dot(pick, piece) for piece in split(terms, 2))
+
+
+def add_terms_kernel(g, keep_ref, received_ref, send_ref):
+    block = unpack_rows(g, received_ref[...]).astype(F32)
+    send_ref[...] = pack_rows(g, keep_ref[...] + block[:, : g.outs])
 
 
 def finish_kernel(g, *refs):
@@ -394,7 +387,7 @@
     first, second = spread(g, add_stats(sums_ref[...], received[1:]))
     first, second = first / g.count, second / g.count
     inv = inv_ref[...]
-    above, below = edges(g, z, received, 2)
+    above, below = edges(g, z, received, 1)
     for k, ref in enumerate(sends):
         for j in range(2):
             row = w ^ (2 * k + j)
@@ -561,32 +554,31 @@
         g,
         norm_grad_kernel,
         "norm_grad",
-        [rows_shape, hidden_shape, ((g.rb, g.cells), F32), stats_shape, rows_shape, sums_shape(4)],
+        [rows_shape, hidden_shape, ((g.rb, g.cells), F32), stats_shape, rows_shape, sums_shape(2)],
         [rows, stats, gamma, beta] + fields + received,
         [pltpu.VMEM(*rows_shape), pltpu.VMEM((g.outer, g.gp, g.cells), BF16)],
     )
     half = g.outer // 2
-    kept_shape = lambda count: [((count, g.sent, g.outs), F32)] if count else []
     scratch = [
         pltpu.VMEM((half, g.used, g.gp, g.outs), F32),
         pltpu.VMEM((half, count, g.gp, wide_shape[-1]), BF16),
     ]
-    (terms,) = call(
+    near, far = call(
         g,
         sent_terms_kernel,
         "sent_terms",
-        [((half * g.wrows, 128), BF16)],
+        [packed_shape] * 2,
         arrived + [hidden],
         scratch,
         flops // 2,
     )
-    sums, send, received = over_z("add_sums", sums, send, 2, [terms])
-    terms = [swap(terms, g.inner)]
-    own, *kept = call(
+    sums, send, received = over_z("add_sums", sums, send, 1, [near])
+    far = swap(far, g.inner)
+    own, keep = call(
         g,
         kept_terms_kernel,
         "kept_terms",
-        [((g.used * g.gp, g.outs), F32)] + kept_shape(half - 1),
+        [((g.used * g.gp, g.outs), F32), ((g.sent, g.outs), F32)],
         arrived + [hidden],
         scratch,
         flops // 2,
@@ -601,18 +593,9 @@
         after=[own],
     )
     direct = [sends[0]] + [swap(sends[k], 2 * k) for k in range(1, g.pairs)]
-    bit = 1
-    while kept:
-        half //= 2
-        send, *kept = call(
-            g,
-            lambda g, *refs, bit=bit: halve_kernel(g, bit, *refs),
-            "halve",
-            [((half * g.wrows, 128), BF16)] + kept_shape(half - 1),
-            [kept[0], terms[-1]],
-        )
-        terms.append(swap(send, g.inner << bit))
-        bit += 1
+    near = swap(pass_on(g, near, [send]), g.inner)
+    (far,) = call(g, add_terms_kernel, "add_terms", [packed_shape], [keep, far], after=[near])
+    terms = [near, swap(far, 2 * g.inner)]
     crossed = cross(g, "cross_grads", direct)
     d_acts, part = call(
         g,

time: 50.8 us -> 50.3 us (level)
  waiting for transfers between devices: 9.48 us -> 8.69 us
    ppermute x23 -> x24, waiting for transfers between devices: 9.48 us -> 8.69 us  [swap(): return lax.ppermute(value, 'tile', [(i, i ^ mask) for i in range(count)])]
    ppermute x23 -> x24, starting transfers between devices: 28.3 us -> 28.5 us  [swap(): return lax.ppermute(value, 'tile', [(i, i ^ mask) for i in range(count)])]
    pallas_call x18 -> x19, Pallas kernels: 11.2 us -> 11.2 us  [call(): pl.pallas_call(lambda *refs: kernel(g, *refs[:count], *refs[rest:]), out_...]
  transfers between devices with their start and end apart: 23 -> 24, of which waited for: 7 -> 6; matrix products, arithmetic and copies ran while one was open for 0% -> 0% of each run, Pallas kernels for 17% -> 17%
where the time goes in v6:
time: 50.3 us; the launch traced here: 50.1 us
  starting transfers between devices  28.5 us (57%)
  Pallas kernels  11.2 us (22%)
  waiting for transfers between devices  8.69 us (17%)
  local copies, waits for them, and re-layouts  0.91 us (2%)
  between operations  0.83 us (2%)
    ppermute x24, starting transfers between devices, swap(): return lax.ppermute(value, 'tile', [(i, i ^ mask) for i in range(count)])  28.5 us
    pallas_call x19, Pallas kernels, call(): pl.pallas_call(lambda *refs: kernel(g, *refs[:count], *refs[rest:]), out_...  11.2 us
    ppermute x24, waiting for transfers between devices, swap(): return lax.ppermute(value, 'tile', [(i, i ^ mask) for i in range(count)])  8.69 us
  transfers between devices with their start and end apart: 24, of which 6 were waited for; matrix products, arithmetic and copies ran while one was open for 0% of the time, Pallas kernels for 17%

profile of v6, /device:TPU:0, one launch (start us, length us, event | category | flops | bytes accessed | tf_op | source)
XLA Modules:
  0.0 50.1 jit_solution(17598665475723048509)
XLA Ops:
  0.6 0.9 %copy-done.4 = bf16[2,1,64,384]{3,2,1,0:T(8,128)(2,1)S(1)} copy-done((bf16[2,1,64,384]{3,2,1,0:T(8,128)(2,1)S(1)}, bf16[2,1,64,384]{3,2,1,0:T(8,128)(2,1)}, u32[]{:S(2)}) %copy-start.4) | copy-done | bytes 98328
  1.8 3.0 %collective-permute-start.7 = (bf16[2,64,128]{2,1,0:T(8,128)(2,1)S(1)}, bf16[2,64,128]{2,1,0:T(8,128)(2,1)S(1)}, u32[]{:S(2)}, u32[]{:S(2)}) collective-permute-start(bf16[2,64,128]{2,1,0:T(8,128)(2,1)S(1)} %get-tuple-element.30), channel_id=1, source_target_pairs={{0,2},{1,3},{2,0},{3,1},{4,6},{5,7},{6,4},{7,5},{8,10},{9,11},{10,... | collective-permute-start | bytes 98312 | tf_op jit(solution)/shard_map/ppermute | solution.py:47
  4.8 1.5 %collective-permute-start.8 = (bf16[2,64,128]{2,1,0:T(8,128)(2,1)S(1)}, bf16[2,64,128]{2,1,0:T(8,128)(2,1)S(1)}, u32[]{:S(2)}, u32[]{:S(2)}) collective-permute-start(bf16[2,64,128]{2,1,0:T(8,128)(2,1)S(1)} %get-tuple-element.31), channel_id=1, source_target_pairs={{0,4},{1,5},{2,6},{3,7},{4,0},{5,1},{6,2},{7,3},{8,12},{9,13},{10,... | collective-permute-start | bytes 98312 | tf_op jit(solution)/shard_map/ppermute | solution.py:47
  6.4 0.6 %pack_weights.1.refs_0_ = bf16[336,128]{1,0:T(8,128)(2,1)S(1)} custom-call(bf16[12,27,192]{2,1,0:T(8,128)(2,1)S(1)} %copy-done.2), custom_call_target="tpu_custom_call" | custom-call | flops 6000000000 | bytes 210432 | tf_op jit(solution)/shard_map/pack_weights/pallas_call | solution.py:446
  6.9 2.1 %collective-permute-start.12 = (bf16[336,128]{1,0:T(8,128)(2,1)S(1)}, bf16[336,128]{1,0:T(8,128)(2,1)S(1)}, u32[]{:S(2)}, u32[]{:S(2)}) collective-permute-start(bf16[336,128]{1,0:T(8,128)(2,1)S(1)} %pack_weights.1.refs_0_), channel_id=1, source_target_pairs={{0,8},{1,9},{2,10},{3,11},{4,12},{5,13},{6,14},{7,15},{8,0},{9,1},... | collective-permute-start | bytes 258056 | tf_op jit(solution)/shard_map/ppermute | solution.py:47
  9.0 2.1 %collective-permute-done.9.refs_3_ = bf16[2,64,128]{2,1,0:T(8,128)(2,1)S(1)} collective-permute-done((bf16[2,64,128]{2,1,0:T(8,128)(2,1)S(1)}, bf16[2,64,128]{2,1,0:T(8,128)(2,1)S(1)}, u32[]{:S(2)}, u32[]{:S(2)}) %collective-permute-start.9) | collective-permute-done | bytes 32800 | tf_op jit(solution)/shard_map/ppermute | solution.py:47
  11.2 0.5 collective-permute-start.2
  11.7 1.6 %collective-permute-start.1 = (bf16[768,128]{1,0:T(8,128)(2,1)S(1)}, bf16[768,128]{1,0:T(8,128)(2,1)S(1)}, u32[]{:S(2)}, u32[]{:S(2)}) collective-permute-start(bf16[768,128]{1,0:T(8,128)(2,1)S(1)} %bitcast.5), channel_id=1, source_target_pairs={{0,4},{1,5},{2,6},{3,7},{4,0},{5,1},{6,2},{7,3},{8,12},{9,13},{10,... | collective-permute-start | bytes 589832 | tf_op jit(solution)/shard_map/ppermute | solution.py:47
  13.2 1.5 %collective-permute-start = (bf16[768,128]{1,0:T(8,128)(2,1)S(1)}, bf16[768,128]{1,0:T(8,128)(2,1)S(1)}, u32[]{:S(2)}, u32[]{:S(2)}) collective-permute-start(bf16[768,128]{1,0:T(8,128)(2,1)S(1)} %bitcast.6), channel_id=1, source_target_pairs={{0,2},{1,3},{2,0},{3,1},{4,6},{5,7},{6,4},{7,5},{8,10},{9,11},{10,... | collective-permute-start | bytes 589832 | tf_op jit(solution)/shard_map/ppermute | solution.py:47
  14.8 2.7 %collective-permute-start.13 = (bf16[672,128]{1,0:T(8,128)(2,1)S(1)}, bf16[672,128]{1,0:T(8,128)(2,1)S(1)}, u32[]{:S(2)}, u32[]{:S(2)}) collective-permute-start(bf16[672,128]{1,0:T(8,128)(2,1)S(1)} %join_kernel_rows.1), channel_id=1, source_target_pairs={{0,16},{1,17},{2,18},{3,19},{4,20},{5,21},{6,22},{7,23},{8,24},{9,... | collective-permute-start | bytes 516104 | tf_op jit(solution)/shard_map/ppermute | solution.py:47
  17.5 1.6 %collective-permute-start.11 = (bf16[176,128]{1,0:T(8,128)(2,1)S(1)}, bf16[176,128]{1,0:T(8,128)(2,1)S(1)}, u32[]{:S(2)}, u32[]{:S(2)}) collective-permute-start(bf16[176,128]{1,0:T(8,128)(2,1)S(1)} %get-tuple-element.35), channel_id=1, source_target_pairs={{0,8},{1,9},{2,10},{3,11},{4,12},{5,13},{6,14},{7,15},{8,0},{9,1},... | collective-permute-start | bytes 135176 | tf_op jit(solution)/shard_map/ppermute | solution.py:47
  19.1 2.7 %collective-permute-done.11.refs_1_.refs_6_ = bf16[176,128]{1,0:T(8,128)(2,1)S(1)} collective-permute-done((bf16[176,128]{1,0:T(8,128)(2,1)S(1)}, bf16[176,128]{1,0:T(8,128)(2,1)S(1)}, u32[]{:S(2)}, u32[]{:S(2)}) %collective-permute-start.11) | collective-permute-done | bytes 45088 | tf_op jit(solution)/shard_map/ppermute | solution.py:47
  21.9 2.4 %collective-permute-start.14 = (bf16[112,128]{1,0:T(8,128)(2,1)S(1)}, bf16[112,128]{1,0:T(8,128)(2,1)S(1)}, u32[]{:S(2)}, u32[]{:S(2)}) collective-permute-start(bf16[112,128]{1,0:T(8,128)(2,1)S(1)} %get-tuple-element.37), channel_id=1, source_target_pairs={{0,16},{1,17},{2,18},{3,19},{4,20},{5,21},{6,22},{7,23},{8,24},{9,... | collective-permute-start | bytes 86024 | tf_op jit(solution)/shard_map/ppermute | solution.py:47
  24.8 0.5 collective-permute-done.13.refs_2_
  25.7 1.3 %field_grad.2.refs_4_ = f32[10,64,768]{2,1,0:T(8,128)S(1)} custom-call(bf16[768,128]{1,0:T(8,128)(2,1)S(1)} %bitcast.8, bf16[768,128]{1,0:T(8,128)(2,1)S(1)} %collective-permute-done.refs_1_, bf16[768,128]{1,0:T(8,128)(2,1)S(1)} %collective-permute-done.1.refs_2_, bf16[768,128]{1,0:T(8,128)(2,1)S(1)} %collective-permute-done.2.refs_3_, ...), custom_call_target="tpu_custom_call" | custom-call | flops 1207959552 | bytes 3342336 | tf_op jit(solution)/shard_map/field_grad/pallas_call | solution.py:446
  27.1 1.2 %field_grad.3.refs_5_ = f32[10,64,768]{2,1,0:T(8,128)S(1)} custom-call(bf16[768,128]{1,0:T(8,128)(2,1)S(1)} %collective-permute-done.3.refs_0_.refs_4_, bf16[768,128]{1,0:T(8,128)(2,1)S(1)} %collective-permute-done.4.refs_1_.refs_5_, bf16[768,128]{1,0:T(8,128)(2,1)S(1)} %collective-permute-done.5.refs_2_.refs_6_, ...), custom_call_target="tpu_custom_call" | custom-call | flops 1207959552 | bytes 3342336 | tf_op jit(solution)/shard_map/field_grad/pallas_call | solution.py:446
  28.4 1.1 %norm_grad.1 = (f32[10,64,128]{2,1,0:T(8,128)S(1)}, bf16[4,10,16,128]{3,2,1,0:T(8,128)(2,1)S(1)}, f32[64,128]{1,0:T(8,128)S(1)}, f32[16,128]{1,0:T(8,128)S(1)}, ...) custom-call(bf16[8,64,128]{2,1,0:T(8,128)(2,1)S(1)} %get-tuple-element.33.refs_0_, ...), custom_call_target="tpu_custom_call" | custom-call | bytes 5053440 | tf_op jit(solution)/shard_map/norm_grad/pallas_call | solution.py:446
  29.5 0.9 %collective-permute-start.15 = (bf16[176,128]{1,0:T(8,128)(2,1)S(1)}, bf16[176,128]{1,0:T(8,128)(2,1)S(1)}, u32[]{:S(2)}, u32[]{:S(2)}) collective-permute-start(bf16[176,128]{1,0:T(8,128)(2,1)S(1)} %get-tuple-element.40), channel_id=1, source_target_pairs={{0,8},{1,9},{2,10},{3,11},{4,12},{5,13},{6,14},{7,15},{8,0},{9,1},... | collective-permute-start | bytes 135176 | tf_op jit(solution)/shard_map/ppermute | solution.py:47
  30.4 1.9 %sent_terms.1 = (bf16[336,128]{1,0:T(8,128)(2,1)S(1)}, bf16[336,128]{1,0:T(8,128)(2,1)S(1)}) custom-call(bf16[768,128]{1,0:T(8,128)(2,1)S(1)} %bitcast.9, bf16[768,128]{1,0:T(8,128)(2,1)S(1)} %collective-permute-done.refs_1_, bf16[768,128]{1,0:T(8,128)(2,1)S(1)} %collective-permute-done.1.refs_2_, bf16[768,128]{1,0:T(8,128)(2,1)S(1)} %collective-permute-done.2.refs_3_, ...), custom_call_target="tpu_custom_call" | custom-call | flops 1207959552 | bytes 1908736 | tf_op jit(solution)/shard_map/sent_terms/pallas_call | solution.py:446
  32.3 1.3 %collective-permute-start.22 = (bf16[336,128]{1,0:T(8,128)(2,1)S(1)}, bf16[336,128]{1,0:T(8,128)(2,1)S(1)}, u32[]{:S(2)}, u32[]{:S(2)}) collective-permute-start(bf16[336,128]{1,0:T(8,128)(2,1)S(1)} %get-tuple-element.55), channel_id=1, source_target_pairs={{0,8},{1,9},{2,10},{3,11},{4,12},{5,13},{6,14},{7,15},{8,0},{9,1},... | collective-permute-start | bytes 258056 | tf_op jit(solution)/shard_map/ppermute | solution.py:47
  33.6 2.5 %collective-permute-start.17 = (bf16[112,128]{1,0:T(8,128)(2,1)S(1)}, bf16[112,128]{1,0:T(8,128)(2,1)S(1)}, u32[]{:S(2)}, u32[]{:S(2)}) collective-permute-start(bf16[112,128]{1,0:T(8,128)(2,1)S(1)} %get-tuple-element.42.refs_9_.refs_1_), channel_id=1, source_target_pairs={{0,16},{1,17},{2,18},{3,19},{4,20},{5,21},{6,22},{7,23},{8,24},{9,... | collective-permute-start | bytes 86024 | tf_op jit(solution)/shard_map/ppermute | solution.py:47
  36.1 1.7 %collective-permute-start.16 = (bf16[336,128]{1,0:T(8,128)(2,1)S(1)}, bf16[336,128]{1,0:T(8,128)(2,1)S(1)}, u32[]{:S(2)}, u32[]{:S(2)}) collective-permute-start(bf16[336,128]{1,0:T(8,128)(2,1)S(1)} %pass_on.1), channel_id=1, source_target_pairs={{0,8},{1,9},{2,10},{3,11},{4,12},{5,13},{6,14},{7,15},{8,0},{9,1},... | collective-permute-start | bytes 258056 | tf_op jit(solution)/shard_map/ppermute | solution.py:47
  37.9 1.9 %kept_terms.1 = (f32[288,192]{1,0:T(8,128)S(1)}, f32[224,192]{1,0:T(8,128)S(1)}) custom-call(bf16[768,128]{1,0:T(8,128)(2,1)S(1)} %bitcast.10, bf16[768,128]{1,0:T(8,128)(2,1)S(1)} %collective-permute-done.refs_1_, bf16[768,128]{1,0:T(8,128)(2,1)S(1)} %collective-permute-done.1.refs_2_, bf16[768,128]{1,0:T(8,128)(2,1)S(1)} %collective-permute-done.2.refs_3_, ...), custom_call_target="tpu_custom_call" | custom-call | flops 1207959552 | bytes 2129920 | tf_op jit(solution)/shard_map/kept_terms/pallas_call | solution.py:446
  39.9 0.6 %collective-permute-start.18 = (bf16[2,64,128]{2,1,0:T(8,128)(2,1)S(1)}, bf16[2,64,128]{2,1,0:T(8,128)(2,1)S(1)}, u32[]{:S(2)}, u32[]{:S(2)}) collective-permute-start(bf16[2,64,128]{2,1,0:T(8,128)(2,1)S(1)} %get-tuple-element.49), channel_id=1, source_target_pairs={{0,2},{1,3},{2,0},{3,1},{4,6},{5,7},{6,4},{7,5},{8,10},{9,11},{10,... | collective-permute-start | bytes 98312 | tf_op jit(solution)/shard_map/ppermute | solution.py:47
  40.5 0.5 %collective-permute-start.19 = (bf16[2,64,128]{2,1,0:T(8,128)(2,1)S(1)}, bf16[2,64,128]{2,1,0:T(8,128)(2,1)S(1)}, u32[]{:S(2)}, u32[]{:S(2)}) collective-permute-start(bf16[2,64,128]{2,1,0:T(8,128)(2,1)S(1)} %get-tuple-element.50), channel_id=1, source_target_pairs={{0,4},{1,5},{2,6},{3,7},{4,0},{5,1},{6,2},{7,3},{8,12},{9,13},{10,... | collective-permute-start | bytes 98312 | tf_op jit(solution)/shard_map/ppermute | solution.py:47
  41.0 2.5 %collective-permute-start.20 = (bf16[2,64,128]{2,1,0:T(8,128)(2,1)S(1)}, bf16[2,64,128]{2,1,0:T(8,128)(2,1)S(1)}, u32[]{:S(2)}, u32[]{:S(2)}) collective-permute-start(bf16[2,64,128]{2,1,0:T(8,128)(2,1)S(1)} %get-tuple-element.51), channel_id=1, source_target_pairs={{0,6},{1,7},{2,4},{3,5},{4,2},{5,3},{6,0},{7,1},{8,14},{9,15},{10,... | collective-permute-start | bytes 98312 | tf_op jit(solution)/shard_map/ppermute | solution.py:47
  43.7 1.1 %collective-permute-start.23 = (bf16[336,128]{1,0:T(8,128)(2,1)S(1)}, bf16[336,128]{1,0:T(8,128)(2,1)S(1)}, u32[]{:S(2)}, u32[]{:S(2)}) collective-permute-start(bf16[336,128]{1,0:T(8,128)(2,1)S(1)} %add_terms.1), channel_id=1, source_target_pairs={{0,16},{1,17},{2,18},{3,19},{4,20},{5,21},{6,22},{7,23},{8,24},{9,... | collective-permute-start | bytes 258056 | tf_op jit(solution)/shard_map/ppermute | solution.py:47
  44.8 1.1 %collective-permute-done.20.refs_3_.refs_5_ = bf16[2,64,128]{2,1,0:T(8,128)(2,1)S(1)} collective-permute-done((bf16[2,64,128]{2,1,0:T(8,128)(2,1)S(1)}, bf16[2,64,128]{2,1,0:T(8,128)(2,1)S(1)}, u32[]{:S(2)}, u32[]{:S(2)}) %collective-permute-start.20) | collective-permute-done | bytes 32800 | tf_op jit(solution)/shard_map/ppermute | solution.py:47
  45.9 1.2 %collective-permute-done.21.refs_6_ = bf16[4,64,128]{2,1,0:T(8,128)(2,1)S(1)} collective-permute-done((bf16[4,64,128]{2,1,0:T(8,128)(2,1)S(1)}, bf16[4,64,128]{2,1,0:T(8,128)(2,1)S(1)}, u32[]{:S(2)}, u32[]{:S(2)}) %collective-permute-start.21) | collective-permute-done | bytes 65568 | tf_op jit(solution)/shard_map/ppermute | solution.py:47
  47.1 1.0 %unpack_acts.1 = (bf16[2,1,64,384]{3,2,1,0:T(8,128)(2,1)}, f32[12,32,192]{2,1,0:T(8,128)S(1)}) custom-call(f32[288,192]{1,0:T(8,128)S(1)} %get-tuple-element.43.refs_6_.refs_0_, bf16[336,128]{1,0:T(8,128)(2,1)S(1)} %collective-permute-done.16.refs_1_.refs_2_, bf16[2,64,128]{2,1,0:T(8,128)(2,1)S(1)} %get-tuple-element.48.refs_0_.refs_2_, ...), custom_call_target="tpu_custom_call" | custom-call | bytes 897024 | tf_op jit(solution)/shard_map/unpack_acts/pallas_call | solution.py:446
  48.1 1.0 %collective-permute-done.23.refs_1_ = bf16[336,128]{1,0:T(8,128)(2,1)S(1)} collective-permute-done((bf16[336,128]{1,0:T(8,128)(2,1)S(1)}, bf16[336,128]{1,0:T(8,128)(2,1)S(1)}, u32[]{:S(2)}, u32[]{:S(2)}) %collective-permute-start.23) | collective-permute-done | bytes 86048 | tf_op jit(solution)/shard_map/ppermute | solution.py:47
  49.1 1.0 %unpack_weights.1 = f32[12,27,192]{2,1,0:T(8,128)} custom-call(f32[12,32,192]{2,1,0:T(8,128)S(1)} %get-tuple-element.53.refs_0_, bf16[336,128]{1,0:T(8,128)(2,1)S(1)} %collective-permute-done.23.refs_1_), custom_call_target="tpu_custom_call" | custom-call | bytes 629760 | tf_op jit(solution)/shard_map/unpack_weights/pallas_call | solution.py:446
  (45 shorter events, 1.7 us)
Async XLA Ops:
  0.6 0.9 %copy-start.4 = (bf16[2,1,64,384]{3,2,1,0:T(8,128)(2,1)S(1)}, bf16[2,1,64,384]{3,2,1,0:T(8,128)(2,1)}, u32[]{:S(2)}) copy-start(bf16[2,1,64,384]{3,2,1,0:T(8,128)(2,1)} %param.5) | copy-start | bytes 294916
  1.5 4.8 %copy-start.2 = (bf16[12,27,192]{2,1,0:T(8,128)(2,1)S(1)}, bf16[12,27,192]{2,1,0:T(8,128)(2,1)}, u32[]{:S(2)}) copy-start(bf16[12,27,192]{2,1,0:T(8,128)(2,1)} %refs_0_.1) | copy-start | bytes 373252
  1.8 7.2 %collective-permute-start.7 = (bf16[2,64,128]{2,1,0:T(8,128)(2,1)S(1)}, bf16[2,64,128]{2,1,0:T(8,128)(2,1)S(1)}, u32[]{:S(2)}, u32[]{:S(2)}) collective-permute-start(bf16[2,64,128]{2,1,0:T(8,128)(2,1)S(1)} %get-tuple-element.30), channel_id=1, source_target_pairs={{0,2},{1,3},{2,0},{3,1},{4,6},{5,7},{6,4},{7,5},{8,10},{9,11},{10,... | collective-permute-start | bytes 98312 | tf_op jit(solution)/shard_map/ppermute | solution.py:47
  4.8 4.2 %collective-permute-start.8 = (bf16[2,64,128]{2,1,0:T(8,128)(2,1)S(1)}, bf16[2,64,128]{2,1,0:T(8,128)(2,1)S(1)}, u32[]{:S(2)}, u32[]{:S(2)}) collective-permute-start(bf16[2,64,128]{2,1,0:T(8,128)(2,1)S(1)} %get-tuple-element.31), channel_id=1, source_target_pairs={{0,4},{1,5},{2,6},{3,7},{4,0},{5,1},{6,2},{7,3},{8,12},{9,13},{10,... | collective-permute-start | bytes 98312 | tf_op jit(solution)/shard_map/ppermute | solution.py:47
  6.3 4.8 %copy-start.3 = (bf16[2,2,128,192]{2,3,1,0:T(8,128)(2,1)S(1)}, bf16[2,2,128,192]{2,3,1,0:T(8,128)(2,1)}, u32[]{:S(2)}) copy-start(bf16[2,2,128,192]{2,3,1,0:T(8,128)(2,1)} %param.9) | copy-start | bytes 589828
  6.3 4.8 %collective-permute-start.9 = (bf16[2,64,128]{2,1,0:T(8,128)(2,1)S(1)}, bf16[2,64,128]{2,1,0:T(8,128)(2,1)S(1)}, u32[]{:S(2)}, u32[]{:S(2)}) collective-permute-start(bf16[2,64,128]{2,1,0:T(8,128)(2,1)S(1)} %get-tuple-element.32), channel_id=1, source_target_pairs={{0,6},{1,7},{2,4},{3,5},{4,2},{5,3},{6,0},{7,1},{8,14},{9,15},{10,... | collective-permute-start | bytes 98312 | tf_op jit(solution)/shard_map/ppermute | solution.py:47
  6.9 7.8 %collective-permute-start.12 = (bf16[336,128]{1,0:T(8,128)(2,1)S(1)}, bf16[336,128]{1,0:T(8,128)(2,1)S(1)}, u32[]{:S(2)}, u32[]{:S(2)}) collective-permute-start(bf16[336,128]{1,0:T(8,128)(2,1)S(1)} %pack_weights.1.refs_0_), channel_id=1, source_target_pairs={{0,8},{1,9},{2,10},{3,11},{4,12},{5,13},{6,14},{7,15},{8,0},{9,1},... | collective-permute-start | bytes 258056 | tf_op jit(solution)/shard_map/ppermute | solution.py:47
  11.2 6.3 %collective-permute-start.10 = (bf16[4,64,128]{2,1,0:T(8,128)(2,1)S(1)}, bf16[4,64,128]{2,1,0:T(8,128)(2,1)S(1)}, u32[]{:S(2)}, u32[]{:S(2)}) collective-permute-start(bf16[4,64,128]{2,1,0:T(8,128)(2,1)S(1)} %cross_acts.1), channel_id=1, source_target_pairs={{0,1},{1,0},{2,3},{3,2},{4,5},{5,4},{6,7},{7,6},{8,9},{9,8},{10,11... | collective-permute-start | bytes 196616 | tf_op jit(solution)/shard_map/ppermute | solution.py:47
  11.2 10.7 %collective-permute-start.2 = (bf16[768,128]{1,0:T(8,128)(2,1)S(1)}, bf16[768,128]{1,0:T(8,128)(2,1)S(1)}, u32[]{:S(2)}, u32[]{:S(2)}) collective-permute-start(bf16[768,128]{1,0:T(8,128)(2,1)S(1)} %bitcast.4), channel_id=1, source_target_pairs={{0,6},{1,7},{2,4},{3,5},{4,2},{5,3},{6,0},{7,1},{8,14},{9,15},{10,... | collective-permute-start | bytes 589832 | tf_op jit(solution)/shard_map/ppermute | solution.py:47
  11.7 12.6 %collective-permute-start.1 = (bf16[768,128]{1,0:T(8,128)(2,1)S(1)}, bf16[768,128]{1,0:T(8,128)(2,1)S(1)}, u32[]{:S(2)}, u32[]{:S(2)}) collective-permute-start(bf16[768,128]{1,0:T(8,128)(2,1)S(1)} %bitcast.5), channel_id=1, source_target_pairs={{0,4},{1,5},{2,6},{3,7},{4,0},{5,1},{6,2},{7,3},{8,12},{9,13},{10,... | collective-permute-start | bytes 589832 | tf_op jit(solution)/shard_map/ppermute | solution.py:47
  13.2 11.3 %collective-permute-start = (bf16[768,128]{1,0:T(8,128)(2,1)S(1)}, bf16[768,128]{1,0:T(8,128)(2,1)S(1)}, u32[]{:S(2)}, u32[]{:S(2)}) collective-permute-start(bf16[768,128]{1,0:T(8,128)(2,1)S(1)} %bitcast.6), channel_id=1, source_target_pairs={{0,2},{1,3},{2,0},{3,1},{4,6},{5,7},{6,4},{7,5},{8,10},{9,11},{10,... | collective-permute-start | bytes 589832 | tf_op jit(solution)/shard_map/ppermute | solution.py:47
  14.8 10.5 %collective-permute-start.13 = (bf16[672,128]{1,0:T(8,128)(2,1)S(1)}, bf16[672,128]{1,0:T(8,128)(2,1)S(1)}, u32[]{:S(2)}, u32[]{:S(2)}) collective-permute-start(bf16[672,128]{1,0:T(8,128)(2,1)S(1)} %join_kernel_rows.1), channel_id=1, source_target_pairs={{0,16},{1,17},{2,18},{3,19},{4,20},{5,21},{6,22},{7,23},{8,24},{9,... | collective-permute-start | bytes 516104 | tf_op jit(solution)/shard_map/ppermute | solution.py:47
  17.5 4.3 %collective-permute-start.11 = (bf16[176,128]{1,0:T(8,128)(2,1)S(1)}, bf16[176,128]{1,0:T(8,128)(2,1)S(1)}, u32[]{:S(2)}, u32[]{:S(2)}) collective-permute-start(bf16[176,128]{1,0:T(8,128)(2,1)S(1)} %get-tuple-element.35), channel_id=1, source_target_pairs={{0,8},{1,9},{2,10},{3,11},{4,12},{5,13},{6,14},{7,15},{8,0},{9,1},... | collective-permute-start | bytes 135176 | tf_op jit(solution)/shard_map/ppermute | solution.py:47
  21.8 5.2 %collective-permute-start.3 = (bf16[768,128]{1,0:T(8,128)(2,1)S(1)}, bf16[768,128]{1,0:T(8,128)(2,1)S(1)}, u32[]{:S(2)}, u32[]{:S(2)}) collective-permute-start(bf16[768,128]{1,0:T(8,128)(2,1)S(1)} %bitcast.7), channel_id=1, source_target_pairs={{0,1},{1,0},{2,3},{3,2},{4,5},{5,4},{6,7},{7,6},{8,9},{9,8},{10,11... | collective-permute-start | bytes 589832 | tf_op jit(solution)/shard_map/ppermute | solution.py:47
  21.9 6.5 %collective-permute-start.14 = (bf16[112,128]{1,0:T(8,128)(2,1)S(1)}, bf16[112,128]{1,0:T(8,128)(2,1)S(1)}, u32[]{:S(2)}, u32[]{:S(2)}) collective-permute-start(bf16[112,128]{1,0:T(8,128)(2,1)S(1)} %get-tuple-element.37), channel_id=1, source_target_pairs={{0,16},{1,17},{2,18},{3,19},{4,20},{5,21},{6,22},{7,23},{8,24},{9,... | collective-permute-start | bytes 86024 | tf_op jit(solution)/shard_map/ppermute | solution.py:47
  24.3 2.8 %collective-permute-start.6 = (bf16[768,128]{1,0:T(8,128)(2,1)S(1)}, bf16[768,128]{1,0:T(8,128)(2,1)S(1)}, u32[]{:S(2)}, u32[]{:S(2)}) collective-permute-start(bf16[768,128]{1,0:T(8,128)(2,1)S(1)} %collective-permute-done.2.refs_3_), channel_id=1, source_target_pairs={{0,1},{1,0},{2,3},{3,2},{4,5},{5,4},{6,7},{7,6},{8,9},{9,8},{10,11... | collective-permute-start | bytes 589832 | tf_op jit(solution)/shard_map/ppermute | solution.py:47
  24.5 2.5 %collective-permute-start.5 = (bf16[768,128]{1,0:T(8,128)(2,1)S(1)}, bf16[768,128]{1,0:T(8,128)(2,1)S(1)}, u32[]{:S(2)}, u32[]{:S(2)}) collective-permute-start(bf16[768,128]{1,0:T(8,128)(2,1)S(1)} %collective-permute-done.1.refs_2_), channel_id=1, source_target_pairs={{0,1},{1,0},{2,3},{3,2},{4,5},{5,4},{6,7},{7,6},{8,9},{9,8},{10,11... | collective-permute-start | bytes 589832 | tf_op jit(solution)/shard_map/ppermute | solution.py:47
  25.3 1.8 %collective-permute-start.4 = (bf16[768,128]{1,0:T(8,128)(2,1)S(1)}, bf16[768,128]{1,0:T(8,128)(2,1)S(1)}, u32[]{:S(2)}, u32[]{:S(2)}) collective-permute-start(bf16[768,128]{1,0:T(8,128)(2,1)S(1)} %collective-permute-done.refs_1_), channel_id=1, source_target_pairs={{0,1},{1,0},{2,3},{3,2},{4,5},{5,4},{6,7},{7,6},{8,9},{9,8},{10,11... | collective-permute-start | bytes 589832 | tf_op jit(solution)/shard_map/ppermute | solution.py:47
  27.0 1.3 %copy-start = (f32[384]{0:T(512)S(1)}, f32[384]{0:T(512)}, u32[]{:S(2)}) copy-start(f32[384]{0:T(512)} %refs_2_.1) | copy-start | bytes 4612
  27.0 1.3 %copy-start.1 = (f32[384]{0:T(512)S(1)}, f32[384]{0:T(512)}, u32[]{:S(2)}) copy-start(f32[384]{0:T(512)} %refs_3_.1) | copy-start | bytes 4612
  29.5 4.1 %collective-permute-start.15 = (bf16[176,128]{1,0:T(8,128)(2,1)S(1)}, bf16[176,128]{1,0:T(8,128)(2,1)S(1)}, u32[]{:S(2)}, u32[]{:S(2)}) collective-permute-start(bf16[176,128]{1,0:T(8,128)(2,1)S(1)} %get-tuple-element.40), channel_id=1, source_target_pairs={{0,8},{1,9},{2,10},{3,11},{4,12},{5,13},{6,14},{7,15},{8,0},{9,1},... | collective-permute-start | bytes 135176 | tf_op jit(solution)/shard_map/ppermute | solution.py:47
  32.3 11.2 %collective-permute-start.22 = (bf16[336,128]{1,0:T(8,128)(2,1)S(1)}, bf16[336,128]{1,0:T(8,128)(2,1)S(1)}, u32[]{:S(2)}, u32[]{:S(2)}) collective-permute-start(bf16[336,128]{1,0:T(8,128)(2,1)S(1)} %get-tuple-element.55), channel_id=1, source_target_pairs={{0,8},{1,9},{2,10},{3,11},{4,12},{5,13},{6,14},{7,15},{8,0},{9,1},... | collective-permute-start | bytes 258056 | tf_op jit(solution)/shard_map/ppermute | solution.py:47
  33.6 6.2 %collective-permute-start.17 = (bf16[112,128]{1,0:T(8,128)(2,1)S(1)}, bf16[112,128]{1,0:T(8,128)(2,1)S(1)}, u32[]{:S(2)}, u32[]{:S(2)}) collective-permute-start(bf16[112,128]{1,0:T(8,128)(2,1)S(1)} %get-tuple-element.42.refs_9_.refs_1_), channel_id=1, source_target_pairs={{0,16},{1,17},{2,18},{3,19},{4,20},{5,21},{6,22},{7,23},{8,24},{9,... | collective-permute-start | bytes 86024 | tf_op jit(solution)/shard_map/ppermute | solution.py:47
  36.1 7.4 %collective-permute-start.16 = (bf16[336,128]{1,0:T(8,128)(2,1)S(1)}, bf16[336,128]{1,0:T(8,128)(2,1)S(1)}, u32[]{:S(2)}, u32[]{:S(2)}) collective-permute-start(bf16[336,128]{1,0:T(8,128)(2,1)S(1)} %pass_on.1), channel_id=1, source_target_pairs={{0,8},{1,9},{2,10},{3,11},{4,12},{5,13},{6,14},{7,15},{8,0},{9,1},... | collective-permute-start | bytes 258056 | tf_op jit(solution)/shard_map/ppermute | solution.py:47
  39.9 4.8 %collective-permute-start.18 = (bf16[2,64,128]{2,1,0:T(8,128)(2,1)S(1)}, bf16[2,64,128]{2,1,0:T(8,128)(2,1)S(1)}, u32[]{:S(2)}, u32[]{:S(2)}) collective-permute-start(bf16[2,64,128]{2,1,0:T(8,128)(2,1)S(1)} %get-tuple-element.49), channel_id=1, source_target_pairs={{0,2},{1,3},{2,0},{3,1},{4,6},{5,7},{6,4},{7,5},{8,10},{9,11},{10,... | collective-permute-start | bytes 98312 | tf_op jit(solution)/shard_map/ppermute | solution.py:47
  40.5 4.3 %collective-permute-start.19 = (bf16[2,64,128]{2,1,0:T(8,128)(2,1)S(1)}, bf16[2,64,128]{2,1,0:T(8,128)(2,1)S(1)}, u32[]{:S(2)}, u32[]{:S(2)}) collective-permute-start(bf16[2,64,128]{2,1,0:T(8,128)(2,1)S(1)} %get-tuple-element.50), channel_id=1, source_target_pairs={{0,4},{1,5},{2,6},{3,7},{4,0},{5,1},{6,2},{7,3},{8,12},{9,13},{10,... | collective-permute-start | bytes 98312 | tf_op jit(solution)/shard_map/ppermute | solution.py:47
  41.0 4.8 %collective-permute-start.20 = (bf16[2,64,128]{2,1,0:T(8,128)(2,1)S(1)}, bf16[2,64,128]{2,1,0:T(8,128)(2,1)S(1)}, u32[]{:S(2)}, u32[]{:S(2)}) collective-permute-start(bf16[2,64,128]{2,1,0:T(8,128)(2,1)S(1)} %get-tuple-element.51), channel_id=1, source_target_pairs={{0,6},{1,7},{2,4},{3,5},{4,2},{5,3},{6,0},{7,1},{8,14},{9,15},{10,... | collective-permute-start | bytes 98312 | tf_op jit(solution)/shard_map/ppermute | solution.py:47
  43.7 5.4 %collective-permute-start.23 = (bf16[336,128]{1,0:T(8,128)(2,1)S(1)}, bf16[336,128]{1,0:T(8,128)(2,1)S(1)}, u32[]{:S(2)}, u32[]{:S(2)}) collective-permute-start(bf16[336,128]{1,0:T(8,128)(2,1)S(1)} %add_terms.1), channel_id=1, source_target_pairs={{0,16},{1,17},{2,18},{3,19},{4,20},{5,21},{6,22},{7,23},{8,24},{9,... | collective-permute-start | bytes 258056 | tf_op jit(solution)/shard_map/ppermute | solution.py:47
  45.9 1.3 %collective-permute-start.21 = (bf16[4,64,128]{2,1,0:T(8,128)(2,1)S(1)}, bf16[4,64,128]{2,1,0:T(8,128)(2,1)S(1)}, u32[]{:S(2)}, u32[]{:S(2)}) collective-permute-start(bf16[4,64,128]{2,1,0:T(8,128)(2,1)S(1)} %cross_grads.1), channel_id=1, source_target_pairs={{0,1},{1,0},{2,3},{3,2},{4,5},{5,4},{6,7},{7,6},{8,9},{9,8},{10,11... | collective-permute-start | bytes 196616 | tf_op jit(solution)/shard_map/ppermute | solution.py:47

commit v7 on v6

--- a/solution.py
+++ b/solution.py
@@ -592,7 +592,8 @@
         [sums, grad, normed, inv] + received,
         after=[own],
     )
-    direct = [sends[0]] + [swap(sends[k], 2 * k) for k in range(1, g.pairs)]
+    direct = [swap(sends[k], 2 * k) for k in range(g.pairs - 1, 0, -1)]
+    direct = [sends[0]] + direct[::-1]
     near = swap(pass_on(g, near, [send]), g.inner)
     (far,) = call(g, add_terms_kernel, "add_terms", [packed_shape], [keep, far], after=[near])
     terms = [near, swap(far, 2 * g.inner)]

time: 50.3 us -> 50.3 us (level)
  no operation moved by 1% of the time
where the time goes in v7:
time: 50.3 us; the launch traced here: 50.1 us
  starting transfers between devices  28.5 us (57%)
  Pallas kernels  11.2 us (22%)
  waiting for transfers between devices  8.69 us (17%)
  local copies, waits for them, and re-layouts  0.91 us (2%)
  between operations  0.83 us (2%)
    ppermute x24, starting transfers between devices, swap(): return lax.ppermute(value, 'tile', [(i, i ^ mask) for i in range(count)])  28.5 us
    pallas_call x19, Pallas kernels, call(): pl.pallas_call(lambda *refs: kernel(g, *refs[:count], *refs[rest:]), out_...  11.2 us
    ppermute x24, waiting for transfers between devices, swap(): return lax.ppermute(value, 'tile', [(i, i ^ mask) for i in range(count)])  8.69 us
  transfers between devices with their start and end apart: 24, of which 6 were waited for; matrix products, arithmetic and copies ran while one was open for 0% of the time, Pallas kernels for 17%

profile of v7, /device:TPU:0, one launch (start us, length us, event | category | flops | bytes accessed | tf_op | source)
XLA Modules:
  0.0 50.1 jit_solution(17598665475723048509)
XLA Ops:
  0.6 0.9 %copy-done.4 = bf16[2,1,64,384]{3,2,1,0:T(8,128)(2,1)S(1)} copy-done((bf16[2,1,64,384]{3,2,1,0:T(8,128)(2,1)S(1)}, bf16[2,1,64,384]{3,2,1,0:T(8,128)(2,1)}, u32[]{:S(2)}) %copy-start.4) | copy-done | bytes 98328
  1.8 3.0 %collective-permute-start.7 = (bf16[2,64,128]{2,1,0:T(8,128)(2,1)S(1)}, bf16[2,64,128]{2,1,0:T(8,128)(2,1)S(1)}, u32[]{:S(2)}, u32[]{:S(2)}) collective-permute-start(bf16[2,64,128]{2,1,0:T(8,128)(2,1)S(1)} %get-tuple-element.30), channel_id=1, source_target_pairs={{0,2},{1,3},{2,0},{3,1},{4,6},{5,7},{6,4},{7,5},{8,10},{9,11},{10,... | collective-permute-start | bytes 98312 | tf_op jit(solution)/shard_map/ppermute | solution.py:47
  4.8 1.5 %collective-permute-start.8 = (bf16[2,64,128]{2,1,0:T(8,128)(2,1)S(1)}, bf16[2,64,128]{2,1,0:T(8,128)(2,1)S(1)}, u32[]{:S(2)}, u32[]{:S(2)}) collective-permute-start(bf16[2,64,128]{2,1,0:T(8,128)(2,1)S(1)} %get-tuple-element.31), channel_id=1, source_target_pairs={{0,4},{1,5},{2,6},{3,7},{4,0},{5,1},{6,2},{7,3},{8,12},{9,13},{10,... | collective-permute-start | bytes 98312 | tf_op jit(solution)/shard_map/ppermute | solution.py:47
  6.4 0.6 %pack_weights.1.refs_0_ = bf16[336,128]{1,0:T(8,128)(2,1)S(1)} custom-call(bf16[12,27,192]{2,1,0:T(8,128)(2,1)S(1)} %copy-done.2), custom_call_target="tpu_custom_call" | custom-call | flops 6000000000 | bytes 210432 | tf_op jit(solution)/shard_map/pack_weights/pallas_call | solution.py:446
  6.9 2.1 %collective-permute-start.12 = (bf16[336,128]{1,0:T(8,128)(2,1)S(1)}, bf16[336,128]{1,0:T(8,128)(2,1)S(1)}, u32[]{:S(2)}, u32[]{:S(2)}) collective-permute-start(bf16[336,128]{1,0:T(8,128)(2,1)S(1)} %pack_weights.1.refs_0_), channel_id=1, source_target_pairs={{0,8},{1,9},{2,10},{3,11},{4,12},{5,13},{6,14},{7,15},{8,0},{9,1},... | collective-permute-start | bytes 258056 | tf_op jit(solution)/shard_map/ppermute | solution.py:47
  9.0 2.1 %collective-permute-done.9.refs_3_ = bf16[2,64,128]{2,1,0:T(8,128)(2,1)S(1)} collective-permute-done((bf16[2,64,128]{2,1,0:T(8,128)(2,1)S(1)}, bf16[2,64,128]{2,1,0:T(8,128)(2,1)S(1)}, u32[]{:S(2)}, u32[]{:S(2)}) %collective-permute-start.9) | collective-permute-done | bytes 32800 | tf_op jit(solution)/shard_map/ppermute | solution.py:47
  11.2 0.5 collective-permute-start.2
  11.7 1.6 %collective-permute-start.1 = (bf16[768,128]{1,0:T(8,128)(2,1)S(1)}, bf16[768,128]{1,0:T(8,128)(2,1)S(1)}, u32[]{:S(2)}, u32[]{:S(2)}) collective-permute-start(bf16[768,128]{1,0:T(8,128)(2,1)S(1)} %bitcast.5), channel_id=1, source_target_pairs={{0,4},{1,5},{2,6},{3,7},{4,0},{5,1},{6,2},{7,3},{8,12},{9,13},{10,... | collective-permute-start | bytes 589832 | tf_op jit(solution)/shard_map/ppermute | solution.py:47
  13.2 1.5 %collective-permute-start = (bf16[768,128]{1,0:T(8,128)(2,1)S(1)}, bf16[768,128]{1,0:T(8,128)(2,1)S(1)}, u32[]{:S(2)}, u32[]{:S(2)}) collective-permute-start(bf16[768,128]{1,0:T(8,128)(2,1)S(1)} %bitcast.6), channel_id=1, source_target_pairs={{0,2},{1,3},{2,0},{3,1},{4,6},{5,7},{6,4},{7,5},{8,10},{9,11},{10,... | collective-permute-start | bytes 589832 | tf_op jit(solution)/shard_map/ppermute | solution.py:47
  14.8 2.7 %collective-permute-start.13 = (bf16[672,128]{1,0:T(8,128)(2,1)S(1)}, bf16[672,128]{1,0:T(8,128)(2,1)S(1)}, u32[]{:S(2)}, u32[]{:S(2)}) collective-permute-start(bf16[672,128]{1,0:T(8,128)(2,1)S(1)} %join_kernel_rows.1), channel_id=1, source_target_pairs={{0,16},{1,17},{2,18},{3,19},{4,20},{5,21},{6,22},{7,23},{8,24},{9,... | collective-permute-start | bytes 516104 | tf_op jit(solution)/shard_map/ppermute | solution.py:47
  17.5 1.6 %collective-permute-start.11 = (bf16[176,128]{1,0:T(8,128)(2,1)S(1)}, bf16[176,128]{1,0:T(8,128)(2,1)S(1)}, u32[]{:S(2)}, u32[]{:S(2)}) collective-permute-start(bf16[176,128]{1,0:T(8,128)(2,1)S(1)} %get-tuple-element.35), channel_id=1, source_target_pairs={{0,8},{1,9},{2,10},{3,11},{4,12},{5,13},{6,14},{7,15},{8,0},{9,1},... | collective-permute-start | bytes 135176 | tf_op jit(solution)/shard_map/ppermute | solution.py:47
  19.1 2.7 %collective-permute-done.11.refs_1_.refs_6_ = bf16[176,128]{1,0:T(8,128)(2,1)S(1)} collective-permute-done((bf16[176,128]{1,0:T(8,128)(2,1)S(1)}, bf16[176,128]{1,0:T(8,128)(2,1)S(1)}, u32[]{:S(2)}, u32[]{:S(2)}) %collective-permute-start.11) | collective-permute-done | bytes 45088 | tf_op jit(solution)/shard_map/ppermute | solution.py:47
  21.9 2.4 %collective-permute-start.14 = (bf16[112,128]{1,0:T(8,128)(2,1)S(1)}, bf16[112,128]{1,0:T(8,128)(2,1)S(1)}, u32[]{:S(2)}, u32[]{:S(2)}) collective-permute-start(bf16[112,128]{1,0:T(8,128)(2,1)S(1)} %get-tuple-element.37), channel_id=1, source_target_pairs={{0,16},{1,17},{2,18},{3,19},{4,20},{5,21},{6,22},{7,23},{8,24},{9,... | collective-permute-start | bytes 86024 | tf_op jit(solution)/shard_map/ppermute | solution.py:47
  24.8 0.5 collective-permute-done.13.refs_2_
  25.7 1.3 %field_grad.2.refs_4_ = f32[10,64,768]{2,1,0:T(8,128)S(1)} custom-call(bf16[768,128]{1,0:T(8,128)(2,1)S(1)} %bitcast.8, bf16[768,128]{1,0:T(8,128)(2,1)S(1)} %collective-permute-done.refs_1_, bf16[768,128]{1,0:T(8,128)(2,1)S(1)} %collective-permute-done.1.refs_2_, bf16[768,128]{1,0:T(8,128)(2,1)S(1)} %collective-permute-done.2.refs_3_, ...), custom_call_target="tpu_custom_call" | custom-call | flops 1207959552 | bytes 3342336 | tf_op jit(solution)/shard_map/field_grad/pallas_call | solution.py:446
  27.1 1.2 %field_grad.3.refs_5_ = f32[10,64,768]{2,1,0:T(8,128)S(1)} custom-call(bf16[768,128]{1,0:T(8,128)(2,1)S(1)} %collective-permute-done.3.refs_0_.refs_4_, bf16[768,128]{1,0:T(8,128)(2,1)S(1)} %collective-permute-done.4.refs_1_.refs_5_, bf16[768,128]{1,0:T(8,128)(2,1)S(1)} %collective-permute-done.5.refs_2_.refs_6_, ...), custom_call_target="tpu_custom_call" | custom-call | flops 1207959552 | bytes 3342336 | tf_op jit(solution)/shard_map/field_grad/pallas_call | solution.py:446
  28.4 1.1 %norm_grad.1 = (f32[10,64,128]{2,1,0:T(8,128)S(1)}, bf16[4,10,16,128]{3,2,1,0:T(8,128)(2,1)S(1)}, f32[64,128]{1,0:T(8,128)S(1)}, f32[16,128]{1,0:T(8,128)S(1)}, ...) custom-call(bf16[8,64,128]{2,1,0:T(8,128)(2,1)S(1)} %get-tuple-element.33.refs_0_, ...), custom_call_target="tpu_custom_call" | custom-call | bytes 5053440 | tf_op jit(solution)/shard_map/norm_grad/pallas_call | solution.py:446
  29.5 0.9 %collective-permute-start.15 = (bf16[176,128]{1,0:T(8,128)(2,1)S(1)}, bf16[176,128]{1,0:T(8,128)(2,1)S(1)}, u32[]{:S(2)}, u32[]{:S(2)}) collective-permute-start(bf16[176,128]{1,0:T(8,128)(2,1)S(1)} %get-tuple-element.40), channel_id=1, source_target_pairs={{0,8},{1,9},{2,10},{3,11},{4,12},{5,13},{6,14},{7,15},{8,0},{9,1},... | collective-permute-start | bytes 135176 | tf_op jit(solution)/shard_map/ppermute | solution.py:47
  30.4 1.9 %sent_terms.1 = (bf16[336,128]{1,0:T(8,128)(2,1)S(1)}, bf16[336,128]{1,0:T(8,128)(2,1)S(1)}) custom-call(bf16[768,128]{1,0:T(8,128)(2,1)S(1)} %bitcast.9, bf16[768,128]{1,0:T(8,128)(2,1)S(1)} %collective-permute-done.refs_1_, bf16[768,128]{1,0:T(8,128)(2,1)S(1)} %collective-permute-done.1.refs_2_, bf16[768,128]{1,0:T(8,128)(2,1)S(1)} %collective-permute-done.2.refs_3_, ...), custom_call_target="tpu_custom_call" | custom-call | flops 1207959552 | bytes 1908736 | tf_op jit(solution)/shard_map/sent_terms/pallas_call | solution.py:446
  32.3 1.3 %collective-permute-start.22 = (bf16[336,128]{1,0:T(8,128)(2,1)S(1)}, bf16[336,128]{1,0:T(8,128)(2,1)S(1)}, u32[]{:S(2)}, u32[]{:S(2)}) collective-permute-start(bf16[336,128]{1,0:T(8,128)(2,1)S(1)} %get-tuple-element.55), channel_id=1, source_target_pairs={{0,8},{1,9},{2,10},{3,11},{4,12},{5,13},{6,14},{7,15},{8,0},{9,1},... | collective-permute-start | bytes 258056 | tf_op jit(solution)/shard_map/ppermute | solution.py:47
  33.6 2.5 %collective-permute-start.17 = (bf16[112,128]{1,0:T(8,128)(2,1)S(1)}, bf16[112,128]{1,0:T(8,128)(2,1)S(1)}, u32[]{:S(2)}, u32[]{:S(2)}) collective-permute-start(bf16[112,128]{1,0:T(8,128)(2,1)S(1)} %get-tuple-element.42.refs_9_.refs_1_), channel_id=1, source_target_pairs={{0,16},{1,17},{2,18},{3,19},{4,20},{5,21},{6,22},{7,23},{8,24},{9,... | collective-permute-start | bytes 86024 | tf_op jit(solution)/shard_map/ppermute | solution.py:47
  36.1 1.7 %collective-permute-start.16 = (bf16[336,128]{1,0:T(8,128)(2,1)S(1)}, bf16[336,128]{1,0:T(8,128)(2,1)S(1)}, u32[]{:S(2)}, u32[]{:S(2)}) collective-permute-start(bf16[336,128]{1,0:T(8,128)(2,1)S(1)} %pass_on.1), channel_id=1, source_target_pairs={{0,8},{1,9},{2,10},{3,11},{4,12},{5,13},{6,14},{7,15},{8,0},{9,1},... | collective-permute-start | bytes 258056 | tf_op jit(solution)/shard_map/ppermute | solution.py:47
  37.9 1.9 %kept_terms.1 = (f32[288,192]{1,0:T(8,128)S(1)}, f32[224,192]{1,0:T(8,128)S(1)}) custom-call(bf16[768,128]{1,0:T(8,128)(2,1)S(1)} %bitcast.10, bf16[768,128]{1,0:T(8,128)(2,1)S(1)} %collective-permute-done.refs_1_, bf16[768,128]{1,0:T(8,128)(2,1)S(1)} %collective-permute-done.1.refs_2_, bf16[768,128]{1,0:T(8,128)(2,1)S(1)} %collective-permute-done.2.refs_3_, ...), custom_call_target="tpu_custom_call" | custom-call | flops 1207959552 | bytes 2129920 | tf_op jit(solution)/shard_map/kept_terms/pallas_call | solution.py:446
  39.9 0.6 %collective-permute-start.18 = (bf16[2,64,128]{2,1,0:T(8,128)(2,1)S(1)}, bf16[2,64,128]{2,1,0:T(8,128)(2,1)S(1)}, u32[]{:S(2)}, u32[]{:S(2)}) collective-permute-start(bf16[2,64,128]{2,1,0:T(8,128)(2,1)S(1)} %get-tuple-element.49), channel_id=1, source_target_pairs={{0,2},{1,3},{2,0},{3,1},{4,6},{5,7},{6,4},{7,5},{8,10},{9,11},{10,... | collective-permute-start | bytes 98312 | tf_op jit(solution)/shard_map/ppermute | solution.py:47
  40.5 0.5 %collective-permute-start.19 = (bf16[2,64,128]{2,1,0:T(8,128)(2,1)S(1)}, bf16[2,64,128]{2,1,0:T(8,128)(2,1)S(1)}, u32[]{:S(2)}, u32[]{:S(2)}) collective-permute-start(bf16[2,64,128]{2,1,0:T(8,128)(2,1)S(1)} %get-tuple-element.50), channel_id=1, source_target_pairs={{0,4},{1,5},{2,6},{3,7},{4,0},{5,1},{6,2},{7,3},{8,12},{9,13},{10,... | collective-permute-start | bytes 98312 | tf_op jit(solution)/shard_map/ppermute | solution.py:47
  41.0 2.5 %collective-permute-start.20 = (bf16[2,64,128]{2,1,0:T(8,128)(2,1)S(1)}, bf16[2,64,128]{2,1,0:T(8,128)(2,1)S(1)}, u32[]{:S(2)}, u32[]{:S(2)}) collective-permute-start(bf16[2,64,128]{2,1,0:T(8,128)(2,1)S(1)} %get-tuple-element.51), channel_id=1, source_target_pairs={{0,6},{1,7},{2,4},{3,5},{4,2},{5,3},{6,0},{7,1},{8,14},{9,15},{10,... | collective-permute-start | bytes 98312 | tf_op jit(solution)/shard_map/ppermute | solution.py:47
  43.7 1.1 %collective-permute-start.23 = (bf16[336,128]{1,0:T(8,128)(2,1)S(1)}, bf16[336,128]{1,0:T(8,128)(2,1)S(1)}, u32[]{:S(2)}, u32[]{:S(2)}) collective-permute-start(bf16[336,128]{1,0:T(8,128)(2,1)S(1)} %add_terms.1), channel_id=1, source_target_pairs={{0,16},{1,17},{2,18},{3,19},{4,20},{5,21},{6,22},{7,23},{8,24},{9,... | collective-permute-start | bytes 258056 | tf_op jit(solution)/shard_map/ppermute | solution.py:47
  44.8 1.1 %collective-permute-done.20.refs_3_.refs_5_ = bf16[2,64,128]{2,1,0:T(8,128)(2,1)S(1)} collective-permute-done((bf16[2,64,128]{2,1,0:T(8,128)(2,1)S(1)}, bf16[2,64,128]{2,1,0:T(8,128)(2,1)S(1)}, u32[]{:S(2)}, u32[]{:S(2)}) %collective-permute-start.20) | collective-permute-done | bytes 32800 | tf_op jit(solution)/shard_map/ppermute | solution.py:47
  45.9 1.2 %collective-permute-done.21.refs_6_ = bf16[4,64,128]{2,1,0:T(8,128)(2,1)S(1)} collective-permute-done((bf16[4,64,128]{2,1,0:T(8,128)(2,1)S(1)}, bf16[4,64,128]{2,1,0:T(8,128)(2,1)S(1)}, u32[]{:S(2)}, u32[]{:S(2)}) %collective-permute-start.21) | collective-permute-done | bytes 65568 | tf_op jit(solution)/shard_map/ppermute | solution.py:47
  47.1 1.0 %unpack_acts.1 = (bf16[2,1,64,384]{3,2,1,0:T(8,128)(2,1)}, f32[12,32,192]{2,1,0:T(8,128)S(1)}) custom-call(f32[288,192]{1,0:T(8,128)S(1)} %get-tuple-element.43.refs_6_.refs_0_, bf16[336,128]{1,0:T(8,128)(2,1)S(1)} %collective-permute-done.16.refs_1_.refs_2_, bf16[2,64,128]{2,1,0:T(8,128)(2,1)S(1)} %get-tuple-element.48.refs_0_.refs_2_, ...), custom_call_target="tpu_custom_call" | custom-call | bytes 897024 | tf_op jit(solution)/shard_map/unpack_acts/pallas_call | solution.py:446
  48.1 1.0 %collective-permute-done.23.refs_1_ = bf16[336,128]{1,0:T(8,128)(2,1)S(1)} collective-permute-done((bf16[336,128]{1,0:T(8,128)(2,1)S(1)}, bf16[336,128]{1,0:T(8,128)(2,1)S(1)}, u32[]{:S(2)}, u32[]{:S(2)}) %collective-permute-start.23) | collective-permute-done | bytes 86048 | tf_op jit(solution)/shard_map/ppermute | solution.py:47
  49.1 1.0 %unpack_weights.1 = f32[12,27,192]{2,1,0:T(8,128)} custom-call(f32[12,32,192]{2,1,0:T(8,128)S(1)} %get-tuple-element.53.refs_0_, bf16[336,128]{1,0:T(8,128)(2,1)S(1)} %collective-permute-done.23.refs_1_), custom_call_target="tpu_custom_call" | custom-call | bytes 629760 | tf_op jit(solution)/shard_map/unpack_weights/pallas_call | solution.py:446
  (45 shorter events, 1.7 us)
Async XLA Ops:
  0.6 0.9 %copy-start.4 = (bf16[2,1,64,384]{3,2,1,0:T(8,128)(2,1)S(1)}, bf16[2,1,64,384]{3,2,1,0:T(8,128)(2,1)}, u32[]{:S(2)}) copy-start(bf16[2,1,64,384]{3,2,1,0:T(8,128)(2,1)} %param.5) | copy-start | bytes 294916
  1.5 4.8 %copy-start.2 = (bf16[12,27,192]{2,1,0:T(8,128)(2,1)S(1)}, bf16[12,27,192]{2,1,0:T(8,128)(2,1)}, u32[]{:S(2)}) copy-start(bf16[12,27,192]{2,1,0:T(8,128)(2,1)} %refs_0_.1) | copy-start | bytes 373252
  1.8 7.2 %collective-permute-start.7 = (bf16[2,64,128]{2,1,0:T(8,128)(2,1)S(1)}, bf16[2,64,128]{2,1,0:T(8,128)(2,1)S(1)}, u32[]{:S(2)}, u32[]{:S(2)}) collective-permute-start(bf16[2,64,128]{2,1,0:T(8,128)(2,1)S(1)} %get-tuple-element.30), channel_id=1, source_target_pairs={{0,2},{1,3},{2,0},{3,1},{4,6},{5,7},{6,4},{7,5},{8,10},{9,11},{10,... | collective-permute-start | bytes 98312 | tf_op jit(solution)/shard_map/ppermute | solution.py:47
  4.8 4.2 %collective-permute-start.8 = (bf16[2,64,128]{2,1,0:T(8,128)(2,1)S(1)}, bf16[2,64,128]{2,1,0:T(8,128)(2,1)S(1)}, u32[]{:S(2)}, u32[]{:S(2)}) collective-permute-start(bf16[2,64,128]{2,1,0:T(8,128)(2,1)S(1)} %get-tuple-element.31), channel_id=1, source_target_pairs={{0,4},{1,5},{2,6},{3,7},{4,0},{5,1},{6,2},{7,3},{8,12},{9,13},{10,... | collective-permute-start | bytes 98312 | tf_op jit(solution)/shard_map/ppermute | solution.py:47
  6.3 4.8 %copy-start.3 = (bf16[2,2,128,192]{2,3,1,0:T(8,128)(2,1)S(1)}, bf16[2,2,128,192]{2,3,1,0:T(8,128)(2,1)}, u32[]{:S(2)}) copy-start(bf16[2,2,128,192]{2,3,1,0:T(8,128)(2,1)} %param.9) | copy-start | bytes 589828
  6.3 4.8 %collective-permute-start.9 = (bf16[2,64,128]{2,1,0:T(8,128)(2,1)S(1)}, bf16[2,64,128]{2,1,0:T(8,128)(2,1)S(1)}, u32[]{:S(2)}, u32[]{:S(2)}) collective-permute-start(bf16[2,64,128]{2,1,0:T(8,128)(2,1)S(1)} %get-tuple-element.32), channel_id=1, source_target_pairs={{0,6},{1,7},{2,4},{3,5},{4,2},{5,3},{6,0},{7,1},{8,14},{9,15},{10,... | collective-permute-start | bytes 98312 | tf_op jit(solution)/shard_map/ppermute | solution.py:47
  6.9 7.8 %collective-permute-start.12 = (bf16[336,128]{1,0:T(8,128)(2,1)S(1)}, bf16[336,128]{1,0:T(8,128)(2,1)S(1)}, u32[]{:S(2)}, u32[]{:S(2)}) collective-permute-start(bf16[336,128]{1,0:T(8,128)(2,1)S(1)} %pack_weights.1.refs_0_), channel_id=1, source_target_pairs={{0,8},{1,9},{2,10},{3,11},{4,12},{5,13},{6,14},{7,15},{8,0},{9,1},... | collective-permute-start | bytes 258056 | tf_op jit(solution)/shard_map/ppermute | solution.py:47
  11.2 6.3 %collective-permute-start.10 = (bf16[4,64,128]{2,1,0:T(8,128)(2,1)S(1)}, bf16[4,64,128]{2,1,0:T(8,128)(2,1)S(1)}, u32[]{:S(2)}, u32[]{:S(2)}) collective-permute-start(bf16[4,64,128]{2,1,0:T(8,128)(2,1)S(1)} %cross_acts.1), channel_id=1, source_target_pairs={{0,1},{1,0},{2,3},{3,2},{4,5},{5,4},{6,7},{7,6},{8,9},{9,8},{10,11... | collective-permute-start | bytes 196616 | tf_op jit(solution)/shard_map/ppermute | solution.py:47
  11.2 10.7 %collective-permute-start.2 = (bf16[768,128]{1,0:T(8,128)(2,1)S(1)}, bf16[768,128]{1,0:T(8,128)(2,1)S(1)}, u32[]{:S(2)}, u32[]{:S(2)}) collective-permute-start(bf16[768,128]{1,0:T(8,128)(2,1)S(1)} %bitcast.4), channel_id=1, source_target_pairs={{0,6},{1,7},{2,4},{3,5},{4,2},{5,3},{6,0},{7,1},{8,14},{9,15},{10,... | collective-permute-start | bytes 589832 | tf_op jit(solution)/shard_map/ppermute | solution.py:47
  11.7 12.6 %collective-permute-start.1 = (bf16[768,128]{1,0:T(8,128)(2,1)S(1)}, bf16[768,128]{1,0:T(8,128)(2,1)S(1)}, u32[]{:S(2)}, u32[]{:S(2)}) collective-permute-start(bf16[768,128]{1,0:T(8,128)(2,1)S(1)} %bitcast.5), channel_id=1, source_target_pairs={{0,4},{1,5},{2,6},{3,7},{4,0},{5,1},{6,2},{7,3},{8,12},{9,13},{10,... | collective-permute-start | bytes 589832 | tf_op jit(solution)/shard_map/ppermute | solution.py:47
  13.2 11.3 %collective-permute-start = (bf16[768,128]{1,0:T(8,128)(2,1)S(1)}, bf16[768,128]{1,0:T(8,128)(2,1)S(1)}, u32[]{:S(2)}, u32[]{:S(2)}) collective-permute-start(bf16[768,128]{1,0:T(8,128)(2,1)S(1)} %bitcast.6), channel_id=1, source_target_pairs={{0,2},{1,3},{2,0},{3,1},{4,6},{5,7},{6,4},{7,5},{8,10},{9,11},{10,... | collective-permute-start | bytes 589832 | tf_op jit(solution)/shard_map/ppermute | solution.py:47
  14.8 10.5 %collective-permute-start.13 = (bf16[672,128]{1,0:T(8,128)(2,1)S(1)}, bf16[672,128]{1,0:T(8,128)(2,1)S(1)}, u32[]{:S(2)}, u32[]{:S(2)}) collective-permute-start(bf16[672,128]{1,0:T(8,128)(2,1)S(1)} %join_kernel_rows.1), channel_id=1, source_target_pairs={{0,16},{1,17},{2,18},{3,19},{4,20},{5,21},{6,22},{7,23},{8,24},{9,... | collective-permute-start | bytes 516104 | tf_op jit(solution)/shard_map/ppermute | solution.py:47
  17.5 4.3 %collective-permute-start.11 = (bf16[176,128]{1,0:T(8,128)(2,1)S(1)}, bf16[176,128]{1,0:T(8,128)(2,1)S(1)}, u32[]{:S(2)}, u32[]{:S(2)}) collective-permute-start(bf16[176,128]{1,0:T(8,128)(2,1)S(1)} %get-tuple-element.35), channel_id=1, source_target_pairs={{0,8},{1,9},{2,10},{3,11},{4,12},{5,13},{6,14},{7,15},{8,0},{9,1},... | collective-permute-start | bytes 135176 | tf_op jit(solution)/shard_map/ppermute | solution.py:47
  21.8 5.2 %collective-permute-start.3 = (bf16[768,128]{1,0:T(8,128)(2,1)S(1)}, bf16[768,128]{1,0:T(8,128)(2,1)S(1)}, u32[]{:S(2)}, u32[]{:S(2)}) collective-permute-start(bf16[768,128]{1,0:T(8,128)(2,1)S(1)} %bitcast.7), channel_id=1, source_target_pairs={{0,1},{1,0},{2,3},{3,2},{4,5},{5,4},{6,7},{7,6},{8,9},{9,8},{10,11... | collective-permute-start | bytes 589832 | tf_op jit(solution)/shard_map/ppermute | solution.py:47
  21.9 6.5 %collective-permute-start.14 = (bf16[112,128]{1,0:T(8,128)(2,1)S(1)}, bf16[112,128]{1,0:T(8,128)(2,1)S(1)}, u32[]{:S(2)}, u32[]{:S(2)}) collective-permute-start(bf16[112,128]{1,0:T(8,128)(2,1)S(1)} %get-tuple-element.37), channel_id=1, source_target_pairs={{0,16},{1,17},{2,18},{3,19},{4,20},{5,21},{6,22},{7,23},{8,24},{9,... | collective-permute-start | bytes 86024 | tf_op jit(solution)/shard_map/ppermute | solution.py:47
  24.3 2.8 %collective-permute-start.6 = (bf16[768,128]{1,0:T(8,128)(2,1)S(1)}, bf16[768,128]{1,0:T(8,128)(2,1)S(1)}, u32[]{:S(2)}, u32[]{:S(2)}) collective-permute-start(bf16[768,128]{1,0:T(8,128)(2,1)S(1)} %collective-permute-done.2.refs_3_), channel_id=1, source_target_pairs={{0,1},{1,0},{2,3},{3,2},{4,5},{5,4},{6,7},{7,6},{8,9},{9,8},{10,11... | collective-permute-start | bytes 589832 | tf_op jit(solution)/shard_map/ppermute | solution.py:47
  24.5 2.5 %collective-permute-start.5 = (bf16[768,128]{1,0:T(8,128)(2,1)S(1)}, bf16[768,128]{1,0:T(8,128)(2,1)S(1)}, u32[]{:S(2)}, u32[]{:S(2)}) collective-permute-start(bf16[768,128]{1,0:T(8,128)(2,1)S(1)} %collective-permute-done.1.refs_2_), channel_id=1, source_target_pairs={{0,1},{1,0},{2,3},{3,2},{4,5},{5,4},{6,7},{7,6},{8,9},{9,8},{10,11... | collective-permute-start | bytes 589832 | tf_op jit(solution)/shard_map/ppermute | solution.py:47
  25.3 1.8 %collective-permute-start.4 = (bf16[768,128]{1,0:T(8,128)(2,1)S(1)}, bf16[768,128]{1,0:T(8,128)(2,1)S(1)}, u32[]{:S(2)}, u32[]{:S(2)}) collective-permute-start(bf16[768,128]{1,0:T(8,128)(2,1)S(1)} %collective-permute-done.refs_1_), channel_id=1, source_target_pairs={{0,1},{1,0},{2,3},{3,2},{4,5},{5,4},{6,7},{7,6},{8,9},{9,8},{10,11... | collective-permute-start | bytes 589832 | tf_op jit(solution)/shard_map/ppermute | solution.py:47
  27.0 1.3 %copy-start = (f32[384]{0:T(512)S(1)}, f32[384]{0:T(512)}, u32[]{:S(2)}) copy-start(f32[384]{0:T(512)} %refs_2_.1) | copy-start | bytes 4612
  27.0 1.3 %copy-start.1 = (f32[384]{0:T(512)S(1)}, f32[384]{0:T(512)}, u32[]{:S(2)}) copy-start(f32[384]{0:T(512)} %refs_3_.1) | copy-start | bytes 4612
  29.5 4.1 %collective-permute-start.15 = (bf16[176,128]{1,0:T(8,128)(2,1)S(1)}, bf16[176,128]{1,0:T(8,128)(2,1)S(1)}, u32[]{:S(2)}, u32[]{:S(2)}) collective-permute-start(bf16[176,128]{1,0:T(8,128)(2,1)S(1)} %get-tuple-element.40), channel_id=1, source_target_pairs={{0,8},{1,9},{2,10},{3,11},{4,12},{5,13},{6,14},{7,15},{8,0},{9,1},... | collective-permute-start | bytes 135176 | tf_op jit(solution)/shard_map/ppermute | solution.py:47
  32.3 11.2 %collective-permute-start.22 = (bf16[336,128]{1,0:T(8,128)(2,1)S(1)}, bf16[336,128]{1,0:T(8,128)(2,1)S(1)}, u32[]{:S(2)}, u32[]{:S(2)}) collective-permute-start(bf16[336,128]{1,0:T(8,128)(2,1)S(1)} %get-tuple-element.55), channel_id=1, source_target_pairs={{0,8},{1,9},{2,10},{3,11},{4,12},{5,13},{6,14},{7,15},{8,0},{9,1},... | collective-permute-start | bytes 258056 | tf_op jit(solution)/shard_map/ppermute | solution.py:47
  33.6 6.2 %collective-permute-start.17 = (bf16[112,128]{1,0:T(8,128)(2,1)S(1)}, bf16[112,128]{1,0:T(8,128)(2,1)S(1)}, u32[]{:S(2)}, u32[]{:S(2)}) collective-permute-start(bf16[112,128]{1,0:T(8,128)(2,1)S(1)} %get-tuple-element.42.refs_9_.refs_1_), channel_id=1, source_target_pairs={{0,16},{1,17},{2,18},{3,19},{4,20},{5,21},{6,22},{7,23},{8,24},{9,... | collective-permute-start | bytes 86024 | tf_op jit(solution)/shard_map/ppermute | solution.py:47
  36.1 7.4 %collective-permute-start.16 = (bf16[336,128]{1,0:T(8,128)(2,1)S(1)}, bf16[336,128]{1,0:T(8,128)(2,1)S(1)}, u32[]{:S(2)}, u32[]{:S(2)}) collective-permute-start(bf16[336,128]{1,0:T(8,128)(2,1)S(1)} %pass_on.1), channel_id=1, source_target_pairs={{0,8},{1,9},{2,10},{3,11},{4,12},{5,13},{6,14},{7,15},{8,0},{9,1},... | collective-permute-start | bytes 258056 | tf_op jit(solution)/shard_map/ppermute | solution.py:47
  39.9 4.8 %collective-permute-start.18 = (bf16[2,64,128]{2,1,0:T(8,128)(2,1)S(1)}, bf16[2,64,128]{2,1,0:T(8,128)(2,1)S(1)}, u32[]{:S(2)}, u32[]{:S(2)}) collective-permute-start(bf16[2,64,128]{2,1,0:T(8,128)(2,1)S(1)} %get-tuple-element.49), channel_id=1, source_target_pairs={{0,2},{1,3},{2,0},{3,1},{4,6},{5,7},{6,4},{7,5},{8,10},{9,11},{10,... | collective-permute-start | bytes 98312 | tf_op jit(solution)/shard_map/ppermute | solution.py:47
  40.5 4.3 %collective-permute-start.19 = (bf16[2,64,128]{2,1,0:T(8,128)(2,1)S(1)}, bf16[2,64,128]{2,1,0:T(8,128)(2,1)S(1)}, u32[]{:S(2)}, u32[]{:S(2)}) collective-permute-start(bf16[2,64,128]{2,1,0:T(8,128)(2,1)S(1)} %get-tuple-element.50), channel_id=1, source_target_pairs={{0,4},{1,5},{2,6},{3,7},{4,0},{5,1},{6,2},{7,3},{8,12},{9,13},{10,... | collective-permute-start | bytes 98312 | tf_op jit(solution)/shard_map/ppermute | solution.py:47
  41.0 4.8 %collective-permute-start.20 = (bf16[2,64,128]{2,1,0:T(8,128)(2,1)S(1)}, bf16[2,64,128]{2,1,0:T(8,128)(2,1)S(1)}, u32[]{:S(2)}, u32[]{:S(2)}) collective-permute-start(bf16[2,64,128]{2,1,0:T(8,128)(2,1)S(1)} %get-tuple-element.51), channel_id=1, source_target_pairs={{0,6},{1,7},{2,4},{3,5},{4,2},{5,3},{6,0},{7,1},{8,14},{9,15},{10,... | collective-permute-start | bytes 98312 | tf_op jit(solution)/shard_map/ppermute | solution.py:47
  43.7 5.4 %collective-permute-start.23 = (bf16[336,128]{1,0:T(8,128)(2,1)S(1)}, bf16[336,128]{1,0:T(8,128)(2,1)S(1)}, u32[]{:S(2)}, u32[]{:S(2)}) collective-permute-start(bf16[336,128]{1,0:T(8,128)(2,1)S(1)} %add_terms.1), channel_id=1, source_target_pairs={{0,16},{1,17},{2,18},{3,19},{4,20},{5,21},{6,22},{7,23},{8,24},{9,... | collective-permute-start | bytes 258056 | tf_op jit(solution)/shard_map/ppermute | solution.py:47
  45.9 1.3 %collective-permute-start.21 = (bf16[4,64,128]{2,1,0:T(8,128)(2,1)S(1)}, bf16[4,64,128]{2,1,0:T(8,128)(2,1)S(1)}, u32[]{:S(2)}, u32[]{:S(2)}) collective-permute-start(bf16[4,64,128]{2,1,0:T(8,128)(2,1)S(1)} %cross_grads.1), channel_id=1, source_target_pairs={{0,1},{1,0},{2,3},{3,2},{4,5},{5,4},{6,7},{7,6},{8,9},{9,8},{10,11... | collective-permute-start | bytes 196616 | tf_op jit(solution)/shard_map/ppermute | solution.py:47
